TPU v7x, 32 devices: a whole 2x2x4 slice. The times are simulated.
32 devices in a mesh: groups: 2 (over x), cache: 4 (over y, core), span: 4 (over z).
Axes of the slice: x: 2, y: 2, z: 4, core: 2. Of those that a mesh axis runs over, the one named last changes fastest.
Arguments:
- block_states: bfloat16 [8192, 1792], P(('groups', 'cache', 'span')), parts along dimension 0, may hold values from -6 to 6
- cross_queries: bfloat16 [8192, 2048], P(('groups', 'cache', 'span')), parts along dimension 0, may hold values from -120 to 120
- neighbour_cache: bfloat16 [64, 64, 896], P(('groups', 'cache')), parts along dimension 0, may hold values from -160 to 160
- neighbour_owner: int32 [128, 2], P(('groups', 'cache', 'span')), parts along dimension 0, may hold values from 0 to 3, all different within a row; in each aligned block of 4 rows (0 to 3, 4 to 7, ...) at most 2 rows name the same one
- neighbour_slot: int32 [128, 2], P(('groups', 'cache', 'span')), parts along dimension 0, may hold values from 0 to 7
- neighbour_lengths: int32 [128, 2], P(('groups', 'cache', 'span')), parts along dimension 0, may hold values from 1 to 64, as said below
- encoder_query: bfloat16 [896, 896], replicated, may hold values from -0.1875 to 0.1875
- cross_weight: bfloat16 [896, 4096], P(None, 'span'), may hold values from -0.1875 to 0.1875
Outputs:
- cross_output: bfloat16 [8192, 2048], P(('groups', 'cache', 'span')), parts along dimension 0
There are 2 independent parts, one for each index of `groups`. A program takes and returns all parts, laid end to end along the dimension named above; an argument that names none is the same for every part. Nothing has to cross between parts.
Inputs may be any that keep to these rules, and one draw needn't show every extreme that they name: `neighbour_owner`: among the rows of one device at most 2 requests name the same owner, and this is reached; each row names 2 different owners. `neighbour_lengths`: both ends are reached in every draw.
All inputs are finite; a program needn't handle non-finite values.
Results may differ from a plain program's by a relative error of at most 0.0055.
The roundings to bfloat16 on the way count: a program that leaves them out, or rounds other values in their place, can miss the bound.
Values may be sent and summed in bfloat16 or wider, within the bound.
No kernel may reach another device: no remote copies, remote signals or barrier semaphores. Data moves between devices by JAX's collectives and lax.ppermute only.
A program may use at most 128 MiB of HBM per device.

v0:
```python
import math

import jax
import jax.numpy as jnp
from jax import lax
from jax.sharding import PartitionSpec as P

ENC_HEADS = 14
ENCODER_HEAD_DIM = 64
ENCODER_WIDTH = 896
CROSS_HEADS = 16
CROSS_HEAD = 128
BLOCK_LEN = 64
NEIGHBOUR_LENGTH = 64
NEIGHBOUR_COUNT = 2


MASKED_SCORE = -1e30


def from_behind(value, axis, steps):
    count = lax.axis_size(axis)
    initial, last = (max(0, -steps), min(count, count - steps))
    return lax.ppermute(value, axis, [(source, source + steps) for source in range(initial, last)])


def attend_encoder(neighbour_rows, query_rows, block_rows):
    batch_size = neighbour_rows.shape[0]
    queries = query_rows.reshape(batch_size, NEIGHBOUR_LENGTH, ENC_HEADS, ENCODER_HEAD_DIM)
    encoder_key_rows = block_rows[..., :ENCODER_WIDTH].reshape(
        batch_size, BLOCK_LEN, ENC_HEADS, ENCODER_HEAD_DIM
    )
    encoder_value_rows = block_rows[..., ENCODER_WIDTH:].reshape(
        batch_size, BLOCK_LEN, ENC_HEADS, ENCODER_HEAD_DIM
    )
    encoder_scores = jnp.einsum(
        "brhd,bmhd->bhmr", queries, encoder_key_rows, preferred_element_type=jnp.float32
    ) / math.sqrt(ENCODER_HEAD_DIM)
    attention_weights = jax.nn.softmax(encoder_scores, axis=2).astype(jnp.bfloat16)
    attended_values = jnp.einsum(
        "bhmr,bmhd->brhd", attention_weights, encoder_value_rows, preferred_element_type=jnp.float32
    )
    attended_values = attended_values.reshape(batch_size, NEIGHBOUR_LENGTH, ENCODER_WIDTH)
    return (neighbour_rows.astype(jnp.float32) + attended_values).astype(jnp.bfloat16)


def attend_cross(queries, states, usable):
    cross_width = CROSS_HEADS * CROSS_HEAD
    groups = queries.shape[0]
    query_heads = queries.reshape(groups, -1, CROSS_HEADS, CROSS_HEAD)
    key_heads = states[..., :cross_width].reshape(groups, -1, CROSS_HEADS, CROSS_HEAD)
    value_heads = states[..., cross_width:].reshape(groups, -1, CROSS_HEADS, CROSS_HEAD)
    encoder_scores = jnp.einsum(
        "gqhd,gkhd->ghqk", query_heads, key_heads, preferred_element_type=jnp.float32
    ) / math.sqrt(CROSS_HEAD)
    encoder_scores = jnp.where(usable[:, None, None, :], encoder_scores, MASKED_SCORE)
    attention_weights = jax.nn.softmax(encoder_scores, axis=-1).astype(jnp.bfloat16)
    attended_values = jnp.einsum(
        "ghqk,gkhd->gqhd", attention_weights, value_heads, preferred_element_type=jnp.float32
    )
    return attended_values.reshape(groups, -1, cross_width).astype(jnp.bfloat16)


def per_device(
    block_states,
    cross_queries,
    neighbour_cache,
    neighbour_owner,
    neighbour_slot,
    neighbour_lengths,
    encoder_query,
    cross_weight,
):
    peer_count = lax.axis_size("cache")
    blocks = neighbour_owner.shape[0]
    requests = blocks * NEIGHBOUR_COUNT
    capacity = max(2, (requests + peer_count - 1) // peer_count)
    slot_total = peer_count * capacity
    cross_width = CROSS_HEADS * CROSS_HEAD
    owner_flat = neighbour_owner.reshape(requests)
    slot_flat = neighbour_slot.reshape(requests)
    request_index = jnp.arange(requests, dtype=jnp.int32)
    earlier = (owner_flat[:, None] == owner_flat[None, :]) & (
        request_index[None, :] < request_index[:, None]
    )
    position = owner_flat * capacity + jnp.sum(earlier.astype(jnp.int32), axis=1)
    placed = jnp.arange(slot_total, dtype=jnp.int32)[:, None] == position[None, :]
    placing = placed.astype(jnp.bfloat16)
    send_slots = jnp.sum(jnp.where(placed, slot_flat[None, :], 0), axis=1).reshape(
        peer_count, capacity
    )
    query_table = jnp.dot(
        neighbour_cache.reshape(-1, ENCODER_WIDTH),
        encoder_query,
        preferred_element_type=jnp.float32,
    )
    query_table = query_table.astype(jnp.bfloat16).reshape(neighbour_cache.shape)
    block_of = request_index // NEIGHBOUR_COUNT
    slot_block = jnp.any(
        placed[:, :, None]
        & (block_of[None, :, None] == jnp.arange(blocks, dtype=jnp.int32)[None, None, :]),
        axis=1,
    )
    send_states = jnp.dot(
        slot_block.astype(jnp.bfloat16),
        block_states.reshape(blocks, -1),
        preferred_element_type=jnp.float32,
    )
    send_states = send_states.astype(jnp.bfloat16).reshape(
        peer_count, capacity, BLOCK_LEN, 2 * ENCODER_WIDTH
    )
    states_in = lax.all_to_all(send_states, "cache", split_axis=0, concat_axis=0, tiled=True)
    slots_in = lax.all_to_all(send_slots, "cache", split_axis=0, concat_axis=0, tiled=True)
    item_count = slots_in.shape[1]
    slot_list = slots_in.reshape(-1)
    cached = jnp.take(neighbour_cache, slot_list, axis=0)
    queried = jnp.take(query_table, slot_list, axis=0)
    encoded = attend_encoder(cached, queried, states_in.reshape(-1, BLOCK_LEN, 2 * ENCODER_WIDTH))
    encoded = encoded.reshape(peer_count, item_count, NEIGHBOUR_LENGTH, ENCODER_WIDTH)
    arrived = lax.all_to_all(encoded, "cache", split_axis=0, concat_axis=0, tiled=True)
    encoded_rows = jnp.dot(
        placing.T, arrived.reshape(slot_total, -1), preferred_element_type=jnp.float32
    )
    encoded_rows = encoded_rows.astype(jnp.bfloat16).reshape(
        requests, NEIGHBOUR_LENGTH, ENCODER_WIDTH
    )
    encoded_flat = encoded_rows.reshape(-1, ENCODER_WIDTH)
    cross_states = jnp.dot(
        encoded_flat,
        lax.all_gather(cross_weight, "span", axis=1, tiled=True),
        preferred_element_type=jnp.float32,
    ).astype(jnp.bfloat16)
    cross_states = cross_states.reshape(blocks, NEIGHBOUR_COUNT * NEIGHBOUR_LENGTH, 2 * cross_width)
    usable = (
        jnp.arange(NEIGHBOUR_LENGTH, dtype=jnp.int32)[None, None, :] < neighbour_lengths[:, :, None]
    ).reshape(blocks, NEIGHBOUR_COUNT * NEIGHBOUR_LENGTH)
    tokens = blocks * BLOCK_LEN
    shift_len = BLOCK_LEN - 1
    prior_states, prior_usable = from_behind(
        (cross_states[-1], usable[-1].astype(jnp.bfloat16)), "span", 1
    )
    states_all = jnp.concatenate([prior_states[None], cross_states], axis=0)
    usable_all = jnp.concatenate([(prior_usable > 0.5)[None], usable], axis=0)
    padded = jnp.concatenate(
        [
            jnp.zeros((1, cross_width), jnp.bfloat16),
            cross_queries,
            jnp.zeros((shift_len, cross_width), jnp.bfloat16),
        ],
        axis=0,
    )
    padded = padded.reshape(blocks + 1, BLOCK_LEN, cross_width)
    result = attend_cross(padded, states_all, usable_all).reshape(-1, cross_width)[1 : tokens + 1]
    return result


def solution(mesh):
    placed = (
        P(("groups", "cache", "span"), None),
        P(("groups", "cache", "span"), None),
        P(("groups", "cache"), None, None),
        P(("groups", "cache", "span"), None),
        P(("groups", "cache", "span"), None),
        P(("groups", "cache", "span"), None),
        P(),
        P(None, "span"),
    )
    return jax.shard_map(
        per_device,
        mesh=mesh,
        in_specs=placed,
        out_specs=P(("groups", "cache", "span"), None),
        check_vma=False,
    )
```

profile of v0, /device:TPU:0, one launch (start us, length us, event | category | flops | bytes accessed | tf_op | source)
XLA Modules:
  0.0 216.0 jit_solution(18445773017884231561)
XLA Ops:
  9.9 4.2 %all-to-all-start = ((s32[4,1,2]{2,1,0:T(1,128)}), s32[4,1,2]{2,1,0:T(1,128)S(1)}, u32[]{:S(2)}, u32[]{:S(2)}) async-start(s32[4,1,2]{2,1,0:T(1,128)} %bitcast), calls=%async_computation | async-start | bytes 4096 | tf_op jit(solution)/shard_map/all_to_all | solution.py:113
  14.2 1.9 reshape.145
  17.0 1.5 copy.57
  18.6 3.6 %all-to-all-start.1 = ((bf16[4,2,64,1792]{3,2,1,0:T(8,128)(2,1)}), bf16[4,2,64,1792]{3,2,1,0:T(8,128)(2,1)S(1)}, u32[]{:S(2)}, u32[]{:S(2)}) async-start(bf16[4,2,64,1792]{3,2,1,0:T(8,128)(2,1)} %bitcast.45), calls=%async_computation.1 | async-start | bytes 3670016 | tf_op jit(solution)/shard_map/all_to_all | solution.py:112
  22.2 3.4 %convolution_convert_fusion.4 = bf16[512,896]{1,0:T(8,128)(2,1)} fusion(bf16[512,896]{1,0:T(8,128)(2,1)} %bitcast.57, bf16[896,896]{1,0:T(8,128)(2,1)S(1)} %copy-done), kind=kOutput, calls=%fused_computation.27 | convolution fusion | flops 822542336 | bytes 3440640 | tf_op jit(solution)/shard_map/dot_general | solution.py:92
  27.0 2.7 %gather_fusion = bf16[8,64,896]{2,1,0:T(8,128)(2,1)} fusion(bf16[8,64,896]{2,1,0:T(8,128)(2,1)} %param.12, s32[1024]{0:T(1024)S(1)} %pad_clamp_fusion), kind=kCustom, calls=%fused_computation.clone | custom fusion | bytes 1835040 | tf_op jit(solution)/shard_map/jit(_take)/gather | solution.py:116
  29.7 1.9 gather_fusion.1
  31.6 1.1 broadcast_select_fusion
  32.7 4.1 %reshape.152 = bf16[8,64,14,64]{3,2,1,0:T(8,128)(2,1)} reshape(bf16[8,64,896]{2,1,0:T(8,128)(2,1)} %broadcast_select_fusion) | data formatting | bytes 1835008 | tf_op jit(solution)/shard_map/reshape | solution.py:29
  36.8 8.2 %all-to-all-done.1 = bf16[4,2,64,1792]{3,2,1,0:T(8,128)(2,1)S(1)} async-done(((bf16[4,2,64,1792]{3,2,1,0:T(8,128)(2,1)}), bf16[4,2,64,1792]{3,2,1,0:T(8,128)(2,1)S(1)}, u32[]{:S(2)}, u32[]{:S(2)}) %all-to-all-start.1) | async-done | bytes 1835040 | tf_op jit(solution)/shard_map/all_to_all | solution.py:112
  45.1 1.2 fusion.30
  46.2 2.4 %reshape.149 = bf16[8,64,14,64]{3,2,1,0:T(8,128)(2,1)} reshape(bf16[8,64,896]{2,1,0:T(8,128)(2,1)S(1)} %get-tuple-element.8) | data formatting | bytes 1835008 | tf_op jit(solution)/shard_map/reshape | solution.py:30
  48.6 1.7 copy.44
  50.3 3.3 %fusion.8 = f32[8,14,64,64]{3,2,1,0:T(8,128)S(1)} fusion(bf16[8,64,14,64]{3,2,1,0:T(8,128)(2,1)} %reshape.152, bf16[8,64,14,64]{3,2,1,0:T(8,128)(2,1)} %reshape.149), kind=kOutput, calls=%fused_computation.20 | convolution fusion | flops 58720256 | bytes 3670016 | tf_op jit(solution)/shard_map/brhd,bmhd->bhmr/dot_general | solution.py:36
  53.7 5.4 %fusion.31 = (f32[8,14,64]{2,1,0:T(8,128)S(1)}, f32[8,14,64,64]{3,2,1,0:T(8,128)S(1)}) fusion(f32[8,14,64,64]{3,2,1,0:T(8,128)S(1)} %fusion.8), kind=kOutput, calls=%fused_computation.65 | output fusion | flops 1835071 | bytes 3698688 | tf_op jit(solution)/shard_map/sub | solution.py:39
  59.1 2.5 %fusion.7 = f32[8,14,64,64]{3,2,1,0:T(8,128)} fusion(bf16[8,64,14,64]{1,3,2,0:T(8,128)(2,1)S(1)} %bitcast.56, f32[8,14,64,64]{3,2,1,0:T(8,128)S(1)} %get-tuple-element.11, f32[8,14,64]{2,1,0:T(8,128)S(1)} %get-tuple-element.10), kind=kOutput, calls=%fused_computation.19 | convolution fusion | flops 59637760 | bytes 4616192 | tf_op jit(solution)/shard_map/bhmr,bmhd->brhd/dot_general | solution.py:40
  61.6 2.7 %copy.47 = f32[8,64,896]{2,1,0:T(8,128)S(1)} copy(f32[8,64,896]{1,2,0:T(8,128)} %bitcast.53) | data formatting | bytes 3670016 | tf_op jit(solution)/shard_map/reshape | solution.py:43
  64.7 15.5 %all_to_all.19 = bf16[4,2,64,896]{3,2,1,0:T(8,128)(2,1)S(1)} all-to-all(bf16[4,2,64,896]{3,2,1,0:T(8,128)(2,1)S(1)} %bitcast.54), channel_id=1, replica_groups=mesh['groups'=2,'cache'=4,'span'=4] {'cache'}, dimensions={0} | all-to-all | bytes 1835008 | tf_op jit(solution)/shard_map/all_to_all | solution.py:120
  81.5 62.6 %all-gather.2.cloned.1.call-done = bf16[896,4096]{1,0:T(8,128)(2,1)} async-done(((bf16[896,1024]{1,0:T(8,128)(2,1)}), bf16[896,4096]{1,0:T(8,128)(2,1)}) %all-gather.2.cloned.1.call-update) | async-done | bytes 7340048 | tf_op jit(solution)/shard_map/all_gather | solution.py:130
  144.2 7.8 %convolution_convert_fusion.2 = bf16[512,4096]{1,0:T(8,128)(2,1)S(1)} fusion(bf16[512,896]{1,0:T(8,128)(2,1)S(1)} %reshape_reshape.6, bf16[896,4096]{1,0:T(8,128)(2,1)} %all-gather.2.cloned.1.call-done), kind=kOutput, calls=%fused_computation.6 | convolution fusion | flops 3760193536 | bytes 12451840 | tf_op jit(solution)/shard_map/dot_general | solution.py:128
  152.0 2.0 copy-done.2
  153.9 1.0 slice.36
  155.0 2.4 %collective-permute-start = (bf16[128,4096]{1,0:T(8,128)(2,1)}, bf16[128,4096]{1,0:T(8,128)(2,1)}, u32[]{:S(2)}, u32[]{:S(2)}) collective-permute-start(bf16[128,4096]{1,0:T(8,128)(2,1)} %slice.36), channel_id=1, source_target_pairs={{0,1},{1,2},{2,3},{4,5},{5,6},{6,7},{8,9},{9,10},{10,11},{12,13},{... | collective-permute-start | bytes 3145736 | tf_op jit(solution)/shard_map/ppermute | solution.py:24
  157.6 2.7 %collective-permute-start.1 = (bf16[128]{0:T(256)(128)(2,1)S(1)}, bf16[128]{0:T(256)(128)(2,1)S(1)}, u32[]{:S(2)}, u32[]{:S(2)}) collective-permute-start(bf16[128]{0:T(256)(128)(2,1)S(1)} %reshape.159), channel_id=1, source_target_pairs={{0,1},{1,2},{2,3},{4,5},{5,6},{6,7},{8,9},{9,10},{10,11},{12,13},{... | collective-permute-start | bytes 776 | tf_op jit(solution)/shard_map/ppermute | solution.py:24
  161.5 17.9 %collective-permute-done.1 = bf16[128]{0:T(256)(128)(2,1)S(1)} collective-permute-done((bf16[128]{0:T(256)(128)(2,1)S(1)}, bf16[128]{0:T(256)(128)(2,1)S(1)}, u32[]{:S(2)}, u32[]{:S(2)}) %collective-permute-start.1) | collective-permute-done | bytes 288 | tf_op jit(solution)/shard_map/ppermute | solution.py:24
  179.5 6.4 %copy.49 = bf16[4,128,4096]{1,2,0:T(8,128)(2,1)} copy(bf16[4,128,4096]{2,1,0:T(8,128)(2,1)} %bitcast.47) | data formatting | bytes 8388608 | tf_op jit(solution)/shard_map/reshape | solution.py:133
  185.8 1.6 copy.48
  187.5 3.9 %pad_maximum_fusion = (bf16[5,128,2048]{1,2,0:T(8,128)(2,1)S(1)}, bf16[5,128,2048]{1,2,0:T(8,128)(2,1)}) fusion(bf16[4,128,4096]{1,2,0:T(8,128)(2,1)} %copy.49, bf16[1,128,4096]{1,2,0:T(8,128)(2,1)S(1)} %copy.48), kind=kLoop, calls=%fused_computation.14 | loop fusion | flops 10485760 | bytes 10485760 | tf_op jit(solution)/shard_map/concatenate | solution.py:142
  192.2 1.5 copy-done.5
  193.7 1.4 fusion.32
  195.1 11.5 %fusion.13 = bf16[5,64,16,128]{3,1,2,0:T(8,128)(2,1)S(1)} fusion(bf16[5,128,16,128]{1,3,2,0:T(8,128)(2,1)} %bitcast.55, f32[5,16,64]{2,1,0:T(8,128)S(1)} %fusion.32, f32[5,16,64,128]{3,2,1,0:T(8,128)} %copy-done.5, pred[5,128]{1,0:T(8,128)(4,1)S(1)} %pad_add_fusion), kind=kOutput, calls=%fused_computation.28 | convolution fusion | flops 171709568 | bytes 6574720 | tf_op jit(solution)/shard_map/ghqk,gkhd->gqhd/dot_general | solution.py:58
  207.9 1.3 slice.40
  (62 shorter events, 11.0 us)
Async XLA Ops:
  6.5 15.7 %copy-start = (bf16[896,896]{1,0:T(8,128)(2,1)S(1)}, bf16[896,896]{1,0:T(8,128)(2,1)}, u32[]{:S(2)}) copy-start(bf16[896,896]{1,0:T(8,128)(2,1)} %param.16) | copy-start | bytes 4816900
  6.5 137.6 %all-gather.2.cloned.1.call-start = ((), (), s32[]{:S(2)}) async-start(), calls=%async_computation.3 | async-start | bytes 9175040 | tf_op jit(solution)/shard_map/all_gather | solution.py:130
  9.9 8.6 %all-to-all-start = ((s32[4,1,2]{2,1,0:T(1,128)}), s32[4,1,2]{2,1,0:T(1,128)S(1)}, u32[]{:S(2)}, u32[]{:S(2)}) async-start(s32[4,1,2]{2,1,0:T(1,128)} %bitcast), calls=%async_computation | async-start | bytes 4096 | tf_op jit(solution)/shard_map/all_to_all | solution.py:113
  18.6 26.5 %all-to-all-start.1 = ((bf16[4,2,64,1792]{3,2,1,0:T(8,128)(2,1)}), bf16[4,2,64,1792]{3,2,1,0:T(8,128)(2,1)S(1)}, u32[]{:S(2)}, u32[]{:S(2)}) async-start(bf16[4,2,64,1792]{3,2,1,0:T(8,128)(2,1)} %bitcast.45), calls=%async_computation.1 | async-start | bytes 3670016 | tf_op jit(solution)/shard_map/all_to_all | solution.py:112
  46.2 2.4 %copy-start.3 = (bf16[8,64,896]{2,1,0:T(8,128)(2,1)S(1)}, bf16[8,64,896]{2,1,0:T(8,128)(2,1)}, u32[]{:S(2)}) copy-start(bf16[8,64,896]{2,1,0:T(8,128)(2,1)} %get-tuple-element.9) | copy-start | bytes 2752516
  53.7 5.4 %copy-start.6 = (bf16[8,64,896]{1,2,0:T(8,128)(2,1)S(1)}, bf16[8,64,896]{1,2,0:T(8,128)(2,1)}, u32[]{:S(2)}) copy-start(bf16[8,64,896]{1,2,0:T(8,128)(2,1)} %copy.44) | copy-start | bytes 2752516
  61.6 2.7 %copy-start.4 = (bf16[8,64,896]{2,1,0:T(8,128)(2,1)S(1)}, bf16[8,64,896]{2,1,0:T(8,128)(2,1)}, u32[]{:S(2)}) copy-start(bf16[8,64,896]{2,1,0:T(8,128)(2,1)} %gather_fusion) | copy-start | bytes 2752516
  81.5 75.8 %copy-start.8 = (s32[4,2]{0,1:T(2,128)S(1)}, s32[4,2]{0,1:T(2,128)}, u32[]{:S(2)}) copy-start(s32[4,2]{0,1:T(2,128)} %param.15) | copy-start | bytes 100
  151.9 2.0 copy-start.2
  153.9 6.7 %copy-start.7 = (bf16[256,2048]{1,0:T(8,128)(2,1)S(1)}, bf16[256,2048]{1,0:T(8,128)(2,1)}, u32[]{:S(2)}) copy-start(bf16[256,2048]{1,0:T(8,128)(2,1)} %param.11) | copy-start | bytes 3145732
  155.0 30.9 %collective-permute-start = (bf16[128,4096]{1,0:T(8,128)(2,1)}, bf16[128,4096]{1,0:T(8,128)(2,1)}, u32[]{:S(2)}, u32[]{:S(2)}) collective-permute-start(bf16[128,4096]{1,0:T(8,128)(2,1)} %slice.36), channel_id=1, source_target_pairs={{0,1},{1,2},{2,3},{4,5},{5,6},{6,7},{8,9},{9,10},{10,11},{12,13},{... | collective-permute-start | bytes 3145736 | tf_op jit(solution)/shard_map/ppermute | solution.py:24
  157.6 21.9 %collective-permute-start.1 = (bf16[128]{0:T(256)(128)(2,1)S(1)}, bf16[128]{0:T(256)(128)(2,1)S(1)}, u32[]{:S(2)}, u32[]{:S(2)}) collective-permute-start(bf16[128]{0:T(256)(128)(2,1)S(1)} %reshape.159), channel_id=1, source_target_pairs={{0,1},{1,2},{2,3},{4,5},{5,6},{6,7},{8,9},{9,10},{10,11},{12,13},{... | collective-permute-start | bytes 776 | tf_op jit(solution)/shard_map/ppermute | solution.py:24
  192.2 1.5 copy-start.5
  206.6 2.5 %copy-start.1 = (bf16[896,896]{1,0:T(8,128)(2,1)S(1)}, bf16[896,896]{1,0:T(8,128)(2,1)}, u32[]{:S(2)}) copy-start(bf16[896,896]{1,0:T(8,128)(2,1)} %param.16) | copy-start | bytes 4816900
Sparse Core Ops, SparseCore 0:
  8.9 135.1 all-gather.1
where the time goes:
time: 217 us; the launch traced here: 216 us
  waiting for transfers between devices  89.5 us (41%)
  local copies, waits for them, and re-layouts  39.8 us (18%)
  matrix products  30.6 us (14%)
  blocking collectives  15.5 us (7%)
  other arithmetic  14.1 us (6%)
  between operations  13.6 us (6%)
  starting transfers between devices  12.9 us (6%)
    all_gather x1, waiting for transfers between devices, per_device(): lax.all_gather(cross_weight, 'span', axis=1, tiled=True)  62.6 us
    ppermute x2, waiting for transfers between devices, from_behind(): lax.ppermute(value, axis, [(source, source + steps) for source in range(i...  17.9 us
    all_to_all x1, blocking collectives, per_device(): lax.all_to_all(encoded, 'cache', split_axis=0, concat_axis=0, tiled=True)  15.5 us
    dot_general x1, matrix products, attend_cross(): jnp.einsum('ghqk,gkhd->gqhd', attention_weights, value_heads, preferred_e...  11.5 us
    all_to_all x1, waiting for transfers between devices, per_device(): lax.all_to_all(send_states, 'cache', split_axis=0, concat_axis=0, tiled=T...  8.22 us
    unnamed x25, local copies, waits for them, and re-layouts  7.8 us
    dot_general x1, matrix products, per_device(): jnp.dot(encoded_flat, lax.all_gather(cross_weight, 'span', axis=1, tiled=...  7.78 us
    reshape x1, local copies, waits for them, and re-layouts, per_device(): cross_states.reshape(blocks, NEIGHBOUR_COUNT * NEIGHBOUR_LENGTH, 2 * cros...  6.36 us
  transfers between devices with their start and end apart: 5, of which 3 were waited for; matrix products, arithmetic and copies ran while one was open for 23% of the time, Pallas kernels for 0%

commit v1 on v0

v1 whole, which is shorter than its diff:
```python
import functools
import math

import jax
import jax.numpy as jnp
from jax import lax
from jax.experimental import pallas as pl
from jax.experimental.pallas import tpu as pltpu
from jax.sharding import PartitionSpec as P

ENC_HEADS = 14
ENCODER_HEAD_DIM = 64
ENCODER_WIDTH = 896
CROSS_HEADS = 16
CROSS_HEAD = 128
BLOCK_LEN = 64
NEIGHBOUR_LENGTH = 64
NEIGHBOUR_COUNT = 2
CROSS_WIDTH = CROSS_HEADS * CROSS_HEAD
KEYS = NEIGHBOUR_COUNT * NEIGHBOUR_LENGTH
LANES = 128
FLAG_ROWS = 16
EDGE = 16

MASKED_SCORE = -1e30
AXES = ("groups", "cache", "span")
VMEM = pl.BlockSpec(memory_space=pltpu.VMEM)
SMEM = pl.BlockSpec(memory_space=pltpu.SMEM)
ANY = pl.BlockSpec(memory_space=pl.ANY)
NT = (((1,), (1,)), ((), ()))
TN = (((0,), (0,)), ((), ()))


def dot(a, b, dims=(((1,), (0,)), ((), ()))):
    return lax.dot_general(a, b, dims, preferred_element_type=jnp.float32)


def fetch_kernel(peers, capacity, cache_slots, *refs):
    wanted = refs[: peers - 1]
    cache_ref = refs[peers - 1]
    outs = refs[peers : 2 * peers - 1]
    sem = refs[2 * peers - 1]
    me = lax.axis_index("cache")
    counts = []
    for r in range(peers - 1):
        count = jnp.int32(0)
        for b in range(wanted[r].shape[0]):
            for n in range(NEIGHBOUR_COUNT):
                hit = (wanted[r][b, n] == me) & (count < capacity)
                slot = jnp.clip(wanted[r][b, NEIGHBOUR_COUNT + n], 0, cache_slots - 1)

                @pl.when(hit)
                def _(r=r, count=count, slot=slot):
                    pltpu.make_async_copy(
                        cache_ref.at[slot], outs[r].at[count], sem.at[r, count]
                    ).start()

                count = count + hit.astype(jnp.int32)
        counts.append(count)
    for r in range(peers - 1):
        for k in range(capacity):

            @pl.when(counts[r] > k)
            def _(r=r, k=k):
                pltpu.make_async_copy(cache_ref.at[0], outs[r].at[k], sem.at[r, k]).wait()


def encode_kernel(peers, capacity, blocks, *refs):
    owner_ref, slot_ref, lengths_ref, states_ref, weight_ref, cache_ref = refs[:6]
    arrived = refs[6 : 6 + peers - 1]
    out_ref, send_ref = refs[6 + peers - 1 : 8 + peers - 1]
    entries, queries, sem = refs[8 + peers - 1 :]
    me = lax.axis_index("cache")
    width = ENCODER_WIDTH
    requests = blocks * NEIGHBOUR_COUNT
    owners = [owner_ref[i // NEIGHBOUR_COUNT, i % NEIGHBOUR_COUNT] for i in range(requests)]
    for i in range(requests):
        rank = jnp.int32(0)
        for j in range(i):
            rank = rank + (owners[j] == owners[i]).astype(jnp.int32)
        rank = jnp.minimum(rank, capacity - 1)
        rel = owners[i] ^ me
        slot = slot_ref[i // NEIGHBOUR_COUNT, i % NEIGHBOUR_COUNT]

        @pl.when(rel == 0)
        def _(i=i, slot=slot):
            pltpu.make_async_copy(cache_ref.at[slot], entries.at[i], sem.at[i]).start()

        for r in range(1, peers):

            @pl.when(rel == r)
            def _(i=i, r=r, rank=rank):
                pltpu.make_async_copy(arrived[r - 1].at[rank], entries.at[i], sem.at[i]).start()

    low = lax.broadcasted_iota(jnp.int32, (BLOCK_LEN, LANES), 1) < ENCODER_HEAD_DIM
    per_pair = LANES // ENCODER_HEAD_DIM
    scale = 1.0 / math.sqrt(ENCODER_HEAD_DIM)
    for b in range(blocks):
        first = b * NEIGHBOUR_COUNT
        for i in range(first, first + NEIGHBOUR_COUNT):
            pltpu.make_async_copy(cache_ref.at[0], entries.at[i], sem.at[i]).wait()
        rows = entries[first : first + NEIGHBOUR_COUNT].reshape(KEYS, width)
        queries[...] = dot(rows, weight_ref[...]).astype(jnp.bfloat16)
        for p in range(width // LANES):
            cols = slice(p * LANES, (p + 1) * LANES)
            states = pl.ds(b * BLOCK_LEN, BLOCK_LEN)
            keys = states_ref[states, cols]
            values = states_ref[states, width + p * LANES : width + (p + 1) * LANES]
            zero = jnp.zeros_like(keys)
            keys = jnp.concatenate([jnp.where(low, keys, zero), jnp.where(low, zero, keys)], axis=0)
            values = jnp.concatenate(
                [jnp.where(low, values, zero), jnp.where(low, zero, values)], axis=0
            )
            scores = dot(keys, queries[:, cols], NT) * scale
            scores = scores.reshape(per_pair, BLOCK_LEN, KEYS)
            weights = jnp.exp(scores - jnp.max(scores, axis=1, keepdims=True))
            weights = weights * (1.0 / jnp.sum(weights, axis=1, keepdims=True))
            weights = weights.reshape(per_pair * BLOCK_LEN, KEYS).astype(jnp.bfloat16)
            attended = dot(weights, values, TN)
            owned = entries[first : first + NEIGHBOUR_COUNT, :, cols].reshape(KEYS, LANES)
            encoded = (owned.astype(jnp.float32) + attended).astype(jnp.bfloat16)
            out_ref[b * KEYS : (b + 1) * KEYS, cols] = encoded
            if b == blocks - 1:
                send_ref[:KEYS, cols] = encoded
    flags = usable_row(lengths_ref[blocks - 1, 0], lengths_ref[blocks - 1, 1]).astype(jnp.float32)
    send_ref[KEYS:, :] = jnp.zeros((FLAG_ROWS, width), jnp.bfloat16)
    send_ref[KEYS:, :LANES] = jnp.broadcast_to(flags, (FLAG_ROWS, LANES)).astype(jnp.bfloat16)


def usable_row(first, second):
    lane = lax.broadcasted_iota(jnp.int32, (1, KEYS), 1)
    limit = jnp.where(lane < NEIGHBOUR_LENGTH, first, second + NEIGHBOUR_LENGTH)
    return lane < limit


def cross_head(blocks, flags, encoded_ref, prior_ref, queries_ref, out_ref, head, first, second, swap):
    span = lax.axis_index("span")
    weights = jnp.concatenate([first, second], axis=1)
    columns = pl.ds(pl.multiple_of(head * CROSS_HEAD, CROSS_HEAD), CROSS_HEAD)
    scale = 1.0 / math.sqrt(CROSS_HEAD)
    own = dot(encoded_ref[...], weights).astype(jnp.bfloat16)
    before = dot(prior_ref[:KEYS, :], weights).astype(jnp.bfloat16)
    last_row = lax.broadcasted_iota(jnp.int32, (EDGE, CROSS_HEAD), 0) == EDGE - 1
    tail = None
    for u in range(-1, blocks):
        states = before if u < 0 else own[u * KEYS : (u + 1) * KEYS]
        left, right = states[:, :CROSS_HEAD], states[:, CROSS_HEAD:]
        if swap is None:
            keys, values = left, right
        else:
            keys, values = jnp.where(swap, right, left), jnp.where(swap, left, right)
        start = max(0, (u + 1) * BLOCK_LEN - EDGE)
        stop = min(blocks * BLOCK_LEN, (u + 2) * BLOCK_LEN)
        scores = dot(queries_ref[start:stop, columns], keys, NT) * scale
        scores = jnp.where(flags[u + 1], scores, MASKED_SCORE)
        parts = jnp.exp(scores - jnp.max(scores, axis=1, keepdims=True))
        parts = parts * (1.0 / jnp.sum(parts, axis=1, keepdims=True))
        result = dot(parts.astype(jnp.bfloat16), values).astype(jnp.bfloat16)
        if u < 0:
            result = jnp.where(span > 0, result, jnp.zeros_like(result))
        else:
            out_ref[start : start + EDGE, columns] = jnp.where(last_row, result[:EDGE], tail)
            result = result[EDGE:]
            start += EDGE
        if u < blocks - 1:
            out_ref[start : stop - EDGE, columns] = result[: stop - EDGE - start]
            tail = result[stop - EDGE - start :]


def block_flags(blocks, lengths_ref, prior_ref):
    flags = [prior_ref[KEYS : KEYS + FLAG_ROWS, :LANES].astype(jnp.float32)[:1] > 0.5]
    for b in range(blocks):
        flags.append(usable_row(lengths_ref[b, 0], lengths_ref[b, 1]))
    return flags


def cross_whole_kernel(
    blocks, lengths_ref, encoded_ref, prior_ref, queries_ref, weight_ref, out_ref
):
    flags = block_flags(blocks, lengths_ref, prior_ref)

    def step(head, carry):
        keys = pl.ds(pl.multiple_of(head * CROSS_HEAD, CROSS_HEAD), CROSS_HEAD)
        values = pl.ds(pl.multiple_of(CROSS_WIDTH + head * CROSS_HEAD, CROSS_HEAD), CROSS_HEAD)
        cross_head(
            blocks, flags, encoded_ref, prior_ref, queries_ref, out_ref,
            head, weight_ref[:, keys], weight_ref[:, values], None,
        )
        return carry

    lax.fori_loop(0, CROSS_HEADS, step, 0)


def piece_heads():
    core = lax.axis_index("cache") % 2
    near = jnp.where(core == 0, 4, 2)
    return [0, near, 6 - near, 6, 1, (6 - near) ^ 1, near ^ 1, 7]


def cross_pieces_kernel(blocks, lengths_ref, encoded_ref, prior_ref, queries_ref, weight_ref, *refs):
    slots = [None, refs[0:8], refs[8:16], refs[16:24]]
    out_ref = refs[24]
    span = lax.axis_index("span")
    place = lax.axis_index("groups") * 4 + lax.axis_index("cache")
    flags = block_flags(blocks, lengths_ref, prior_ref)
    offsets = piece_heads()
    swap = span >= 2
    for low in (1, 0):
        for k in range(8):
            column = offsets[k] ^ place
            head = ((low ^ span) & 1) * 8 + column
            if low == 0:
                first = weight_ref[
                    :, pl.ds(pl.multiple_of(column * CROSS_HEAD, CROSS_HEAD), CROSS_HEAD)
                ]
            else:
                first = slots[low][k][...]
            cross_head(
                blocks, flags, encoded_ref, prior_ref, queries_ref, out_ref,
                head, first, slots[low ^ 2][k][...], swap,
            )


def permute(value, move):
    sizes = [lax.axis_size(axis) for axis in AXES]
    pairs = []
    for g in range(sizes[0]):
        for c in range(sizes[1]):
            for s in range(sizes[2]):
                to = move(g, c, s)
                if to is not None:
                    flat = lambda p: (p[0] * sizes[1] + p[1]) * sizes[2] + p[2]
                    pairs.append((flat((g, c, s)), flat(to)))
    return lax.ppermute(value, AXES, pairs)


def gather_pieces(cross_weight):
    place = lax.axis_index("groups") * 4 + lax.axis_index("cache")
    span = lax.axis_index("span")
    own = lax.dynamic_slice_in_dim(cross_weight, place * CROSS_HEAD, CROSS_HEAD, axis=1)
    first = permute(own, lambda g, c, s: (g, c, s ^ 1))
    third = permute(own, lambda g, c, s: (g, c, s ^ 3))
    inner = (span == 1) | (span == 2)
    onward = jnp.where(inner, third, own)
    second = permute(onward, lambda g, c, s: (g, c, {0: 2, 1: 0, 2: 3, 3: 1}[s]))
    near = lambda g, c, s: (g ^ 1, c, s) if c % 2 == 0 else (g, c ^ 2, s)
    far = lambda g, c, s: (g ^ 1, c, s) if c % 2 == 1 else (g, c ^ 2, s)
    pieces = []
    for a in (first, second, third):
        b = permute(a, near)
        group = [a, b, permute(a, far), permute(b, far)]
        group += [permute(v, lambda g, c, s: (g, c ^ 1, s)) for v in group]
        pieces += group
    return pieces


def per_device(
    block_states,
    cross_queries,
    neighbour_cache,
    neighbour_owner,
    neighbour_slot,
    neighbour_lengths,
    encoder_query,
    cross_weight,
):
    peers = lax.axis_size("cache")
    spans = lax.axis_size("span")
    blocks = neighbour_owner.shape[0]
    requests = blocks * NEIGHBOUR_COUNT
    capacity = max(2, (requests + peers - 1) // peers)
    cache_slots = neighbour_cache.shape[0]
    swap = lambda v, r: lax.ppermute(v, "cache", [(i, i ^ r) for i in range(peers)])
    pieced = lax.axis_size("groups") == 2 and peers == 4 and spans == 4

    wanted = jnp.concatenate([neighbour_owner, neighbour_slot], axis=1)
    wanted = [swap(wanted, r) for r in range(1, peers)]
    if pieced:
        weights = gather_pieces(cross_weight)
    else:
        weights = lax.all_gather(cross_weight, "span", axis=1, tiled=True)
    entry = jax.ShapeDtypeStruct((capacity, NEIGHBOUR_LENGTH, ENCODER_WIDTH), jnp.bfloat16)
    fetched = pl.pallas_call(
        functools.partial(fetch_kernel, peers, capacity, cache_slots),
        out_shape=[entry] * (peers - 1),
        in_specs=[SMEM] * (peers - 1) + [ANY],
        out_specs=[ANY] * (peers - 1),
        scratch_shapes=[pltpu.SemaphoreType.DMA((peers - 1, capacity))],
        name="fetch",
    )(*wanted, neighbour_cache)
    arrived = [swap(v, r) for r, v in enumerate(fetched, 1)]
    encoded, outgoing = pl.pallas_call(
        functools.partial(encode_kernel, peers, capacity, blocks),
        out_shape=[
            jax.ShapeDtypeStruct((blocks * KEYS, ENCODER_WIDTH), jnp.bfloat16),
            jax.ShapeDtypeStruct((KEYS + FLAG_ROWS, ENCODER_WIDTH), jnp.bfloat16),
        ],
        in_specs=[SMEM] * 3 + [VMEM] * 2 + [ANY] * peers,
        out_specs=[VMEM] * 2,
        scratch_shapes=[
            pltpu.VMEM((requests, NEIGHBOUR_LENGTH, ENCODER_WIDTH), jnp.bfloat16),
            pltpu.VMEM((KEYS, ENCODER_WIDTH), jnp.bfloat16),
            pltpu.SemaphoreType.DMA((requests,)),
        ],
        compiler_params=pltpu.CompilerParams(vmem_limit_bytes=16 * 2**20),
        name="encode",
    )(
        neighbour_owner, neighbour_slot, neighbour_lengths, block_states, encoder_query,
        neighbour_cache, *arrived,
    )
    prior = lax.ppermute(outgoing, "span", [(i, i + 1) for i in range(spans - 1)])
    kernel = cross_pieces_kernel if pieced else cross_whole_kernel
    operands = [cross_weight, *weights] if pieced else [weights]
    return pl.pallas_call(
        functools.partial(kernel, blocks),
        out_shape=jax.ShapeDtypeStruct(cross_queries.shape, jnp.bfloat16),
        in_specs=[SMEM] + [VMEM] * (3 + len(operands)),
        out_specs=VMEM,
        compiler_params=pltpu.CompilerParams(vmem_limit_bytes=32 * 2**20),
        name="cross",
    )(neighbour_lengths, encoded, prior, cross_queries, *operands)


def solution(mesh):
    placed = (
        P(("groups", "cache", "span"), None),
        P(("groups", "cache", "span"), None),
        P(("groups", "cache"), None, None),
        P(("groups", "cache", "span"), None),
        P(("groups", "cache", "span"), None),
        P(("groups", "cache", "span"), None),
        P(),
        P(None, "span"),
    )
    return jax.shard_map(
        per_device,
        mesh=mesh,
        in_specs=placed,
        out_specs=P(("groups", "cache", "span"), None),
        check_vma=False,
    )
```

time: 217 us -> 123 us (0.57)
  Pallas kernels: 0 us -> 64.5 us
  waiting for transfers between devices: 89.5 us -> 26.9 us
  local copies, waits for them, and re-layouts: 39.8 us -> 5.98 us
  matrix products: 30.6 us -> 0 us
  blocking collectives: 15.5 us -> 0 us
  between operations: 13.6 us -> 0.1 us
  other arithmetic: 14.1 us -> 1.78 us
  starting transfers between devices: 12.9 us -> 23 us
    pallas_call x0 -> x3, Pallas kernels: none -> 64.5 us  [the longest x1 31 us: per_device(): pl.pallas_call(functools.partial(kernel, blocks), out_shape=jax.ShapeDtyp...]
    all_gather x1 -> x0, waiting for transfers between devices: 62.6 us -> none  [per_device(): lax.all_gather(cross_weight, 'span', axis=1, tiled=True)]
    dot_general x8 -> x0, matrix products: 30.6 us -> none  [the longest x1 11.5 us: attend_cross(): jnp.einsum('ghqk,gkhd->gqhd', attention_weights, value_heads, preferred_e...]
    ppermute x2 -> x31, starting transfers between devices: 5.02 us -> 23 us  [the longest x24 17.5 us: permute(): return lax.ppermute(value, AXES, pairs)]
    reshape x7 -> x0, local copies, waits for them, and re-layouts: 17.5 us -> none  [the longest x1 6.36 us: per_device(): cross_states.reshape(blocks, NEIGHBOUR_COUNT * NEIGHBOUR_LENGTH, 2 * cros...]
    all_to_all x1 -> x0, blocking collectives: 15.5 us -> none  [per_device(): lax.all_to_all(encoded, 'cache', split_axis=0, concat_axis=0, tiled=True)]
    ppermute x2 -> x31, waiting for transfers between devices: 17.9 us -> 26.9 us  [the longest x24 16.6 us: permute(): return lax.ppermute(value, AXES, pairs)]
    all_to_all x2 -> x0, waiting for transfers between devices: 8.22 us -> none  [the longest x1 8.22 us: per_device(): lax.all_to_all(send_states, 'cache', split_axis=0, concat_axis=0, tiled=T...]
  transfers between devices with their start and end apart: 5 -> 31, of which waited for: 3 -> 11; matrix products, arithmetic and copies ran while one was open for 23% -> 3% of each run, Pallas kernels for 0% -> 27%
where the time goes in v1:
time: 123 us; the launch traced here: 122 us
  Pallas kernels  64.5 us (52%)
  waiting for transfers between devices  26.9 us (22%)
  starting transfers between devices  23 us (19%)
  local copies, waits for them, and re-layouts  5.98 us (5%)
  other arithmetic  1.78 us (1%)
    pallas_call x1, Pallas kernels, per_device(): pl.pallas_call(functools.partial(kernel, blocks), out_shape=jax.ShapeDtyp...  31 us
    pallas_call x1, Pallas kernels, per_device(): pl.pallas_call(functools.partial(fetch_kernel, peers, capacity, cache_slo...  22.8 us
    ppermute x24, starting transfers between devices, permute(): return lax.ppermute(value, AXES, pairs)  17.5 us
    ppermute x24, waiting for transfers between devices, permute(): return lax.ppermute(value, AXES, pairs)  16.6 us
    pallas_call x1, Pallas kernels, per_device(): pl.pallas_call(functools.partial(encode_kernel, peers, capacity, blocks),...  10.6 us
    ppermute x6, waiting for transfers between devices, per_device(): lax.ppermute(v, 'cache', [(i, i ^ r) for i in range(peers)])  10.3 us
    unnamed x21, local copies, waits for them, and re-layouts  4.2 us
    ppermute x6, starting transfers between devices, per_device(): lax.ppermute(v, 'cache', [(i, i ^ r) for i in range(peers)])  3.8 us
  transfers between devices with their start and end apart: 31, of which 11 were waited for; matrix products, arithmetic and copies ran while one was open for 3% of the time, Pallas kernels for 27%

profile of v1, /device:TPU:0, one launch (start us, length us, event | category | flops | bytes accessed | tf_op | source)
XLA Modules:
  0.0 122.3 jit_solution(15019765408231692132)
XLA Ops:
  0.0 1.8 %constant_dynamic-slice_fusion = bf16[896,128]{1,0:T(8,128)(2,1)} fusion(bf16[896,1024]{1,0:T(8,128)(2,1)} %weight_ref.1, s32[]{:T(128)S(6)} %select_n.11), kind=kLoop, calls=%fused_computation.2 | loop fusion | bytes 458756 | tf_op jit(solution)/shard_map/dynamic_slice | solution.py:240
  1.8 5.1 %collective-permute-start.15 = (bf16[896,128]{1,0:T(8,128)(2,1)}, bf16[896,128]{1,0:T(8,128)(2,1)S(1)}, u32[]{:S(2)}, u32[]{:S(2)}) collective-permute-start(bf16[896,128]{1,0:T(8,128)(2,1)} %constant_dynamic-slice_fusion), channel_id=1, source_target_pairs={{0,3},{1,2},{2,1},{3,0},{4,7},{5,6},{6,5},{7,4},{8,11},{9,10},{10,... | collective-permute-start | bytes 688136 | tf_op jit(solution)/shard_map/ppermute | solution.py:234
  6.8 0.8 copy.11.refs_0_
  7.6 0.8 copy.12.refs_1_
  8.4 0.7 collective-permute-start.2
  9.1 0.9 collective-permute-start.1
  10.3 1.1 collective-permute-done.2.refs_2_
  11.5 1.3 %collective-permute-done.1.refs_1_ = s32[4,4]{1,0:T(4,128)S(1)} collective-permute-done((s32[4,4]{1,0:T(4,128)S(1)}, s32[4,4]{1,0:T(4,128)S(1)}, u32[]{:S(2)}, u32[]{:S(2)}) %collective-permute-start.1) | collective-permute-done | bytes 96 | tf_op jit(solution)/shard_map/ppermute | solution.py:273
  13.9 22.8 %fetch.1 = (bf16[2,64,896]{2,1,0:T(8,128)(2,1)}, bf16[2,64,896]{2,1,0:T(8,128)(2,1)}, bf16[2,64,896]{2,1,0:T(8,128)(2,1)}) custom-call(s32[4,4]{1,0:T(4,128)} %copy-done.7, s32[4,4]{1,0:T(4,128)} %copy-done.6, s32[4,4]{1,0:T(4,128)} %copy-done.5, bf16[8,64,896]{2,1,0:T(8,128)(2,1)} %refs_5_.1), custom_call_target="tpu_custom_call" | custom-call | tf_op jit(solution)/shard_map/fetch/pallas_call | solution.py:283
  36.8 0.9 collective-permute-start.4
  37.7 0.9 collective-permute-start.5
  38.6 1.7 %broadcast_select_fusion = bf16[896,128]{1,0:T(8,128)(2,1)} fusion(bf16[896,128]{1,0:T(8,128)(2,1)S(1)} %collective-permute-done.15.refs_16_, pred[]{:T(512)S(6)} %or.3, bf16[896,1024]{1,0:T(8,128)(2,1)} %weight_ref.1, s32[]{:T(128)S(6)} %select_n.11), kind=kLoop, calls=%fused_computation | loop fusion | flops 114688 | bytes 688133 | tf_op jit(solution)/shard_map/jit(_where)/select_n | solution.py:244
  40.7 4.8 %collective-permute-done.4.refs_7_ = bf16[2,64,896]{2,1,0:T(8,128)(2,1)S(1)} collective-permute-done((bf16[2,64,896]{2,1,0:T(8,128)(2,1)}, bf16[2,64,896]{2,1,0:T(8,128)(2,1)S(1)}, u32[]{:S(2)}, u32[]{:S(2)}) %collective-permute-start.4) | collective-permute-done | bytes 229408 | tf_op jit(solution)/shard_map/ppermute | solution.py:273
  45.4 0.9 collective-permute-start.25
  46.4 3.1 %collective-permute-done.5.refs_8_ = bf16[2,64,896]{2,1,0:T(8,128)(2,1)} collective-permute-done((bf16[2,64,896]{2,1,0:T(8,128)(2,1)}, bf16[2,64,896]{2,1,0:T(8,128)(2,1)}, u32[]{:S(2)}, u32[]{:S(2)}) %collective-permute-start.5) | collective-permute-done | bytes 229408 | tf_op jit(solution)/shard_map/ppermute | solution.py:273
  49.6 1.4 %copy-done.2 = bf16[896,896]{1,0:T(8,128)(2,1)S(1)} copy-done((bf16[896,896]{1,0:T(8,128)(2,1)S(1)}, bf16[896,896]{1,0:T(8,128)(2,1)}, u32[]{:S(2)}) %copy-start.2) | copy-done | bytes 1605656
  51.0 10.6 %encode.1 = (bf16[512,896]{1,0:T(8,128)(2,1)S(1)}, bf16[144,896]{1,0:T(8,128)(2,1)S(1)}) custom-call(s32[4,2]{1,0:T(4,128)S(1)} %copy.11.refs_0_, s32[4,2]{1,0:T(4,128)S(1)} %copy.12.refs_1_, s32[4,2]{1,0:T(4,128)S(1)} %copy.14.refs_2_.lengths_ref, bf16[256,1792]{1,0:T(8,128)(2,1)S(1)} %copy-done.4, bf16[896,896]{1,0:T(8,128)(2,1)S(1)} %copy-done.2, ...), custom_call_target="tpu_custom_call" | custom-call | tf_op jit(solution)/shard_map/encode/pallas_call | solution.py:292
  61.6 1.7 %collective-permute-start.6 = (bf16[144,896]{1,0:T(8,128)(2,1)S(1)}, bf16[144,896]{1,0:T(8,128)(2,1)S(1)}, u32[]{:S(2)}, u32[]{:S(2)}) collective-permute-start(bf16[144,896]{1,0:T(8,128)(2,1)S(1)} %get-tuple-element.14), channel_id=1, source_target_pairs={{0,1},{1,2},{2,3},{4,5},{5,6},{6,7},{8,9},{9,10},{10,11},{12,13},{... | collective-permute-start | bytes 774152 | tf_op jit(solution)/shard_map/ppermute | solution.py:311
  63.3 1.6 %collective-permute-start.24 = (bf16[896,128]{1,0:T(8,128)(2,1)S(1)}, bf16[896,128]{1,0:T(8,128)(2,1)S(1)}, u32[]{:S(2)}, u32[]{:S(2)}) collective-permute-start(bf16[896,128]{1,0:T(8,128)(2,1)S(1)} %collective-permute-done.15.refs_16_), channel_id=1, source_target_pairs={{0,16},{1,17},{2,18},{3,19},{4,12},{5,13},{6,14},{7,15},{8,24},{9,... | collective-permute-start | bytes 688136 | tf_op jit(solution)/shard_map/ppermute | solution.py:234
  64.9 1.6 %collective-permute-start.9 = (bf16[896,128]{1,0:T(8,128)(2,1)S(1)}, bf16[896,128]{1,0:T(8,128)(2,1)S(1)}, u32[]{:S(2)}, u32[]{:S(2)}) collective-permute-start(bf16[896,128]{1,0:T(8,128)(2,1)S(1)} %collective-permute-done.7.refs_0_), channel_id=1, source_target_pairs={{0,8},{1,9},{2,10},{3,11},{4,20},{5,21},{6,22},{7,23},{8,0},{9,1},... | collective-permute-start | bytes 688136 | tf_op jit(solution)/shard_map/ppermute | solution.py:234
  67.0 3.8 %collective-permute-done.24.refs_17_ = bf16[896,128]{1,0:T(8,128)(2,1)S(1)} collective-permute-done((bf16[896,128]{1,0:T(8,128)(2,1)S(1)}, bf16[896,128]{1,0:T(8,128)(2,1)S(1)}, u32[]{:S(2)}, u32[]{:S(2)}) %collective-permute-start.24) | collective-permute-done | bytes 229408 | tf_op jit(solution)/shard_map/ppermute | solution.py:234
  70.8 1.5 %collective-permute-start.18 = (bf16[896,128]{1,0:T(8,128)(2,1)S(1)}, bf16[896,128]{1,0:T(8,128)(2,1)S(1)}, u32[]{:S(2)}, u32[]{:S(2)}) collective-permute-start(bf16[896,128]{1,0:T(8,128)(2,1)S(1)} %collective-permute-done.16.refs_8_), channel_id=1, source_target_pairs={{0,8},{1,9},{2,10},{3,11},{4,20},{5,21},{6,22},{7,23},{8,0},{9,1},... | collective-permute-start | bytes 688136 | tf_op jit(solution)/shard_map/ppermute | solution.py:234
  72.4 1.1 collective-permute-done.9.refs_2_
  73.5 1.4 %collective-permute-start.17 = (bf16[896,128]{1,0:T(8,128)(2,1)S(1)}, bf16[896,128]{1,0:T(8,128)(2,1)S(1)}, u32[]{:S(2)}, u32[]{:S(2)}) collective-permute-start(bf16[896,128]{1,0:T(8,128)(2,1)S(1)} %collective-permute-done.16.refs_8_), channel_id=1, source_target_pairs={{0,16},{1,17},{2,18},{3,19},{4,12},{5,13},{6,14},{7,15},{8,24},{9,... | collective-permute-start | bytes 688136 | tf_op jit(solution)/shard_map/ppermute | solution.py:234
  75.4 1.0 collective-permute-start.26
  76.4 1.3 %collective-permute-done.18.refs_10_ = bf16[896,128]{1,0:T(8,128)(2,1)S(1)} collective-permute-done((bf16[896,128]{1,0:T(8,128)(2,1)S(1)}, bf16[896,128]{1,0:T(8,128)(2,1)S(1)}, u32[]{:S(2)}, u32[]{:S(2)}) %collective-permute-start.18) | collective-permute-done | bytes 229408 | tf_op jit(solution)/shard_map/ppermute | solution.py:234
  77.7 3.2 %collective-permute-done.17.refs_9_ = bf16[896,128]{1,0:T(8,128)(2,1)S(1)} collective-permute-done((bf16[896,128]{1,0:T(8,128)(2,1)S(1)}, bf16[896,128]{1,0:T(8,128)(2,1)S(1)}, u32[]{:S(2)}, u32[]{:S(2)}) %collective-permute-start.17) | collective-permute-done | bytes 229408 | tf_op jit(solution)/shard_map/ppermute | solution.py:234
  80.9 2.3 %collective-permute-start.10 = (bf16[896,128]{1,0:T(8,128)(2,1)S(1)}, bf16[896,128]{1,0:T(8,128)(2,1)S(1)}, u32[]{:S(2)}, u32[]{:S(2)}) collective-permute-start(bf16[896,128]{1,0:T(8,128)(2,1)S(1)} %collective-permute-done.8.refs_1_), channel_id=1, source_target_pairs={{0,8},{1,9},{2,10},{3,11},{4,20},{5,21},{6,22},{7,23},{8,0},{9,1},... | collective-permute-start | bytes 688136 | tf_op jit(solution)/shard_map/ppermute | solution.py:234
  84.0 3.3 %collective-permute-done.10.refs_3_ = bf16[896,128]{1,0:T(8,128)(2,1)S(1)} collective-permute-done((bf16[896,128]{1,0:T(8,128)(2,1)S(1)}, bf16[896,128]{1,0:T(8,128)(2,1)S(1)}, u32[]{:S(2)}, u32[]{:S(2)}) %collective-permute-start.10) | collective-permute-done | bytes 229408 | tf_op jit(solution)/shard_map/ppermute | solution.py:234
  87.3 2.5 %collective-permute-done.19.refs_11_ = bf16[896,128]{1,0:T(8,128)(2,1)S(1)} collective-permute-done((bf16[896,128]{1,0:T(8,128)(2,1)S(1)}, bf16[896,128]{1,0:T(8,128)(2,1)S(1)}, u32[]{:S(2)}, u32[]{:S(2)}) %collective-permute-start.19) | collective-permute-done | bytes 229408 | tf_op jit(solution)/shard_map/ppermute | solution.py:234
  89.8 1.5 %collective-permute-done.23.refs_15_ = bf16[896,128]{1,0:T(8,128)(2,1)S(1)} collective-permute-done((bf16[896,128]{1,0:T(8,128)(2,1)S(1)}, bf16[896,128]{1,0:T(8,128)(2,1)S(1)}, u32[]{:S(2)}, u32[]{:S(2)}) %collective-permute-start.23) | collective-permute-done | bytes 229408 | tf_op jit(solution)/shard_map/ppermute | solution.py:234
  91.2 31.0 %cross.1 = bf16[256,2048]{1,0:T(8,128)(2,1)} custom-call(s32[4,2]{1,0:T(4,128)S(1)} %copy.14.refs_2_.lengths_ref, bf16[512,896]{1,0:T(8,128)(2,1)S(1)} %get-tuple-element.13.encoded_ref, bf16[144,896]{1,0:T(8,128)(2,1)S(1)} %collective-permute-done.6.prior_ref, bf16[256,2048]{1,0:T(8,128)(2,1)S(1)} %copy-done.3, bf16[896,1024]{1,0:T(8,128)(2,1)S(1)} %copy-done.1, ...), custom_call_target="tpu_custom_call" | custom-call | tf_op jit(solution)/shard_map/cross/pallas_call | solution.py:314
  (57 shorter events, 3.9 us)
Async XLA Ops:
  0.0 49.6 %copy-start = (bf16[8,64,896]{2,1,0:T(8,128)(2,1)S(1)}, bf16[8,64,896]{2,1,0:T(8,128)(2,1)}, u32[]{:S(2)}) copy-start(bf16[8,64,896]{2,1,0:T(8,128)(2,1)} %refs_5_.1) | copy-start | bytes 2752516
  1.8 36.8 %collective-permute-start.15 = (bf16[896,128]{1,0:T(8,128)(2,1)}, bf16[896,128]{1,0:T(8,128)(2,1)S(1)}, u32[]{:S(2)}, u32[]{:S(2)}) collective-permute-start(bf16[896,128]{1,0:T(8,128)(2,1)} %constant_dynamic-slice_fusion), channel_id=1, source_target_pairs={{0,3},{1,2},{2,1},{3,0},{4,7},{5,6},{6,5},{7,4},{8,11},{9,10},{10,... | collective-permute-start | bytes 688136 | tf_op jit(solution)/shard_map/ppermute | solution.py:234
  8.4 3.0 %collective-permute-start.2 = (s32[4,4]{1,0:T(4,128)S(1)}, s32[4,4]{1,0:T(4,128)S(1)}, u32[]{:S(2)}, u32[]{:S(2)}) collective-permute-start(s32[4,4]{1,0:T(4,128)S(1)} %pad_add_fusion), channel_id=1, source_target_pairs={{0,12},{4,8},{8,4},{12,0},{1,13},{5,9},{9,5},{13,1},{2,14},{6,10},... | collective-permute-start | bytes 200 | tf_op jit(solution)/shard_map/ppermute | solution.py:273
  9.1 3.6 %collective-permute-start.1 = (s32[4,4]{1,0:T(4,128)S(1)}, s32[4,4]{1,0:T(4,128)S(1)}, u32[]{:S(2)}, u32[]{:S(2)}) collective-permute-start(s32[4,4]{1,0:T(4,128)S(1)} %pad_add_fusion), channel_id=1, source_target_pairs={{0,8},{4,12},{8,0},{12,4},{1,9},{5,13},{9,1},{13,5},{2,10},{6,14},... | collective-permute-start | bytes 200 | tf_op jit(solution)/shard_map/ppermute | solution.py:273
  10.0 2.7 %collective-permute-start = (s32[4,4]{1,0:T(4,128)S(1)}, s32[4,4]{1,0:T(4,128)S(1)}, u32[]{:S(2)}, u32[]{:S(2)}) collective-permute-start(s32[4,4]{1,0:T(4,128)S(1)} %pad_add_fusion), channel_id=1, source_target_pairs={{0,4},{4,0},{8,12},{12,8},{1,5},{5,1},{9,13},{13,9},{2,6},{6,2},{1... | collective-permute-start | bytes 200 | tf_op jit(solution)/shard_map/ppermute | solution.py:273
  10.3 53.0 %collective-permute-start.7 = (bf16[896,128]{1,0:T(8,128)(2,1)}, bf16[896,128]{1,0:T(8,128)(2,1)S(1)}, u32[]{:S(2)}, u32[]{:S(2)}) collective-permute-start(bf16[896,128]{1,0:T(8,128)(2,1)} %constant_dynamic-slice_fusion), channel_id=1, source_target_pairs={{0,1},{1,0},{2,3},{3,2},{4,5},{5,4},{6,7},{7,6},{8,9},{9,8},{10,11... | collective-permute-start | bytes 688136 | tf_op jit(solution)/shard_map/ppermute | solution.py:234
  36.7 3.7 %collective-permute-start.3 = (bf16[2,64,896]{2,1,0:T(8,128)(2,1)}, bf16[2,64,896]{2,1,0:T(8,128)(2,1)S(1)}, u32[]{:S(2)}, u32[]{:S(2)}) collective-permute-start(bf16[2,64,896]{2,1,0:T(8,128)(2,1)} %get-tuple-element.10), channel_id=1, source_target_pairs={{0,4},{4,0},{8,12},{12,8},{1,5},{5,1},{9,13},{13,9},{2,6},{6,2},{1... | collective-permute-start | bytes 688136 | tf_op jit(solution)/shard_map/ppermute | solution.py:273
  36.8 8.6 %collective-permute-start.4 = (bf16[2,64,896]{2,1,0:T(8,128)(2,1)}, bf16[2,64,896]{2,1,0:T(8,128)(2,1)S(1)}, u32[]{:S(2)}, u32[]{:S(2)}) collective-permute-start(bf16[2,64,896]{2,1,0:T(8,128)(2,1)} %get-tuple-element.11), channel_id=1, source_target_pairs={{0,8},{4,12},{8,0},{12,4},{1,9},{5,13},{9,1},{13,5},{2,10},{6,14},... | collective-permute-start | bytes 688136 | tf_op jit(solution)/shard_map/ppermute | solution.py:273
  37.7 11.8 %collective-permute-start.5 = (bf16[2,64,896]{2,1,0:T(8,128)(2,1)}, bf16[2,64,896]{2,1,0:T(8,128)(2,1)}, u32[]{:S(2)}, u32[]{:S(2)}) collective-permute-start(bf16[2,64,896]{2,1,0:T(8,128)(2,1)} %get-tuple-element.12), channel_id=1, source_target_pairs={{0,12},{4,8},{8,4},{12,0},{1,13},{5,9},{9,5},{13,1},{2,14},{6,10},... | collective-permute-start | bytes 688136 | tf_op jit(solution)/shard_map/ppermute | solution.py:273
  40.3 24.6 %collective-permute-start.16 = (bf16[896,128]{1,0:T(8,128)(2,1)}, bf16[896,128]{1,0:T(8,128)(2,1)S(1)}, u32[]{:S(2)}, u32[]{:S(2)}) collective-permute-start(bf16[896,128]{1,0:T(8,128)(2,1)} %broadcast_select_fusion), channel_id=1, source_target_pairs={{0,2},{1,0},{2,3},{3,1},{4,6},{5,4},{6,7},{7,5},{8,10},{9,8},{10,1... | collective-permute-start | bytes 688136 | tf_op jit(solution)/shard_map/ppermute | solution.py:234
  40.3 24.6 %collective-permute-start.27 = (bf16[896,128]{1,0:T(8,128)(2,1)S(1)}, bf16[896,128]{1,0:T(8,128)(2,1)S(1)}, u32[]{:S(2)}, u32[]{:S(2)}) collective-permute-start(bf16[896,128]{1,0:T(8,128)(2,1)S(1)} %collective-permute-done.15.refs_16_), channel_id=1, source_target_pairs={{0,4},{1,5},{2,6},{3,7},{4,0},{5,1},{6,2},{7,3},{8,12},{9,13},{10,... | collective-permute-start | bytes 688136 | tf_op jit(solution)/shard_map/ppermute | solution.py:234
  45.4 21.1 %collective-permute-start.25 = (bf16[896,128]{1,0:T(8,128)(2,1)S(1)}, bf16[896,128]{1,0:T(8,128)(2,1)S(1)}, u32[]{:S(2)}, u32[]{:S(2)}) collective-permute-start(bf16[896,128]{1,0:T(8,128)(2,1)S(1)} %collective-permute-done.15.refs_16_), channel_id=1, source_target_pairs={{0,8},{1,9},{2,10},{3,11},{4,20},{5,21},{6,22},{7,23},{8,0},{9,1},... | collective-permute-start | bytes 688136 | tf_op jit(solution)/shard_map/ppermute | solution.py:234
  61.6 13.2 %collective-permute-start.6 = (bf16[144,896]{1,0:T(8,128)(2,1)S(1)}, bf16[144,896]{1,0:T(8,128)(2,1)S(1)}, u32[]{:S(2)}, u32[]{:S(2)}) collective-permute-start(bf16[144,896]{1,0:T(8,128)(2,1)S(1)} %get-tuple-element.14), channel_id=1, source_target_pairs={{0,1},{1,2},{2,3},{4,5},{5,6},{6,7},{8,9},{9,10},{10,11},{12,13},{... | collective-permute-start | bytes 774152 | tf_op jit(solution)/shard_map/ppermute | solution.py:311
  63.3 7.5 %collective-permute-start.24 = (bf16[896,128]{1,0:T(8,128)(2,1)S(1)}, bf16[896,128]{1,0:T(8,128)(2,1)S(1)}, u32[]{:S(2)}, u32[]{:S(2)}) collective-permute-start(bf16[896,128]{1,0:T(8,128)(2,1)S(1)} %collective-permute-done.15.refs_16_), channel_id=1, source_target_pairs={{0,16},{1,17},{2,18},{3,19},{4,12},{5,13},{6,14},{7,15},{8,24},{9,... | collective-permute-start | bytes 688136 | tf_op jit(solution)/shard_map/ppermute | solution.py:234
  64.9 5.9 %collective-permute-start.11 = (bf16[896,128]{1,0:T(8,128)(2,1)S(1)}, bf16[896,128]{1,0:T(8,128)(2,1)S(1)}, u32[]{:S(2)}, u32[]{:S(2)}) collective-permute-start(bf16[896,128]{1,0:T(8,128)(2,1)S(1)} %collective-permute-done.7.refs_0_), channel_id=1, source_target_pairs={{0,4},{1,5},{2,6},{3,7},{4,0},{5,1},{6,2},{7,3},{8,12},{9,13},{10,... | collective-permute-start | bytes 688136 | tf_op jit(solution)/shard_map/ppermute | solution.py:234
  64.9 8.5 %collective-permute-start.9 = (bf16[896,128]{1,0:T(8,128)(2,1)S(1)}, bf16[896,128]{1,0:T(8,128)(2,1)S(1)}, u32[]{:S(2)}, u32[]{:S(2)}) collective-permute-start(bf16[896,128]{1,0:T(8,128)(2,1)S(1)} %collective-permute-done.7.refs_0_), channel_id=1, source_target_pairs={{0,8},{1,9},{2,10},{3,11},{4,20},{5,21},{6,22},{7,23},{8,0},{9,1},... | collective-permute-start | bytes 688136 | tf_op jit(solution)/shard_map/ppermute | solution.py:234
  66.5 8.3 %collective-permute-start.8 = (bf16[896,128]{1,0:T(8,128)(2,1)S(1)}, bf16[896,128]{1,0:T(8,128)(2,1)S(1)}, u32[]{:S(2)}, u32[]{:S(2)}) collective-permute-start(bf16[896,128]{1,0:T(8,128)(2,1)S(1)} %collective-permute-done.7.refs_0_), channel_id=1, source_target_pairs={{0,16},{1,17},{2,18},{3,19},{4,12},{5,13},{6,14},{7,15},{8,24},{9,... | collective-permute-start | bytes 688136 | tf_op jit(solution)/shard_map/ppermute | solution.py:234
  70.8 4.6 %collective-permute-start.20 = (bf16[896,128]{1,0:T(8,128)(2,1)S(1)}, bf16[896,128]{1,0:T(8,128)(2,1)S(1)}, u32[]{:S(2)}, u32[]{:S(2)}) collective-permute-start(bf16[896,128]{1,0:T(8,128)(2,1)S(1)} %collective-permute-done.16.refs_8_), channel_id=1, source_target_pairs={{0,4},{1,5},{2,6},{3,7},{4,0},{5,1},{6,2},{7,3},{8,12},{9,13},{10,... | collective-permute-start | bytes 688136 | tf_op jit(solution)/shard_map/ppermute | solution.py:234
  70.8 6.9 %collective-permute-start.18 = (bf16[896,128]{1,0:T(8,128)(2,1)S(1)}, bf16[896,128]{1,0:T(8,128)(2,1)S(1)}, u32[]{:S(2)}, u32[]{:S(2)}) collective-permute-start(bf16[896,128]{1,0:T(8,128)(2,1)S(1)} %collective-permute-done.16.refs_8_), channel_id=1, source_target_pairs={{0,8},{1,9},{2,10},{3,11},{4,20},{5,21},{6,22},{7,23},{8,0},{9,1},... | collective-permute-start | bytes 688136 | tf_op jit(solution)/shard_map/ppermute | solution.py:234
  73.5 7.5 %collective-permute-start.17 = (bf16[896,128]{1,0:T(8,128)(2,1)S(1)}, bf16[896,128]{1,0:T(8,128)(2,1)S(1)}, u32[]{:S(2)}, u32[]{:S(2)}) collective-permute-start(bf16[896,128]{1,0:T(8,128)(2,1)S(1)} %collective-permute-done.16.refs_8_), channel_id=1, source_target_pairs={{0,16},{1,17},{2,18},{3,19},{4,12},{5,13},{6,14},{7,15},{8,24},{9,... | collective-permute-start | bytes 688136 | tf_op jit(solution)/shard_map/ppermute | solution.py:234
  74.9 6.1 %collective-permute-start.29 = (bf16[896,128]{1,0:T(8,128)(2,1)S(1)}, bf16[896,128]{1,0:T(8,128)(2,1)S(1)}, u32[]{:S(2)}, u32[]{:S(2)}) collective-permute-start(bf16[896,128]{1,0:T(8,128)(2,1)S(1)} %collective-permute-done.25.refs_18_), channel_id=1, source_target_pairs={{0,4},{1,5},{2,6},{3,7},{4,0},{5,1},{6,2},{7,3},{8,12},{9,13},{10,... | collective-permute-start | bytes 688136 | tf_op jit(solution)/shard_map/ppermute | solution.py:234
  74.9 8.4 %collective-permute-start.28 = (bf16[896,128]{1,0:T(8,128)(2,1)S(1)}, bf16[896,128]{1,0:T(8,128)(2,1)S(1)}, u32[]{:S(2)}, u32[]{:S(2)}) collective-permute-start(bf16[896,128]{1,0:T(8,128)(2,1)S(1)} %collective-permute-done.24.refs_17_), channel_id=1, source_target_pairs={{0,4},{1,5},{2,6},{3,7},{4,0},{5,1},{6,2},{7,3},{8,12},{9,13},{10,... | collective-permute-start | bytes 688136 | tf_op jit(solution)/shard_map/ppermute | solution.py:234
  75.4 8.0 %collective-permute-start.26 = (bf16[896,128]{1,0:T(8,128)(2,1)S(1)}, bf16[896,128]{1,0:T(8,128)(2,1)S(1)}, u32[]{:S(2)}, u32[]{:S(2)}) collective-permute-start(bf16[896,128]{1,0:T(8,128)(2,1)S(1)} %collective-permute-done.24.refs_17_), channel_id=1, source_target_pairs={{0,8},{1,9},{2,10},{3,11},{4,20},{5,21},{6,22},{7,23},{8,0},{9,1},... | collective-permute-start | bytes 688136 | tf_op jit(solution)/shard_map/ppermute | solution.py:234
  77.7 5.8 %collective-permute-start.13 = (bf16[896,128]{1,0:T(8,128)(2,1)S(1)}, bf16[896,128]{1,0:T(8,128)(2,1)S(1)}, u32[]{:S(2)}, u32[]{:S(2)}) collective-permute-start(bf16[896,128]{1,0:T(8,128)(2,1)S(1)} %collective-permute-done.9.refs_2_), channel_id=1, source_target_pairs={{0,4},{1,5},{2,6},{3,7},{4,0},{5,1},{6,2},{7,3},{8,12},{9,13},{10,... | collective-permute-start | bytes 688136 | tf_op jit(solution)/shard_map/ppermute | solution.py:234
  80.9 3.0 %collective-permute-start.12 = (bf16[896,128]{1,0:T(8,128)(2,1)S(1)}, bf16[896,128]{1,0:T(8,128)(2,1)S(1)}, u32[]{:S(2)}, u32[]{:S(2)}) collective-permute-start(bf16[896,128]{1,0:T(8,128)(2,1)S(1)} %collective-permute-done.8.refs_1_), channel_id=1, source_target_pairs={{0,4},{1,5},{2,6},{3,7},{4,0},{5,1},{6,2},{7,3},{8,12},{9,13},{10,... | collective-permute-start | bytes 688136 | tf_op jit(solution)/shard_map/ppermute | solution.py:234
  80.9 6.3 %collective-permute-start.10 = (bf16[896,128]{1,0:T(8,128)(2,1)S(1)}, bf16[896,128]{1,0:T(8,128)(2,1)S(1)}, u32[]{:S(2)}, u32[]{:S(2)}) collective-permute-start(bf16[896,128]{1,0:T(8,128)(2,1)S(1)} %collective-permute-done.8.refs_1_), channel_id=1, source_target_pairs={{0,8},{1,9},{2,10},{3,11},{4,20},{5,21},{6,22},{7,23},{8,0},{9,1},... | collective-permute-start | bytes 688136 | tf_op jit(solution)/shard_map/ppermute | solution.py:234
  83.3 6.5 %collective-permute-start.19 = (bf16[896,128]{1,0:T(8,128)(2,1)S(1)}, bf16[896,128]{1,0:T(8,128)(2,1)S(1)}, u32[]{:S(2)}, u32[]{:S(2)}) collective-permute-start(bf16[896,128]{1,0:T(8,128)(2,1)S(1)} %collective-permute-done.17.refs_9_), channel_id=1, source_target_pairs={{0,8},{1,9},{2,10},{3,11},{4,20},{5,21},{6,22},{7,23},{8,0},{9,1},... | collective-permute-start | bytes 688136 | tf_op jit(solution)/shard_map/ppermute | solution.py:234
  83.4 6.4 %collective-permute-start.21 = (bf16[896,128]{1,0:T(8,128)(2,1)S(1)}, bf16[896,128]{1,0:T(8,128)(2,1)S(1)}, u32[]{:S(2)}, u32[]{:S(2)}) collective-permute-start(bf16[896,128]{1,0:T(8,128)(2,1)S(1)} %collective-permute-done.17.refs_9_), channel_id=1, source_target_pairs={{0,4},{1,5},{2,6},{3,7},{4,0},{5,1},{6,2},{7,3},{8,12},{9,13},{10,... | collective-permute-start | bytes 688136 | tf_op jit(solution)/shard_map/ppermute | solution.py:234
  83.5 6.2 %collective-permute-start.22 = (bf16[896,128]{1,0:T(8,128)(2,1)S(1)}, bf16[896,128]{1,0:T(8,128)(2,1)S(1)}, u32[]{:S(2)}, u32[]{:S(2)}) collective-permute-start(bf16[896,128]{1,0:T(8,128)(2,1)S(1)} %collective-permute-done.18.refs_10_), channel_id=1, source_target_pairs={{0,4},{1,5},{2,6},{3,7},{4,0},{5,1},{6,2},{7,3},{8,12},{9,13},{10,... | collective-permute-start | bytes 688136 | tf_op jit(solution)/shard_map/ppermute | solution.py:234
  83.9 5.9 %collective-permute-start.30 = (bf16[896,128]{1,0:T(8,128)(2,1)S(1)}, bf16[896,128]{1,0:T(8,128)(2,1)S(1)}, u32[]{:S(2)}, u32[]{:S(2)}) collective-permute-start(bf16[896,128]{1,0:T(8,128)(2,1)S(1)} %collective-permute-done.26.refs_19_), channel_id=1, source_target_pairs={{0,4},{1,5},{2,6},{3,7},{4,0},{5,1},{6,2},{7,3},{8,12},{9,13},{10,... | collective-permute-start | bytes 688136 | tf_op jit(solution)/shard_map/ppermute | solution.py:234
  87.3 2.5 %collective-permute-start.14 = (bf16[896,128]{1,0:T(8,128)(2,1)S(1)}, bf16[896,128]{1,0:T(8,128)(2,1)S(1)}, u32[]{:S(2)}, u32[]{:S(2)}) collective-permute-start(bf16[896,128]{1,0:T(8,128)(2,1)S(1)} %collective-permute-done.10.refs_3_), channel_id=1, source_target_pairs={{0,4},{1,5},{2,6},{3,7},{4,0},{5,1},{6,2},{7,3},{8,12},{9,13},{10,... | collective-permute-start | bytes 688136 | tf_op jit(solution)/shard_map/ppermute | solution.py:234
  89.7 1.5 %collective-permute-start.23 = (bf16[896,128]{1,0:T(8,128)(2,1)S(1)}, bf16[896,128]{1,0:T(8,128)(2,1)S(1)}, u32[]{:S(2)}, u32[]{:S(2)}) collective-permute-start(bf16[896,128]{1,0:T(8,128)(2,1)S(1)} %collective-permute-done.19.refs_11_), channel_id=1, source_target_pairs={{0,4},{1,5},{2,6},{3,7},{4,0},{5,1},{6,2},{7,3},{8,12},{9,13},{10,... | collective-permute-start | bytes 688136 | tf_op jit(solution)/shard_map/ppermute | solution.py:234
  (8 other events, 184.8 us)

commit v2 on v1

v2 whole, which is shorter than its diff:
```python
import functools
import math

import jax
import jax.numpy as jnp
from jax import lax
from jax.experimental import pallas as pl
from jax.experimental.pallas import tpu as pltpu
from jax.sharding import PartitionSpec as P

ENC_HEADS = 14
ENCODER_HEAD_DIM = 64
ENCODER_WIDTH = 896
CROSS_HEADS = 16
CROSS_HEAD = 128
BLOCK_LEN = 64
NEIGHBOUR_LENGTH = 64
NEIGHBOUR_COUNT = 2
CROSS_WIDTH = CROSS_HEADS * CROSS_HEAD
KEYS = NEIGHBOUR_COUNT * NEIGHBOUR_LENGTH
LANES = 128
FLAG_ROWS = 16
EDGE = 16
PAIRS_AT_ONCE = 2

MASKED_SCORE = -1e30
AXES = ("groups", "cache", "span")
VMEM = pl.BlockSpec(memory_space=pltpu.VMEM)
SMEM = pl.BlockSpec(memory_space=pltpu.SMEM)
ANY = pl.BlockSpec(memory_space=pl.ANY)
NT = (((1,), (1,)), ((), ()))
TN = (((0,), (0,)), ((), ()))


def dot(a, b, dims=(((1,), (0,)), ((), ()))):
    return lax.dot_general(a, b, dims, preferred_element_type=jnp.float32)


def entry_id(ids_ref, request):
    return ids_ref[request % NEIGHBOUR_COUNT, request // NEIGHBOUR_COUNT]


def fetch_kernel(peers, capacity, cache_slots, requests, *refs):
    wanted = refs[: peers - 1]
    cache_ref = refs[peers - 1]
    outs = refs[peers : 2 * peers - 1]
    ids, ids_sem, sem = refs[2 * peers - 1 :]
    me = lax.axis_index("cache")
    for r in range(peers - 1):
        pltpu.make_async_copy(wanted[r], ids.at[r], ids_sem.at[r]).start()
    counts = []
    for r in range(peers - 1):
        pltpu.make_async_copy(wanted[r], ids.at[r], ids_sem.at[r]).wait()
        count = jnp.int32(0)
        for i in range(requests):
            slot = entry_id(ids.at[r], i) - me * cache_slots
            hit = (slot >= 0) & (slot < cache_slots) & (count < capacity)

            @pl.when(hit)
            def _(r=r, count=count, slot=slot):
                pltpu.make_async_copy(
                    cache_ref.at[slot], outs[r].at[count], sem.at[r, count]
                ).start()

            count = count + hit.astype(jnp.int32)
        counts.append(count)
    for r in range(peers - 1):
        for k in range(capacity):

            @pl.when(counts[r] > k)
            def _(r=r, k=k):
                pltpu.make_async_copy(cache_ref.at[0], outs[r].at[k], sem.at[r, k]).wait()


def usable_row(first, second):
    lane = lax.broadcasted_iota(jnp.int32, (1, KEYS), 1)
    limit = jnp.where(lane < NEIGHBOUR_LENGTH, first, second + NEIGHBOUR_LENGTH)
    return lane < limit


def encode_kernel(peers, capacity, cache_slots, blocks, *refs):
    ids_ref, lengths_ref, states_ref, weight_ref, cache_ref = refs[:5]
    arrived = refs[5 : 5 + peers - 1]
    out_ref, send_ref = refs[5 + peers - 1 : 7 + peers - 1]
    entries, queries, sem = refs[7 + peers - 1 :]
    me = lax.axis_index("cache")
    width = ENCODER_WIDTH
    requests = blocks * NEIGHBOUR_COUNT
    ids = [entry_id(ids_ref, i) for i in range(requests)]
    owners = [v // cache_slots for v in ids]
    for i in range(requests):
        rank = jnp.int32(0)
        for j in range(i):
            rank = rank + (owners[j] == owners[i]).astype(jnp.int32)
        rank = jnp.minimum(rank, capacity - 1)
        rel = owners[i] ^ me
        slot = ids[i] - owners[i] * cache_slots

        @pl.when(rel == 0)
        def _(i=i, slot=slot):
            pltpu.make_async_copy(cache_ref.at[slot], entries.at[i], sem.at[i]).start()

        for r in range(1, peers):

            @pl.when(rel == r)
            def _(i=i, r=r, rank=rank):
                pltpu.make_async_copy(arrived[r - 1].at[rank], entries.at[i], sem.at[i]).start()

    low = lax.broadcasted_iota(jnp.int32, (BLOCK_LEN, LANES), 1) < ENCODER_HEAD_DIM
    per_pair = LANES // ENCODER_HEAD_DIM
    scale = 1.0 / math.sqrt(ENCODER_HEAD_DIM)

    def both(rows):
        zero = jnp.zeros_like(rows)
        return jnp.concatenate([jnp.where(low, rows, zero), jnp.where(low, zero, rows)], axis=0)

    def project(b):
        first = b * NEIGHBOUR_COUNT
        for i in range(first, first + NEIGHBOUR_COUNT):
            pltpu.make_async_copy(cache_ref.at[0], entries.at[i], sem.at[i]).wait()
        rows = entries[first : first + NEIGHBOUR_COUNT].reshape(KEYS, width)
        queries[b * KEYS : (b + 1) * KEYS, :] = dot(rows, weight_ref[...]).astype(jnp.bfloat16)

    def scores_of(b, pairs):
        scores = []
        for p in pairs:
            cols = slice(p * LANES, (p + 1) * LANES)
            keys = both(states_ref[b * BLOCK_LEN : (b + 1) * BLOCK_LEN, cols])
            scores.append(dot(keys, queries[b * KEYS : (b + 1) * KEYS, cols], NT))
        return jnp.concatenate(scores, axis=0).reshape(-1, BLOCK_LEN, KEYS) * scale

    def finish(b, pairs, scores):
        weights = jnp.exp(scores - jnp.max(scores, axis=1, keepdims=True))
        weights = weights * (1.0 / jnp.sum(weights, axis=1, keepdims=True))
        weights = weights.reshape(-1, KEYS).astype(jnp.bfloat16)
        first = b * NEIGHBOUR_COUNT
        for n, p in enumerate(pairs):
            cols = slice(p * LANES, (p + 1) * LANES)
            values = slice(width + p * LANES, width + (p + 1) * LANES)
            values = both(states_ref[b * BLOCK_LEN : (b + 1) * BLOCK_LEN, values])
            height = per_pair * BLOCK_LEN
            attended = dot(weights[n * height : (n + 1) * height], values, TN)
            owned = entries[first : first + NEIGHBOUR_COUNT, :, cols].reshape(KEYS, LANES)
            encoded = (owned.astype(jnp.float32) + attended).astype(jnp.bfloat16)
            out_ref[b * KEYS : (b + 1) * KEYS, cols] = encoded
            if b == blocks - 1:
                send_ref[:KEYS, cols] = encoded

    for b in range(blocks):
        project(b)
    pairs = width // LANES
    groups = [range(p, min(p + PAIRS_AT_ONCE, pairs)) for p in range(0, pairs, PAIRS_AT_ONCE)]
    steps = [(b, g) for b in reversed(range(blocks)) for g in groups]
    scores = scores_of(*steps[0])
    for n, step in enumerate(steps):
        after = scores_of(*steps[n + 1]) if n + 1 < len(steps) else None
        finish(*step, scores)
        scores = after
    flags = usable_row(lengths_ref[0, blocks - 1], lengths_ref[1, blocks - 1])
    flags = jnp.broadcast_to(flags.astype(jnp.float32), (FLAG_ROWS, LANES))
    send_ref[KEYS:, :] = jnp.zeros((FLAG_ROWS, width), jnp.bfloat16)
    send_ref[KEYS:, :LANES] = flags.astype(jnp.bfloat16)


def cross_heads(blocks, lengths_ref, encoded_ref, prior_ref, queries_ref, out_ref, items, swap):
    span = lax.axis_index("span")
    scale = 1.0 / math.sqrt(CROSS_HEAD)
    last_row = lax.broadcasted_iota(jnp.int32, (EDGE, CROSS_HEAD), 0) == EDGE - 1
    flags = [prior_ref[KEYS : KEYS + FLAG_ROWS, :LANES].astype(jnp.float32)[:1] > 0.5]
    for b in range(blocks):
        flags.append(usable_row(lengths_ref[0, b], lengths_ref[1, b]))
    tokens = blocks * BLOCK_LEN
    ranges = [
        (max(0, (u + 1) * BLOCK_LEN - EDGE), min(tokens, (u + 2) * BLOCK_LEN))
        for u in range(-1, blocks)
    ]

    def project(load):
        weights = jnp.concatenate(load(), axis=1)
        before = dot(prior_ref[:KEYS, :], weights).astype(jnp.bfloat16)
        own = dot(encoded_ref[...], weights).astype(jnp.bfloat16)
        return [before] + [own[b * KEYS : (b + 1) * KEYS] for b in range(blocks)]

    states = project(items[0][2])
    for n, (columns, target, _) in enumerate(items):
        scores, values = [], []
        for (start, stop), state, flag in zip(ranges, states, flags):
            left, right = state[:, :CROSS_HEAD], state[:, CROSS_HEAD:]
            if swap is not None:
                left, right = jnp.where(swap, right, left), jnp.where(swap, left, right)
            score = dot(queries_ref[start:stop, columns], left, NT) * scale
            scores.append(jnp.where(flag, score, MASKED_SCORE))
            values.append(right)
        scores = jnp.concatenate(scores, axis=0)
        if n + 1 < len(items):
            states = project(items[n + 1][2])
        weights = jnp.exp(scores - jnp.max(scores, axis=1, keepdims=True))
        weights = weights * (1.0 / jnp.sum(weights, axis=1, keepdims=True))
        weights = weights.astype(jnp.bfloat16)
        at, tail = 0, None
        for u, (start, stop) in enumerate(ranges):
            part = weights[at : at + stop - start]
            result = dot(part, values[u]).astype(jnp.bfloat16)
            at += stop - start
            if u == 0:
                result = jnp.where(span > 0, result, jnp.zeros_like(result))
            else:
                out_ref[start : start + EDGE, target] = jnp.where(last_row, result[:EDGE], tail)
                result = result[EDGE:]
                start += EDGE
            if u < blocks:
                out_ref[start : stop - EDGE, target] = result[: stop - EDGE - start]
                tail = result[stop - EDGE - start :]


def head_columns(head):
    if isinstance(head, int):
        return slice(head * CROSS_HEAD, (head + 1) * CROSS_HEAD)
    return pl.ds(pl.multiple_of(head * CROSS_HEAD, CROSS_HEAD), CROSS_HEAD)


def whole_kernel(blocks, lengths_ref, encoded_ref, prior_ref, queries_ref, weight_ref, out_ref):
    def item(head):
        load = lambda: [
            weight_ref[:, head_columns(head)],
            weight_ref[:, head_columns(CROSS_HEADS + head)],
        ]
        return head_columns(head), head_columns(head), load

    items = [item(head) for head in range(CROSS_HEADS)]
    cross_heads(blocks, lengths_ref, encoded_ref, prior_ref, queries_ref, out_ref, items, None)


def place_of():
    return lax.axis_index("groups") * 4 + lax.axis_index("cache")


def head_of(low, place):
    return ((low ^ lax.axis_index("span")) & 1) * 8 + place


FAR_ORDER = (0, 4, 2, 6, 1, 5, 3, 7)
NEAR_ORDER = (0, 2, 4, 6, 1, 3, 5, 7)


def far_kernel(blocks, lengths_ref, encoded_ref, prior_ref, queries_ref, *refs):
    first = refs[:4]
    third = refs[4:12]
    out_ref = refs[12]

    def item(k, offset):
        place, pair = 2 * (offset % 2) + offset // 4, offset // 2 % 2
        load = lambda: [first[place][pair], third[k][...]]
        columns = head_columns(head_of(1, offset ^ place_of()))
        return columns, head_columns(k), load

    items = [item(k, offset) for k, offset in enumerate(FAR_ORDER)]
    swap = lax.axis_index("span") >= 2
    cross_heads(blocks, lengths_ref, encoded_ref, prior_ref, queries_ref, out_ref, items, swap)


def near_kernel(
    blocks, lengths_ref, encoded_ref, prior_ref, queries_ref, weight_ref, half_ref, *refs
):
    second = refs[:8]
    out_ref = refs[8]
    for k, offset in enumerate(FAR_ORDER):
        columns = head_columns(head_of(1, offset ^ place_of()))
        out_ref[:, columns] = half_ref[:, head_columns(k)]

    def item(k, offset):
        column = offset ^ place_of()
        load = lambda: [weight_ref[:, head_columns(column)], second[k][...]]
        columns = head_columns(head_of(0, column))
        return columns, columns, load

    items = [item(k, offset) for k, offset in enumerate(NEAR_ORDER)]
    swap = lax.axis_index("span") >= 2
    cross_heads(blocks, lengths_ref, encoded_ref, prior_ref, queries_ref, out_ref, items, swap)


def permute(value, move):
    sizes = [lax.axis_size(axis) for axis in AXES]
    flat = lambda g, c, s: (g * sizes[1] + c) * sizes[2] + s
    pairs = []
    for g in range(sizes[0]):
        for c in range(sizes[1]):
            for s in range(sizes[2]):
                pairs.append((flat(g, c, s), flat(*move(g, c, s))))
    return lax.ppermute(value, AXES, pairs)


def over_x(value):
    return permute(value, lambda g, c, s: (g ^ 1, c, s))


def over_y(value):
    return permute(value, lambda g, c, s: (g, c ^ 2, s))


def over_core(value):
    return permute(value, lambda g, c, s: (g, c ^ 1, s))


def gather_pieces(cross_weight):
    columns = [place * CROSS_HEAD for place in (place_of(), place_of() ^ 2)]
    own, other = [
        lax.dynamic_slice_in_dim(cross_weight, c, CROSS_HEAD, axis=1) for c in columns
    ]
    first = [permute(jnp.stack([own, other]), lambda g, c, s: (g, c, s ^ 1))]
    third = [permute(own, lambda g, c, s: (g, c, s ^ 3))]
    second = [permute(own, lambda g, c, s: (g, c, s ^ 2))]
    first += [over_x(v) for v in first]
    first += [over_core(v) for v in first]
    third += [over_x(v) for v in third]
    third += [over_y(v) for v in third]
    third += [over_core(v) for v in third]
    second += [over_y(v) for v in second]
    second += [over_x(v) for v in second]
    second += [over_core(v) for v in second]
    return first, third, second


def per_device(
    block_states,
    cross_queries,
    neighbour_cache,
    neighbour_owner,
    neighbour_slot,
    neighbour_lengths,
    encoder_query,
    cross_weight,
):
    peers = lax.axis_size("cache")
    spans = lax.axis_size("span")
    blocks = neighbour_owner.shape[0]
    requests = blocks * NEIGHBOUR_COUNT
    capacity = max(2, (requests + peers - 1) // peers)
    cache_slots = neighbour_cache.shape[0]
    swap = lambda v, r: lax.ppermute(v, "cache", [(i, i ^ r) for i in range(peers)])
    pieced = lax.axis_size("groups") == 2 and peers == 4 and spans == 4

    ids = neighbour_owner.T * cache_slots + neighbour_slot.T
    lengths = neighbour_lengths.T
    wanted = [swap(ids, r) for r in range(1, peers)]
    if pieced:
        first, third, second = gather_pieces(cross_weight)
    else:
        weights = lax.all_gather(cross_weight, "span", axis=1, tiled=True)
    entry = jax.ShapeDtypeStruct((capacity, NEIGHBOUR_LENGTH, ENCODER_WIDTH), jnp.bfloat16)
    fetched = pl.pallas_call(
        functools.partial(fetch_kernel, peers, capacity, cache_slots, requests),
        out_shape=[entry] * (peers - 1),
        in_specs=[ANY] * peers,
        out_specs=[VMEM] * (peers - 1),
        scratch_shapes=[
            pltpu.SMEM((peers - 1, NEIGHBOUR_COUNT, blocks), jnp.int32),
            pltpu.SemaphoreType.DMA((peers - 1,)),
            pltpu.SemaphoreType.DMA((peers - 1, capacity)),
        ],
        compiler_params=pltpu.CompilerParams(vmem_limit_bytes=16 * 2**20),
        name="fetch",
    )(*wanted, neighbour_cache)
    arrived = [swap(v, r) for r, v in enumerate(fetched, 1)]
    encoded, outgoing = pl.pallas_call(
        functools.partial(encode_kernel, peers, capacity, cache_slots, blocks),
        out_shape=[
            jax.ShapeDtypeStruct((blocks * KEYS, ENCODER_WIDTH), jnp.bfloat16),
            jax.ShapeDtypeStruct((KEYS + FLAG_ROWS, ENCODER_WIDTH), jnp.bfloat16),
        ],
        in_specs=[SMEM] * 2 + [VMEM] * 2 + [ANY] * peers,
        out_specs=[VMEM] * 2,
        scratch_shapes=[
            pltpu.VMEM((requests, NEIGHBOUR_LENGTH, ENCODER_WIDTH), jnp.bfloat16),
            pltpu.VMEM((blocks * KEYS, ENCODER_WIDTH), jnp.bfloat16),
            pltpu.SemaphoreType.DMA((requests,)),
        ],
        compiler_params=pltpu.CompilerParams(vmem_limit_bytes=16 * 2**20),
        cost_estimate=pl.CostEstimate(
            flops=2 * blocks * KEYS * ENCODER_WIDTH * (ENCODER_WIDTH + 4 * LANES),
            bytes_accessed=8 * 2**20,
            transcendentals=blocks * KEYS * ENC_HEADS * BLOCK_LEN,
        ),
        name="encode",
    )(ids, lengths, block_states, encoder_query, neighbour_cache, *arrived)
    prior = lax.ppermute(outgoing, "span", [(i, i + 1) for i in range(spans - 1)])

    def cross(kernel, heads, *operands):
        return pl.pallas_call(
            functools.partial(kernel, blocks),
            out_shape=jax.ShapeDtypeStruct(
                (blocks * BLOCK_LEN, heads * CROSS_HEAD), jnp.bfloat16
            ),
            in_specs=[SMEM] + [VMEM] * (3 + len(operands)),
            out_specs=VMEM,
            compiler_params=pltpu.CompilerParams(vmem_limit_bytes=32 * 2**20),
            cost_estimate=pl.CostEstimate(
                flops=4 * (blocks + 1) * KEYS * (ENCODER_WIDTH + 2 * LANES) * heads * CROSS_HEAD,
                bytes_accessed=8 * 2**20,
                transcendentals=(blocks + 1) * KEYS * BLOCK_LEN * heads,
            ),
            name="cross",
        )(lengths, encoded, prior, cross_queries, *operands)

    if not pieced:
        return cross(whole_kernel, CROSS_HEADS, weights)
    half = cross(far_kernel, CROSS_HEADS // 2, *first, *third)
    return cross(near_kernel, CROSS_HEADS, cross_weight, half, *second)


def solution(mesh):
    placed = (
        P(("groups", "cache", "span"), None),
        P(("groups", "cache", "span"), None),
        P(("groups", "cache"), None, None),
        P(("groups", "cache", "span"), None),
        P(("groups", "cache", "span"), None),
        P(("groups", "cache", "span"), None),
        P(),
        P(None, "span"),
    )
    return jax.shard_map(
        per_device,
        mesh=mesh,
        in_specs=placed,
        out_specs=P(("groups", "cache", "span"), None),
        check_vma=False,
    )
```

time: 123 us -> 76.1 us (0.62)
  Pallas kernels: 64.5 us -> 23.9 us
  local copies, waits for them, and re-layouts: 5.98 us -> 2.45 us
  other arithmetic: 1.78 us -> 0.05 us
    pallas_call x1, Pallas kernels: 22.8 us -> 1.78 us  [per_device(): pl.pallas_call(functools.partial(fetch_kernel, peers, capacity, cache_slo...]
    pallas_call x2 -> x3, Pallas kernels: 41.7 us -> 22.2 us  [the longest x2 16.1 us: cross(): pl.pallas_call(functools.partial(kernel, blocks), out_shape=jax.ShapeDtyp...]
    ppermute x6, waiting for transfers between devices: 10.3 us -> 2.59 us  [per_device(): lax.ppermute(v, 'cache', [(i, i ^ r) for i in range(peers)])]
    ppermute x24 -> x20, waiting for transfers between devices: 16.6 us -> 23.4 us  [permute(): return lax.ppermute(value, AXES, pairs)]
    unnamed x21 -> x16, local copies, waits for them, and re-layouts: 4.2 us -> 1.21 us
    ppermute x24 -> x20, starting transfers between devices: 17.5 us -> 15.2 us  [permute(): return lax.ppermute(value, AXES, pairs)]
    select_n x1 -> x0, other arithmetic: 1.7 us -> none  [gather_pieces(): onward = jnp.where(inner, third, own)]
    ppermute x1, waiting for transfers between devices: 0.01 us -> 1.44 us  [per_device(): lax.ppermute(outgoing, 'span', [(i, i + 1) for i in range(spans - 1)])]
  transfers between devices with their start and end apart: 31 -> 27, of which waited for: 11 -> 9; matrix products, arithmetic and copies ran while one was open for 3% -> 0% of each run, Pallas kernels for 27% -> 20%
where the time goes in v2:
time: 76.1 us; the launch traced here: 75.9 us
  waiting for transfers between devices  27.4 us (36%)
  Pallas kernels  23.9 us (31%)
  starting transfers between devices  21.9 us (29%)
  local copies, waits for them, and re-layouts  2.45 us (3%)
    ppermute x20, waiting for transfers between devices, permute(): return lax.ppermute(value, AXES, pairs)  23.4 us
    pallas_call x2, Pallas kernels, cross(): pl.pallas_call(functools.partial(kernel, blocks), out_shape=jax.ShapeDtyp...  16.1 us
    ppermute x20, starting transfers between devices, permute(): return lax.ppermute(value, AXES, pairs)  15.2 us
    pallas_call x1, Pallas kernels, per_device(): pl.pallas_call(functools.partial(encode_kernel, peers, capacity, cache_sl...  6.06 us
    ppermute x6, starting transfers between devices, per_device(): lax.ppermute(v, 'cache', [(i, i ^ r) for i in range(peers)])  4.12 us
    ppermute x1, starting transfers between devices, per_device(): lax.ppermute(outgoing, 'span', [(i, i + 1) for i in range(spans - 1)])  2.6 us
    ppermute x6, waiting for transfers between devices, per_device(): lax.ppermute(v, 'cache', [(i, i ^ r) for i in range(peers)])  2.59 us
    pallas_call x1, Pallas kernels, per_device(): pl.pallas_call(functools.partial(fetch_kernel, peers, capacity, cache_slo...  1.78 us
  transfers between devices with their start and end apart: 27, of which 9 were waited for; matrix products, arithmetic and copies ran while one was open for 0% of the time, Pallas kernels for 20%

profile of v2, /device:TPU:0, one launch (start us, length us, event | category | flops | bytes accessed | tf_op | source)
XLA Modules:
  0.0 75.9 jit_solution(15329673019027356619)
XLA Ops:
  0.0 1.2 %constant_dynamic-slice_fusion = (bf16[896,128]{1,0:T(8,128)(2,1)S(1)}, bf16[1,896,128]{2,1,0:T(8,128)(2,1)S(1)}) fusion(bf16[896,1024]{1,0:T(8,128)(2,1)} %weight_ref.1, s32[]{:T(128)S(6)} %select_n.6, s32[]{:T(128)S(6)} %select_n.7), kind=kLoop, calls=%fused_computation.3 | loop fusion | bytes 917512 | tf_op jit(solution)/shard_map/dynamic_slice | solution.py:308
  1.3 3.1 %collective-permute-start.7 = (bf16[2,896,128]{2,1,0:T(8,128)(2,1)S(1)}, bf16[2,896,128]{2,1,0:T(8,128)(2,1)S(1)}, u32[]{:S(2)}, u32[]{:S(2)}) collective-permute-start(bf16[2,896,128]{2,1,0:T(8,128)(2,1)S(1)} %pad_maximum_fusion), channel_id=1, source_target_pairs={{0,1},{1,0},{2,3},{3,2},{4,5},{5,4},{6,7},{7,6},{8,9},{9,8},{10,11... | collective-permute-start | bytes 1376264 | tf_op jit(solution)/shard_map/ppermute | solution.py:290
  4.4 2.5 %collective-permute-start.11 = (bf16[896,128]{1,0:T(8,128)(2,1)S(1)}, bf16[896,128]{1,0:T(8,128)(2,1)S(1)}, u32[]{:S(2)}, u32[]{:S(2)}) collective-permute-start(bf16[896,128]{1,0:T(8,128)(2,1)S(1)} %get-tuple-element.15), channel_id=1, source_target_pairs={{0,3},{1,2},{2,1},{3,0},{4,7},{5,6},{6,5},{7,4},{8,11},{9,10},{10,... | collective-permute-start | bytes 688136 | tf_op jit(solution)/shard_map/ppermute | solution.py:290
  7.1 1.6 %collective-permute-start.1 = (s32[2,4]{1,0:T(2,128)S(1)}, s32[2,4]{1,0:T(2,128)S(1)}, u32[]{:S(2)}, u32[]{:S(2)}) collective-permute-start(s32[2,4]{1,0:T(2,128)S(1)} %add_bitcast_fusion.refs_0_), channel_id=1, source_target_pairs={{0,8},{4,12},{8,0},{12,4},{1,9},{5,13},{9,1},{13,5},{2,10},{6,14},... | collective-permute-start | bytes 104 | tf_op jit(solution)/shard_map/ppermute | solution.py:340
  8.7 0.9 %collective-permute-start.2 = (s32[2,4]{1,0:T(2,128)S(1)}, s32[2,4]{1,0:T(2,128)S(1)}, u32[]{:S(2)}, u32[]{:S(2)}) collective-permute-start(s32[2,4]{1,0:T(2,128)S(1)} %add_bitcast_fusion.refs_0_), channel_id=1, source_target_pairs={{0,12},{4,8},{8,4},{12,0},{1,13},{5,9},{9,5},{13,1},{2,14},{6,10},... | collective-permute-start | bytes 104 | tf_op jit(solution)/shard_map/ppermute | solution.py:340
  9.6 1.2 %collective-permute-done.1.refs_1_ = s32[2,4]{1,0:T(2,128)S(1)} collective-permute-done((s32[2,4]{1,0:T(2,128)S(1)}, s32[2,4]{1,0:T(2,128)S(1)}, u32[]{:S(2)}, u32[]{:S(2)}) %collective-permute-start.1) | collective-permute-done | bytes 64 | tf_op jit(solution)/shard_map/ppermute | solution.py:340
  10.7 0.9 %collective-permute-done.2.refs_2_ = s32[2,4]{1,0:T(2,128)S(1)} collective-permute-done((s32[2,4]{1,0:T(2,128)S(1)}, s32[2,4]{1,0:T(2,128)S(1)}, u32[]{:S(2)}, u32[]{:S(2)}) %collective-permute-start.2) | collective-permute-done | bytes 64 | tf_op jit(solution)/shard_map/ppermute | solution.py:340
  11.7 1.8 %fetch.1 = (bf16[2,64,896]{2,1,0:T(8,128)(2,1)S(1)}, bf16[2,64,896]{2,1,0:T(8,128)(2,1)S(1)}, bf16[2,64,896]{2,1,0:T(8,128)(2,1)S(1)}) custom-call(s32[2,4]{1,0:T(2,128)S(1)} %collective-permute-done.refs_0_, s32[2,4]{1,0:T(2,128)S(1)} %collective-permute-done.1.refs_1_, s32[2,4]{1,0:T(2,128)S(1)} %collective-permute-done.2.refs_2_, ...), custom_call_target="tpu_custom_call" | custom-call | tf_op jit(solution)/shard_map/fetch/pallas_call | solution.py:351
  13.5 0.5 collective-permute-start.3
  14.0 1.1 %collective-permute-start.4 = (bf16[2,64,896]{2,1,0:T(8,128)(2,1)S(1)}, bf16[2,64,896]{2,1,0:T(8,128)(2,1)S(1)}, u32[]{:S(2)}, u32[]{:S(2)}) collective-permute-start(bf16[2,64,896]{2,1,0:T(8,128)(2,1)S(1)} %get-tuple-element.11), channel_id=1, source_target_pairs={{0,8},{4,12},{8,0},{12,4},{1,9},{5,13},{9,1},{13,5},{2,10},{6,14},... | collective-permute-start | bytes 688136 | tf_op jit(solution)/shard_map/ppermute | solution.py:340
  15.1 8.2 %collective-permute-done.11.refs_4_ = bf16[896,128]{1,0:T(8,128)(2,1)S(1)} collective-permute-done((bf16[896,128]{1,0:T(8,128)(2,1)S(1)}, bf16[896,128]{1,0:T(8,128)(2,1)S(1)}, u32[]{:S(2)}, u32[]{:S(2)}) %collective-permute-start.11) | collective-permute-done | bytes 229408 | tf_op jit(solution)/shard_map/ppermute | solution.py:290
  23.3 3.8 %collective-permute-done.19.refs_0_ = bf16[896,128]{1,0:T(8,128)(2,1)S(1)} collective-permute-done((bf16[896,128]{1,0:T(8,128)(2,1)S(1)}, bf16[896,128]{1,0:T(8,128)(2,1)S(1)}, u32[]{:S(2)}, u32[]{:S(2)}) %collective-permute-start.19) | collective-permute-done | bytes 229408 | tf_op jit(solution)/shard_map/ppermute | solution.py:290
  27.1 1.5 %collective-permute-start.12 = (bf16[896,128]{1,0:T(8,128)(2,1)S(1)}, bf16[896,128]{1,0:T(8,128)(2,1)S(1)}, u32[]{:S(2)}, u32[]{:S(2)}) collective-permute-start(bf16[896,128]{1,0:T(8,128)(2,1)S(1)} %collective-permute-done.11.refs_4_), channel_id=1, source_target_pairs={{0,16},{1,17},{2,18},{3,19},{4,20},{5,21},{6,22},{7,23},{8,24},{9,... | collective-permute-start | bytes 688136 | tf_op jit(solution)/shard_map/ppermute | solution.py:290
  28.6 0.5 collective-permute-start.8
  29.2 1.5 %collective-permute-start.13 = (bf16[896,128]{1,0:T(8,128)(2,1)S(1)}, bf16[896,128]{1,0:T(8,128)(2,1)S(1)}, u32[]{:S(2)}, u32[]{:S(2)}) collective-permute-start(bf16[896,128]{1,0:T(8,128)(2,1)S(1)} %collective-permute-done.11.refs_4_), channel_id=1, source_target_pairs={{0,8},{1,9},{2,10},{3,11},{4,12},{5,13},{6,14},{7,15},{8,0},{9,1},... | collective-permute-start | bytes 688136 | tf_op jit(solution)/shard_map/ppermute | solution.py:290
  30.7 0.4 collective-permute-done.5.refs_7_
  31.1 0.6 collective-permute-start.20
  31.8 3.9 %collective-permute-done.12.refs_5_ = bf16[896,128]{1,0:T(8,128)(2,1)S(1)} collective-permute-done((bf16[896,128]{1,0:T(8,128)(2,1)S(1)}, bf16[896,128]{1,0:T(8,128)(2,1)S(1)}, u32[]{:S(2)}, u32[]{:S(2)}) %collective-permute-start.12) | collective-permute-done | bytes 229408 | tf_op jit(solution)/shard_map/ppermute | solution.py:290
  35.7 1.5 %collective-permute-start.21 = (bf16[896,128]{1,0:T(8,128)(2,1)S(1)}, bf16[896,128]{1,0:T(8,128)(2,1)S(1)}, u32[]{:S(2)}, u32[]{:S(2)}) collective-permute-start(bf16[896,128]{1,0:T(8,128)(2,1)S(1)} %collective-permute-done.19.refs_0_), channel_id=1, source_target_pairs={{0,16},{1,17},{2,18},{3,19},{4,20},{5,21},{6,22},{7,23},{8,24},{9,... | collective-permute-start | bytes 688136 | tf_op jit(solution)/shard_map/ppermute | solution.py:290
  37.2 1.2 %copy-done.4 = bf16[256,1792]{1,0:T(8,128)(2,1)S(1)} copy-done((bf16[256,1792]{1,0:T(8,128)(2,1)S(1)}, bf16[256,1792]{1,0:T(8,128)(2,1)}, u32[]{:S(2)}) %copy-start.4) | copy-done | bytes 917528
  38.4 6.1 %encode.1 = (bf16[512,896]{1,0:T(8,128)(2,1)S(1)}, bf16[144,896]{1,0:T(8,128)(2,1)S(1)}) custom-call(s32[2,4]{1,0:T(2,128)S(1)} %add_bitcast_fusion.refs_0_, s32[2,4]{1,0:T(2,128)S(1)} %bitcast.6, bf16[256,1792]{1,0:T(8,128)(2,1)S(1)} %copy-done.4, bf16[896,896]{1,0:T(8,128)(2,1)S(1)} %copy-done.2, bf16[8,64,896]{2,1,0:T(8,128)(2,1)S(1)} %copy-done, ...), custom_call_target="tpu_custom_call" | custom-call | flops 1291845632 | bytes 8388608 | tf_op jit(solution)/shard_map/encode/pallas_call | solution.py:365
  44.4 2.6 %collective-permute-start.6 = (bf16[144,896]{1,0:T(8,128)(2,1)S(1)}, bf16[144,896]{1,0:T(8,128)(2,1)S(1)}, u32[]{:S(2)}, u32[]{:S(2)}) collective-permute-start(bf16[144,896]{1,0:T(8,128)(2,1)S(1)} %get-tuple-element.14), channel_id=1, source_target_pairs={{0,1},{1,2},{2,3},{4,5},{5,6},{6,7},{8,9},{9,10},{10,11},{12,13},{... | collective-permute-start | bytes 774152 | tf_op jit(solution)/shard_map/ppermute | solution.py:386
  47.0 1.6 %collective-permute-start.14 = (bf16[896,128]{1,0:T(8,128)(2,1)S(1)}, bf16[896,128]{1,0:T(8,128)(2,1)S(1)}, u32[]{:S(2)}, u32[]{:S(2)}) collective-permute-start(bf16[896,128]{1,0:T(8,128)(2,1)S(1)} %collective-permute-done.12.refs_5_), channel_id=1, source_target_pairs={{0,8},{1,9},{2,10},{3,11},{4,12},{5,13},{6,14},{7,15},{8,0},{9,1},... | collective-permute-start | bytes 688136 | tf_op jit(solution)/shard_map/ppermute | solution.py:290
  48.7 0.5 collective-permute-start.16
  49.2 1.4 %collective-permute-done.6.prior_ref = bf16[144,896]{1,0:T(8,128)(2,1)S(1)} collective-permute-done((bf16[144,896]{1,0:T(8,128)(2,1)S(1)}, bf16[144,896]{1,0:T(8,128)(2,1)S(1)}, u32[]{:S(2)}, u32[]{:S(2)}) %collective-permute-start.6) | collective-permute-done | bytes 258080 | tf_op jit(solution)/shard_map/ppermute | solution.py:386
  50.7 2.5 %collective-permute-done.14.refs_7_ = bf16[896,128]{1,0:T(8,128)(2,1)S(1)} collective-permute-done((bf16[896,128]{1,0:T(8,128)(2,1)S(1)}, bf16[896,128]{1,0:T(8,128)(2,1)S(1)}, u32[]{:S(2)}, u32[]{:S(2)}) %collective-permute-start.14) | collective-permute-done | bytes 229408 | tf_op jit(solution)/shard_map/ppermute | solution.py:290
  53.1 0.5 collective-permute-start.22
  53.7 0.5 collective-permute-start.23
  54.2 5.0 %collective-permute-done.22.refs_3_ = bf16[896,128]{1,0:T(8,128)(2,1)S(1)} collective-permute-done((bf16[896,128]{1,0:T(8,128)(2,1)S(1)}, bf16[896,128]{1,0:T(8,128)(2,1)S(1)}, u32[]{:S(2)}, u32[]{:S(2)}) %collective-permute-start.22) | collective-permute-done | bytes 229408 | tf_op jit(solution)/shard_map/ppermute | solution.py:290
  59.2 0.5 collective-permute-start.25
  59.8 7.5 %cross.2.half_ref = bf16[256,1024]{1,0:T(8,128)(2,1)S(1)} custom-call(s32[2,4]{1,0:T(2,128)S(1)} %bitcast.7, bf16[512,896]{1,0:T(8,128)(2,1)S(1)} %get-tuple-element.13.encoded_ref, bf16[144,896]{1,0:T(8,128)(2,1)S(1)} %collective-permute-done.6.prior_ref, bf16[256,2048]{1,0:T(8,128)(2,1)S(1)} %copy-done.3, ...), custom_call_target="tpu_custom_call" | custom-call | flops 3019898880 | bytes 8388608 | tf_op jit(solution)/shard_map/cross/pallas_call | solution.py:389
  67.3 8.6 %cross.3 = bf16[256,2048]{1,0:T(8,128)(2,1)} custom-call(s32[2,4]{1,0:T(2,128)S(1)} %bitcast.8, bf16[512,896]{1,0:T(8,128)(2,1)S(1)} %get-tuple-element.13.encoded_ref, bf16[144,896]{1,0:T(8,128)(2,1)S(1)} %collective-permute-done.6.prior_ref, bf16[256,2048]{1,0:T(8,128)(2,1)S(1)} %copy-done.3, bf16[896,1024]{1,0:T(8,128)(2,1)S(1)} %copy-done.1, ...), custom_call_target="tpu_custom_call" | custom-call | flops 6039797760 | bytes 8388608 | tf_op jit(solution)/shard_map/cross/pallas_call | solution.py:389
  (45 shorter events, 0.5 us)
Async XLA Ops:
  0.0 11.7 %copy-start = (bf16[8,64,896]{2,1,0:T(8,128)(2,1)S(1)}, bf16[8,64,896]{2,1,0:T(8,128)(2,1)}, u32[]{:S(2)}) copy-start(bf16[8,64,896]{2,1,0:T(8,128)(2,1)} %refs_4_.1) | copy-start | bytes 2752516
  0.0 37.2 %copy-start.5 = (s32[4,2]{0,1:T(2,128)S(1)}, s32[4,2]{0,1:T(2,128)}, u32[]{:S(2)}) copy-start(s32[4,2]{0,1:T(2,128)} %param.13) | copy-start | bytes 100
  0.0 37.2 %copy-start.2 = (bf16[896,896]{1,0:T(8,128)(2,1)S(1)}, bf16[896,896]{1,0:T(8,128)(2,1)}, u32[]{:S(2)}) copy-start(bf16[896,896]{1,0:T(8,128)(2,1)} %refs_3_.3) | copy-start | bytes 4816900
  1.3 27.3 %collective-permute-start.7 = (bf16[2,896,128]{2,1,0:T(8,128)(2,1)S(1)}, bf16[2,896,128]{2,1,0:T(8,128)(2,1)S(1)}, u32[]{:S(2)}, u32[]{:S(2)}) collective-permute-start(bf16[2,896,128]{2,1,0:T(8,128)(2,1)S(1)} %pad_maximum_fusion), channel_id=1, source_target_pairs={{0,1},{1,0},{2,3},{3,2},{4,5},{5,4},{6,7},{7,6},{8,9},{9,8},{10,11... | collective-permute-start | bytes 1376264 | tf_op jit(solution)/shard_map/ppermute | solution.py:290
  4.4 18.9 %collective-permute-start.11 = (bf16[896,128]{1,0:T(8,128)(2,1)S(1)}, bf16[896,128]{1,0:T(8,128)(2,1)S(1)}, u32[]{:S(2)}, u32[]{:S(2)}) collective-permute-start(bf16[896,128]{1,0:T(8,128)(2,1)S(1)} %get-tuple-element.15), channel_id=1, source_target_pairs={{0,3},{1,2},{2,1},{3,0},{4,7},{5,6},{6,5},{7,4},{8,11},{9,10},{10,... | collective-permute-start | bytes 688136 | tf_op jit(solution)/shard_map/ppermute | solution.py:290
  6.9 20.2 %collective-permute-start.19 = (bf16[896,128]{1,0:T(8,128)(2,1)S(1)}, bf16[896,128]{1,0:T(8,128)(2,1)S(1)}, u32[]{:S(2)}, u32[]{:S(2)}) collective-permute-start(bf16[896,128]{1,0:T(8,128)(2,1)S(1)} %get-tuple-element.15), channel_id=1, source_target_pairs={{0,2},{1,3},{2,0},{3,1},{4,6},{5,7},{6,4},{7,5},{8,10},{9,11},{10,... | collective-permute-start | bytes 688136 | tf_op jit(solution)/shard_map/ppermute | solution.py:290
  7.0 1.7 %collective-permute-start = (s32[2,4]{1,0:T(2,128)S(1)}, s32[2,4]{1,0:T(2,128)S(1)}, u32[]{:S(2)}, u32[]{:S(2)}) collective-permute-start(s32[2,4]{1,0:T(2,128)S(1)} %add_bitcast_fusion.refs_0_), channel_id=1, source_target_pairs={{0,4},{4,0},{8,12},{12,8},{1,5},{5,1},{9,13},{13,9},{2,6},{6,2},{1... | collective-permute-start | bytes 104 | tf_op jit(solution)/shard_map/ppermute | solution.py:340
  7.1 3.6 %collective-permute-start.1 = (s32[2,4]{1,0:T(2,128)S(1)}, s32[2,4]{1,0:T(2,128)S(1)}, u32[]{:S(2)}, u32[]{:S(2)}) collective-permute-start(s32[2,4]{1,0:T(2,128)S(1)} %add_bitcast_fusion.refs_0_), channel_id=1, source_target_pairs={{0,8},{4,12},{8,0},{12,4},{1,9},{5,13},{9,1},{13,5},{2,10},{6,14},... | collective-permute-start | bytes 104 | tf_op jit(solution)/shard_map/ppermute | solution.py:340
  8.7 3.0 %collective-permute-start.2 = (s32[2,4]{1,0:T(2,128)S(1)}, s32[2,4]{1,0:T(2,128)S(1)}, u32[]{:S(2)}, u32[]{:S(2)}) collective-permute-start(s32[2,4]{1,0:T(2,128)S(1)} %add_bitcast_fusion.refs_0_), channel_id=1, source_target_pairs={{0,12},{4,8},{8,4},{12,0},{1,13},{5,9},{9,5},{13,1},{2,14},{6,10},... | collective-permute-start | bytes 104 | tf_op jit(solution)/shard_map/ppermute | solution.py:340
  13.5 15.7 %collective-permute-start.3 = (bf16[2,64,896]{2,1,0:T(8,128)(2,1)S(1)}, bf16[2,64,896]{2,1,0:T(8,128)(2,1)S(1)}, u32[]{:S(2)}, u32[]{:S(2)}) collective-permute-start(bf16[2,64,896]{2,1,0:T(8,128)(2,1)S(1)} %get-tuple-element.10), channel_id=1, source_target_pairs={{0,4},{4,0},{8,12},{12,8},{1,5},{5,1},{9,13},{13,9},{2,6},{6,2},{1... | collective-permute-start | bytes 688136 | tf_op jit(solution)/shard_map/ppermute | solution.py:340
  14.0 16.7 %collective-permute-start.4 = (bf16[2,64,896]{2,1,0:T(8,128)(2,1)S(1)}, bf16[2,64,896]{2,1,0:T(8,128)(2,1)S(1)}, u32[]{:S(2)}, u32[]{:S(2)}) collective-permute-start(bf16[2,64,896]{2,1,0:T(8,128)(2,1)S(1)} %get-tuple-element.11), channel_id=1, source_target_pairs={{0,8},{4,12},{8,0},{12,4},{1,9},{5,13},{9,1},{13,5},{2,10},{6,14},... | collective-permute-start | bytes 688136 | tf_op jit(solution)/shard_map/ppermute | solution.py:340
  23.3 7.8 %collective-permute-start.5 = (bf16[2,64,896]{2,1,0:T(8,128)(2,1)S(1)}, bf16[2,64,896]{2,1,0:T(8,128)(2,1)S(1)}, u32[]{:S(2)}, u32[]{:S(2)}) collective-permute-start(bf16[2,64,896]{2,1,0:T(8,128)(2,1)S(1)} %get-tuple-element.12), channel_id=1, source_target_pairs={{0,12},{4,8},{8,4},{12,0},{1,13},{5,9},{9,5},{13,1},{2,14},{6,10},... | collective-permute-start | bytes 688136 | tf_op jit(solution)/shard_map/ppermute | solution.py:340
  27.1 8.5 %collective-permute-start.12 = (bf16[896,128]{1,0:T(8,128)(2,1)S(1)}, bf16[896,128]{1,0:T(8,128)(2,1)S(1)}, u32[]{:S(2)}, u32[]{:S(2)}) collective-permute-start(bf16[896,128]{1,0:T(8,128)(2,1)S(1)} %collective-permute-done.11.refs_4_), channel_id=1, source_target_pairs={{0,16},{1,17},{2,18},{3,19},{4,20},{5,21},{6,22},{7,23},{8,24},{9,... | collective-permute-start | bytes 688136 | tf_op jit(solution)/shard_map/ppermute | solution.py:290
  28.6 20.5 %collective-permute-start.8 = (bf16[2,896,128]{2,1,0:T(8,128)(2,1)S(1)}, bf16[2,896,128]{2,1,0:T(8,128)(2,1)S(1)}, u32[]{:S(2)}, u32[]{:S(2)}) collective-permute-start(bf16[2,896,128]{2,1,0:T(8,128)(2,1)S(1)} %collective-permute-done.7.refs_0_), channel_id=1, source_target_pairs={{0,16},{1,17},{2,18},{3,19},{4,20},{5,21},{6,22},{7,23},{8,24},{9,... | collective-permute-start | bytes 1376264 | tf_op jit(solution)/shard_map/ppermute | solution.py:290
  29.2 15.3 %collective-permute-start.13 = (bf16[896,128]{1,0:T(8,128)(2,1)S(1)}, bf16[896,128]{1,0:T(8,128)(2,1)S(1)}, u32[]{:S(2)}, u32[]{:S(2)}) collective-permute-start(bf16[896,128]{1,0:T(8,128)(2,1)S(1)} %collective-permute-done.11.refs_4_), channel_id=1, source_target_pairs={{0,8},{1,9},{2,10},{3,11},{4,12},{5,13},{6,14},{7,15},{8,0},{9,1},... | collective-permute-start | bytes 688136 | tf_op jit(solution)/shard_map/ppermute | solution.py:290
  30.7 16.3 %collective-permute-start.15 = (bf16[896,128]{1,0:T(8,128)(2,1)S(1)}, bf16[896,128]{1,0:T(8,128)(2,1)S(1)}, u32[]{:S(2)}, u32[]{:S(2)}) collective-permute-start(bf16[896,128]{1,0:T(8,128)(2,1)S(1)} %collective-permute-done.11.refs_4_), channel_id=1, source_target_pairs={{0,4},{1,5},{2,6},{3,7},{4,0},{5,1},{6,2},{7,3},{8,12},{9,13},{10,... | collective-permute-start | bytes 688136 | tf_op jit(solution)/shard_map/ppermute | solution.py:290
  31.1 17.5 %collective-permute-start.20 = (bf16[896,128]{1,0:T(8,128)(2,1)S(1)}, bf16[896,128]{1,0:T(8,128)(2,1)S(1)}, u32[]{:S(2)}, u32[]{:S(2)}) collective-permute-start(bf16[896,128]{1,0:T(8,128)(2,1)S(1)} %collective-permute-done.19.refs_0_), channel_id=1, source_target_pairs={{0,8},{1,9},{2,10},{3,11},{4,12},{5,13},{6,14},{7,15},{8,0},{9,1},... | collective-permute-start | bytes 688136 | tf_op jit(solution)/shard_map/ppermute | solution.py:290
  35.7 13.0 %collective-permute-start.21 = (bf16[896,128]{1,0:T(8,128)(2,1)S(1)}, bf16[896,128]{1,0:T(8,128)(2,1)S(1)}, u32[]{:S(2)}, u32[]{:S(2)}) collective-permute-start(bf16[896,128]{1,0:T(8,128)(2,1)S(1)} %collective-permute-done.19.refs_0_), channel_id=1, source_target_pairs={{0,16},{1,17},{2,18},{3,19},{4,20},{5,21},{6,22},{7,23},{8,24},{9,... | collective-permute-start | bytes 688136 | tf_op jit(solution)/shard_map/ppermute | solution.py:290
  38.4 21.4 %copy-start.3 = (bf16[256,2048]{1,0:T(8,128)(2,1)S(1)}, bf16[256,2048]{1,0:T(8,128)(2,1)}, u32[]{:S(2)}) copy-start(bf16[256,2048]{1,0:T(8,128)(2,1)} %queries_ref.3) | copy-start | bytes 3145732
  44.4 6.2 %collective-permute-start.6 = (bf16[144,896]{1,0:T(8,128)(2,1)S(1)}, bf16[144,896]{1,0:T(8,128)(2,1)S(1)}, u32[]{:S(2)}, u32[]{:S(2)}) collective-permute-start(bf16[144,896]{1,0:T(8,128)(2,1)S(1)} %get-tuple-element.14), channel_id=1, source_target_pairs={{0,1},{1,2},{2,3},{4,5},{5,6},{6,7},{8,9},{9,10},{10,11},{12,13},{... | collective-permute-start | bytes 774152 | tf_op jit(solution)/shard_map/ppermute | solution.py:386
  47.0 6.1 %collective-permute-start.14 = (bf16[896,128]{1,0:T(8,128)(2,1)S(1)}, bf16[896,128]{1,0:T(8,128)(2,1)S(1)}, u32[]{:S(2)}, u32[]{:S(2)}) collective-permute-start(bf16[896,128]{1,0:T(8,128)(2,1)S(1)} %collective-permute-done.12.refs_5_), channel_id=1, source_target_pairs={{0,8},{1,9},{2,10},{3,11},{4,12},{5,13},{6,14},{7,15},{8,0},{9,1},... | collective-permute-start | bytes 688136 | tf_op jit(solution)/shard_map/ppermute | solution.py:290
  48.6 10.5 %collective-permute-start.9 = (bf16[2,896,128]{2,1,0:T(8,128)(2,1)S(1)}, bf16[2,896,128]{2,1,0:T(8,128)(2,1)S(1)}, u32[]{:S(2)}, u32[]{:S(2)}) collective-permute-start(bf16[2,896,128]{2,1,0:T(8,128)(2,1)S(1)} %collective-permute-done.7.refs_0_), channel_id=1, source_target_pairs={{0,4},{1,5},{2,6},{3,7},{4,0},{5,1},{6,2},{7,3},{8,12},{9,13},{10,... | collective-permute-start | bytes 1376264 | tf_op jit(solution)/shard_map/ppermute | solution.py:290
  48.7 5.0 %collective-permute-start.16 = (bf16[896,128]{1,0:T(8,128)(2,1)S(1)}, bf16[896,128]{1,0:T(8,128)(2,1)S(1)}, u32[]{:S(2)}, u32[]{:S(2)}) collective-permute-start(bf16[896,128]{1,0:T(8,128)(2,1)S(1)} %collective-permute-done.12.refs_5_), channel_id=1, source_target_pairs={{0,4},{1,5},{2,6},{3,7},{4,0},{5,1},{6,2},{7,3},{8,12},{9,13},{10,... | collective-permute-start | bytes 688136 | tf_op jit(solution)/shard_map/ppermute | solution.py:290
  49.2 10.6 %collective-permute-start.10 = (bf16[2,896,128]{2,1,0:T(8,128)(2,1)S(1)}, bf16[2,896,128]{2,1,0:T(8,128)(2,1)S(1)}, u32[]{:S(2)}, u32[]{:S(2)}) collective-permute-start(bf16[2,896,128]{2,1,0:T(8,128)(2,1)S(1)} %collective-permute-done.8.refs_1_), channel_id=1, source_target_pairs={{0,4},{1,5},{2,6},{3,7},{4,0},{5,1},{6,2},{7,3},{8,12},{9,13},{10,... | collective-permute-start | bytes 1376264 | tf_op jit(solution)/shard_map/ppermute | solution.py:290
  50.7 3.0 %collective-permute-start.17 = (bf16[896,128]{1,0:T(8,128)(2,1)S(1)}, bf16[896,128]{1,0:T(8,128)(2,1)S(1)}, u32[]{:S(2)}, u32[]{:S(2)}) collective-permute-start(bf16[896,128]{1,0:T(8,128)(2,1)S(1)} %collective-permute-done.13.refs_6_), channel_id=1, source_target_pairs={{0,4},{1,5},{2,6},{3,7},{4,0},{5,1},{6,2},{7,3},{8,12},{9,13},{10,... | collective-permute-start | bytes 688136 | tf_op jit(solution)/shard_map/ppermute | solution.py:290
  53.1 6.0 %collective-permute-start.22 = (bf16[896,128]{1,0:T(8,128)(2,1)S(1)}, bf16[896,128]{1,0:T(8,128)(2,1)S(1)}, u32[]{:S(2)}, u32[]{:S(2)}) collective-permute-start(bf16[896,128]{1,0:T(8,128)(2,1)S(1)} %collective-permute-done.20.refs_1_), channel_id=1, source_target_pairs={{0,16},{1,17},{2,18},{3,19},{4,20},{5,21},{6,22},{7,23},{8,24},{9,... | collective-permute-start | bytes 688136 | tf_op jit(solution)/shard_map/ppermute | solution.py:290
  53.7 6.0 %collective-permute-start.18 = (bf16[896,128]{1,0:T(8,128)(2,1)S(1)}, bf16[896,128]{1,0:T(8,128)(2,1)S(1)}, u32[]{:S(2)}, u32[]{:S(2)}) collective-permute-start(bf16[896,128]{1,0:T(8,128)(2,1)S(1)} %collective-permute-done.14.refs_7_), channel_id=1, source_target_pairs={{0,4},{1,5},{2,6},{3,7},{4,0},{5,1},{6,2},{7,3},{8,12},{9,13},{10,... | collective-permute-start | bytes 688136 | tf_op jit(solution)/shard_map/ppermute | solution.py:290
  53.7 13.6 %collective-permute-start.23 = (bf16[896,128]{1,0:T(8,128)(2,1)S(1)}, bf16[896,128]{1,0:T(8,128)(2,1)S(1)}, u32[]{:S(2)}, u32[]{:S(2)}) collective-permute-start(bf16[896,128]{1,0:T(8,128)(2,1)S(1)} %collective-permute-done.19.refs_0_), channel_id=1, source_target_pairs={{0,4},{1,5},{2,6},{3,7},{4,0},{5,1},{6,2},{7,3},{8,12},{9,13},{10,... | collective-permute-start | bytes 688136 | tf_op jit(solution)/shard_map/ppermute | solution.py:290
  59.2 8.1 %collective-permute-start.24 = (bf16[896,128]{1,0:T(8,128)(2,1)S(1)}, bf16[896,128]{1,0:T(8,128)(2,1)S(1)}, u32[]{:S(2)}, u32[]{:S(2)}) collective-permute-start(bf16[896,128]{1,0:T(8,128)(2,1)S(1)} %collective-permute-done.20.refs_1_), channel_id=1, source_target_pairs={{0,4},{1,5},{2,6},{3,7},{4,0},{5,1},{6,2},{7,3},{8,12},{9,13},{10,... | collective-permute-start | bytes 688136 | tf_op jit(solution)/shard_map/ppermute | solution.py:290
  59.2 8.1 %collective-permute-start.25 = (bf16[896,128]{1,0:T(8,128)(2,1)S(1)}, bf16[896,128]{1,0:T(8,128)(2,1)S(1)}, u32[]{:S(2)}, u32[]{:S(2)}) collective-permute-start(bf16[896,128]{1,0:T(8,128)(2,1)S(1)} %collective-permute-done.21.refs_2_), channel_id=1, source_target_pairs={{0,4},{1,5},{2,6},{3,7},{4,0},{5,1},{6,2},{7,3},{8,12},{9,13},{10,... | collective-permute-start | bytes 688136 | tf_op jit(solution)/shard_map/ppermute | solution.py:290
  59.7 7.6 %collective-permute-start.26 = (bf16[896,128]{1,0:T(8,128)(2,1)S(1)}, bf16[896,128]{1,0:T(8,128)(2,1)S(1)}, u32[]{:S(2)}, u32[]{:S(2)}) collective-permute-start(bf16[896,128]{1,0:T(8,128)(2,1)S(1)} %collective-permute-done.22.refs_3_), channel_id=1, source_target_pairs={{0,4},{1,5},{2,6},{3,7},{4,0},{5,1},{6,2},{7,3},{8,12},{9,13},{10,... | collective-permute-start | bytes 688136 | tf_op jit(solution)/shard_map/ppermute | solution.py:290
  59.7 7.6 %copy-start.1 = (bf16[896,1024]{1,0:T(8,128)(2,1)S(1)}, bf16[896,1024]{1,0:T(8,128)(2,1)}, u32[]{:S(2)}) copy-start(bf16[896,1024]{1,0:T(8,128)(2,1)} %weight_ref.1) | copy-start | bytes 5505028
  (3 other events, 15.2 us)

commit v3 on v2

v3 whole, which is shorter than its diff:
```python
import functools
import math

import jax
import jax.numpy as jnp
from jax import lax
from jax.experimental import pallas as pl
from jax.experimental.pallas import tpu as pltpu
from jax.sharding import PartitionSpec as P

ENC_HEADS = 14
ENCODER_HEAD_DIM = 64
ENCODER_WIDTH = 896
CROSS_HEADS = 16
CROSS_HEAD = 128
BLOCK_LEN = 64
NEIGHBOUR_LENGTH = 64
NEIGHBOUR_COUNT = 2
CROSS_WIDTH = CROSS_HEADS * CROSS_HEAD
KEYS = NEIGHBOUR_COUNT * NEIGHBOUR_LENGTH
LANES = 128
FLAG_ROWS = 16
EDGE = 16
PAIRS_AT_ONCE = 2
DISTANCES = (3, 1, 2)

MASKED_SCORE = -1e30
AXES = ("groups", "cache", "span")
VMEM = pl.BlockSpec(memory_space=pltpu.VMEM)
SMEM = pl.BlockSpec(memory_space=pltpu.SMEM)
ANY = pl.BlockSpec(memory_space=pl.ANY)
NT = (((1,), (1,)), ((), ()))
TN = (((0,), (0,)), ((), ()))


def dot(a, b, dims=(((1,), (0,)), ((), ()))):
    return lax.dot_general(a, b, dims, preferred_element_type=jnp.float32)


def entry_id(ids_ref, request):
    return ids_ref[request % NEIGHBOUR_COUNT, request // NEIGHBOUR_COUNT]


def fetch_kernel(peers, capacity, cache_slots, requests, targets, *refs):
    wanted = refs[: peers - 1]
    cache_ref = refs[peers - 1]
    outs = refs[peers:-3]
    ids, ids_sem, sem = refs[-3:]

    def place(r, k):
        out, base = targets[r]
        return outs[out].at[base + k]

    me = lax.axis_index("cache")
    for r in range(peers - 1):
        pltpu.make_async_copy(wanted[r], ids.at[r], ids_sem.at[r]).start()
    counts = []
    for r in range(peers - 1):
        pltpu.make_async_copy(wanted[r], ids.at[r], ids_sem.at[r]).wait()
        count = jnp.int32(0)
        for i in range(requests):
            slot = entry_id(ids.at[r], i) - me * cache_slots
            hit = (slot >= 0) & (slot < cache_slots) & (count < capacity)

            @pl.when(hit)
            def _(r=r, count=count, slot=slot):
                pltpu.make_async_copy(
                    cache_ref.at[slot], place(r, count), sem.at[r, count]
                ).start()

            count = count + hit.astype(jnp.int32)
        counts.append(count)
    for r in range(peers - 1):
        for k in range(capacity):

            @pl.when(counts[r] > k)
            def _(r=r, k=k):
                pltpu.make_async_copy(cache_ref.at[0], place(r, k), sem.at[r, k]).wait()


def usable_row(first, second):
    lane = lax.broadcasted_iota(jnp.int32, (1, KEYS), 1)
    limit = jnp.where(lane < NEIGHBOUR_LENGTH, first, second + NEIGHBOUR_LENGTH)
    return lane < limit


def encode_kernel(peers, capacity, cache_slots, blocks, chosen, *refs):
    ids_ref, lengths_ref, states_ref, weight_ref, cache_ref = refs[:5]
    arrived = refs[5 : 5 + peers - 1]
    out_ref, entries, queries, sem = refs[5 + peers - 1 :]
    me = lax.axis_index("cache")
    width = ENCODER_WIDTH
    start = chosen[0]
    ids = [entry_id(ids_ref, i) for i in range((chosen[-1] + 1) * NEIGHBOUR_COUNT)]
    owners = [v // cache_slots for v in ids]
    first_request = start * NEIGHBOUR_COUNT
    for i in range(first_request, len(ids)):
        rank = jnp.int32(0)
        for j in range(i):
            rank = rank + (owners[j] == owners[i]).astype(jnp.int32)
        rank = jnp.minimum(rank, capacity - 1)
        rel = owners[i] ^ me
        slot = ids[i] - owners[i] * cache_slots
        at = i - first_request

        @pl.when(rel == 0)
        def _(at=at, slot=slot):
            pltpu.make_async_copy(cache_ref.at[slot], entries.at[at], sem.at[at]).start()

        for r in range(1, peers):

            @pl.when(rel == r)
            def _(at=at, r=r, rank=rank):
                pltpu.make_async_copy(arrived[r - 1].at[rank], entries.at[at], sem.at[at]).start()

    low = lax.broadcasted_iota(jnp.int32, (BLOCK_LEN, LANES), 1) < ENCODER_HEAD_DIM
    per_pair = LANES // ENCODER_HEAD_DIM
    scale = 1.0 / math.sqrt(ENCODER_HEAD_DIM)

    def both(rows):
        zero = jnp.zeros_like(rows)
        return jnp.concatenate([jnp.where(low, rows, zero), jnp.where(low, zero, rows)], axis=0)

    def project(b):
        first = b * NEIGHBOUR_COUNT
        for i in range(first, first + NEIGHBOUR_COUNT):
            pltpu.make_async_copy(cache_ref.at[0], entries.at[i], sem.at[i]).wait()
        rows = entries[first : first + NEIGHBOUR_COUNT].reshape(KEYS, width)
        queries[b * KEYS : (b + 1) * KEYS, :] = dot(rows, weight_ref[...]).astype(jnp.bfloat16)

    def scores_of(b, pairs):
        scores = []
        for p in pairs:
            cols = slice(p * LANES, (p + 1) * LANES)
            keys = both(states_ref[(start + b) * BLOCK_LEN : (start + b + 1) * BLOCK_LEN, cols])
            scores.append(dot(keys, queries[b * KEYS : (b + 1) * KEYS, cols], NT))
        return jnp.concatenate(scores, axis=0).reshape(-1, BLOCK_LEN, KEYS) * scale

    def finish(b, pairs, scores):
        weights = jnp.exp(scores - jnp.max(scores, axis=1, keepdims=True))
        weights = weights * (1.0 / jnp.sum(weights, axis=1, keepdims=True))
        weights = weights.reshape(-1, KEYS).astype(jnp.bfloat16)
        first = b * NEIGHBOUR_COUNT
        for n, p in enumerate(pairs):
            cols = slice(p * LANES, (p + 1) * LANES)
            values = slice(width + p * LANES, width + (p + 1) * LANES)
            values = both(
                states_ref[(start + b) * BLOCK_LEN : (start + b + 1) * BLOCK_LEN, values]
            )
            height = per_pair * BLOCK_LEN
            attended = dot(weights[n * height : (n + 1) * height], values, TN)
            owned = entries[first : first + NEIGHBOUR_COUNT, :, cols].reshape(KEYS, LANES)
            encoded = (owned.astype(jnp.float32) + attended).astype(jnp.bfloat16)
            out_ref[b * KEYS : (b + 1) * KEYS, cols] = encoded

    for b in range(len(chosen)):
        project(b)
    pairs = width // LANES
    groups = [range(p, min(p + PAIRS_AT_ONCE, pairs)) for p in range(0, pairs, PAIRS_AT_ONCE)]
    steps = [(b, g) for b in range(len(chosen)) for g in groups]
    scores = scores_of(*steps[0])
    for n, step in enumerate(steps):
        after = scores_of(*steps[n + 1]) if n + 1 < len(steps) else None
        finish(*step, scores)
        scores = after
    if chosen[-1] == blocks - 1:
        flags = usable_row(lengths_ref[0, blocks - 1], lengths_ref[1, blocks - 1])
        flags = jnp.broadcast_to(flags.astype(jnp.float32), (FLAG_ROWS, LANES))
        out_ref[len(chosen) * KEYS :, :] = jnp.zeros((FLAG_ROWS, width), jnp.bfloat16)
        out_ref[len(chosen) * KEYS :, :LANES] = flags.astype(jnp.bfloat16)


def cross_heads(blocks, lengths_ref, encoded_ref, last_ref, prior_ref, queries_ref, out_ref, items, swap):
    span = lax.axis_index("span")
    scale = 1.0 / math.sqrt(CROSS_HEAD)
    last_row = lax.broadcasted_iota(jnp.int32, (EDGE, CROSS_HEAD), 0) == EDGE - 1
    flags = [prior_ref[KEYS : KEYS + FLAG_ROWS, :LANES].astype(jnp.float32)[:1] > 0.5]
    for b in range(blocks):
        flags.append(usable_row(lengths_ref[0, b], lengths_ref[1, b]))
    tokens = blocks * BLOCK_LEN
    ranges = [
        (max(0, (u + 1) * BLOCK_LEN - EDGE), min(tokens, (u + 2) * BLOCK_LEN))
        for u in range(-1, blocks)
    ]

    def project(load):
        weights = jnp.concatenate(load(), axis=1)
        rows = jnp.concatenate(
            [prior_ref[:KEYS, :], encoded_ref[...], last_ref[:KEYS, :]], axis=0
        )
        states = dot(rows, weights).astype(jnp.bfloat16)
        return [states[b * KEYS : (b + 1) * KEYS] for b in range(blocks + 1)]

    states = project(items[0][2])
    for n, (columns, target, _) in enumerate(items):
        scores, values = [], []
        for (start, stop), state, flag in zip(ranges, states, flags):
            left, right = state[:, :CROSS_HEAD], state[:, CROSS_HEAD:]
            if swap is not None:
                left, right = jnp.where(swap, right, left), jnp.where(swap, left, right)
            score = dot(queries_ref[start:stop, columns], left, NT) * scale
            scores.append(jnp.where(flag, score, MASKED_SCORE))
            values.append(right)
        scores = jnp.concatenate(scores, axis=0)
        if n + 1 < len(items):
            states = project(items[n + 1][2])
        weights = jnp.exp(scores - jnp.max(scores, axis=1, keepdims=True))
        weights = weights * (1.0 / jnp.sum(weights, axis=1, keepdims=True))
        weights = weights.astype(jnp.bfloat16)
        at, tail = 0, None
        for u, (start, stop) in enumerate(ranges):
            part = weights[at : at + stop - start]
            result = dot(part, values[u]).astype(jnp.bfloat16)
            at += stop - start
            if u == 0:
                result = jnp.where(span > 0, result, jnp.zeros_like(result))
            else:
                out_ref[start : start + EDGE, target] = jnp.where(last_row, result[:EDGE], tail)
                result = result[EDGE:]
                start += EDGE
            if u < blocks:
                out_ref[start : stop - EDGE, target] = result[: stop - EDGE - start]
                tail = result[stop - EDGE - start :]


def head_columns(head):
    if isinstance(head, int):
        return slice(head * CROSS_HEAD, (head + 1) * CROSS_HEAD)
    return pl.ds(pl.multiple_of(head * CROSS_HEAD, CROSS_HEAD), CROSS_HEAD)


def whole_kernel(
    blocks, lengths_ref, encoded_ref, last_ref, prior_ref, queries_ref, weight_ref, out_ref
):
    def item(head):
        load = lambda: [
            weight_ref[:, head_columns(head)],
            weight_ref[:, head_columns(CROSS_HEADS + head)],
        ]
        return head_columns(head), head_columns(head), load

    items = [item(head) for head in range(CROSS_HEADS)]
    cross_heads(
        blocks, lengths_ref, encoded_ref, last_ref, prior_ref, queries_ref, out_ref, items, None
    )


def place_of():
    return lax.axis_index("groups") * 4 + lax.axis_index("cache")


def head_of(low, place):
    return ((low ^ lax.axis_index("span")) & 1) * 8 + place


def pieces_kernel(offsets, resumed, blocks, *refs):
    lengths_ref, encoded_ref, last_ref, prior_ref, queries_ref, weight_ref = refs[:6]
    out_ref = refs[-1]
    groups = refs[6:-1]
    if resumed:
        out_ref[...] = groups[-1][...]
        groups = groups[:-1]
    share = len(groups) // len(offsets)

    def piece(held, distance):
        start = DISTANCES.index(distance) * ENCODER_WIDTH
        stop = start + ENCODER_WIDTH
        parts = []
        for ref in held:
            rows = ref.shape[0]
            if start < rows and stop > 0:
                parts.append(ref[max(start, 0) : min(stop, rows), :])
            start, stop = start - rows, stop - rows
        return parts[0] if len(parts) == 1 else jnp.concatenate(parts, axis=0)

    def item(offset, held, own):
        column = offset ^ place_of()

        def load():
            if own:
                return [weight_ref[:, head_columns(column)], piece(held, 2)]
            return [piece(held, 1), piece(held, 3)]

        columns = head_columns(head_of(0 if own else 1, column))
        return columns, columns, load

    items = []
    for n, offset in enumerate(offsets):
        held = groups[n * share : (n + 1) * share]
        items += [item(offset, held, False), item(offset, held, True)]
    swap = lax.axis_index("span") >= 2
    cross_heads(
        blocks, lengths_ref, encoded_ref, last_ref, prior_ref, queries_ref, out_ref, items, swap
    )


def permute(value, move):
    sizes = [lax.axis_size(axis) for axis in AXES]
    flat = lambda g, c, s: (g * sizes[1] + c) * sizes[2] + s
    pairs = []
    for g in range(sizes[0]):
        for c in range(sizes[1]):
            for s in range(sizes[2]):
                pairs.append((flat(g, c, s), flat(*move(g, c, s))))
    return lax.ppermute(value, AXES, pairs)


def over_x(value):
    return permute(value, lambda g, c, s: (g ^ 1, c, s))


def over_y(value):
    return permute(value, lambda g, c, s: (g, c ^ 2, s))


def over_core(value):
    return permute(value, lambda g, c, s: (g, c ^ 1, s))


def after(value, *others):
    return lax.optimization_barrier((value, *others))[0]


def from_spans(cross_weight):
    own = lax.dynamic_slice_in_dim(cross_weight, place_of() * CROSS_HEAD, CROSS_HEAD, axis=1)
    return [permute(own, lambda g, c, s, d=d: (g, c, s ^ d)) for d in DISTANCES]


def per_device(
    block_states,
    cross_queries,
    neighbour_cache,
    neighbour_owner,
    neighbour_slot,
    neighbour_lengths,
    encoder_query,
    cross_weight,
):
    peers = lax.axis_size("cache")
    spans = lax.axis_size("span")
    blocks = neighbour_owner.shape[0]
    requests = blocks * NEIGHBOUR_COUNT
    capacity = max(2, (requests + peers - 1) // peers)
    cache_slots = neighbour_cache.shape[0]
    swap = lambda v, r: lax.ppermute(v, "cache", [(i, i ^ r) for i in range(peers)])
    pieced = lax.axis_size("groups") == 2 and peers == 4 and spans == 4

    ids = neighbour_owner.T * cache_slots + neighbour_slot.T
    lengths = neighbour_lengths.T
    wanted = [swap(ids, r) for r in range(1, peers)]
    if pieced:
        pieces = from_spans(cross_weight)
    else:
        weights = lax.all_gather(cross_weight, "span", axis=1, tiled=True)
    counts = [1, 2] if pieced else [1] * (peers - 1)
    targets = [(0, 0), (1, 0), (1, capacity)] if pieced else [(r, 0) for r in range(peers - 1)]
    fetched = pl.pallas_call(
        functools.partial(fetch_kernel, peers, capacity, cache_slots, requests, targets),
        out_shape=[
            jax.ShapeDtypeStruct((n * capacity, NEIGHBOUR_LENGTH, ENCODER_WIDTH), jnp.bfloat16)
            for n in counts
        ],
        in_specs=[ANY] * peers,
        out_specs=[VMEM] * len(counts),
        scratch_shapes=[
            pltpu.SMEM((peers - 1, NEIGHBOUR_COUNT, blocks), jnp.int32),
            pltpu.SemaphoreType.DMA((peers - 1,)),
            pltpu.SemaphoreType.DMA((peers - 1, capacity)),
        ],
        compiler_params=pltpu.CompilerParams(vmem_limit_bytes=16 * 2**20),
        name="fetch",
    )(*wanted, neighbour_cache)
    if pieced:
        beside = over_y(fetched[1])
        arrived = [over_core(fetched[0]), beside, over_core(beside[capacity:])]
        pieces = jnp.concatenate([after(v, fetched[0]) for v in pieces], axis=0)
        x_pieces, y_pieces = over_x(pieces), over_y(pieces)
    else:
        arrived = [swap(v, r) for r, v in enumerate(fetched, 1)]

    def encode(chosen, extra):
        count = len(chosen)
        return pl.pallas_call(
            functools.partial(encode_kernel, peers, capacity, cache_slots, blocks, chosen),
            out_shape=jax.ShapeDtypeStruct((count * KEYS + extra, ENCODER_WIDTH), jnp.bfloat16),
            in_specs=[SMEM] * 2 + [VMEM] * 2 + [ANY] * peers,
            out_specs=VMEM,
            scratch_shapes=[
                pltpu.VMEM((2 * count, NEIGHBOUR_LENGTH, ENCODER_WIDTH), jnp.bfloat16),
                pltpu.VMEM((count * KEYS, ENCODER_WIDTH), jnp.bfloat16),
                pltpu.SemaphoreType.DMA((2 * count,)),
            ],
            compiler_params=pltpu.CompilerParams(vmem_limit_bytes=16 * 2**20),
            cost_estimate=pl.CostEstimate(
                flops=2 * count * KEYS * ENCODER_WIDTH * (ENCODER_WIDTH + 4 * LANES),
                bytes_accessed=2 * count * 2**20,
                transcendentals=count * KEYS * ENC_HEADS * BLOCK_LEN,
            ),
            name="encode",
        )(ids, lengths, block_states, encoder_query, neighbour_cache, *arrived)

    last = encode(range(blocks - 1, blocks), FLAG_ROWS)
    prior = lax.ppermute(last, "span", [(i, i + 1) for i in range(spans - 1)])
    encoded = encode(range(blocks - 1), 0)

    def cross(kernel, heads, *operands):
        return pl.pallas_call(
            functools.partial(kernel, blocks),
            out_shape=jax.ShapeDtypeStruct(cross_queries.shape, jnp.bfloat16),
            in_specs=[SMEM] + [VMEM] * (4 + len(operands)),
            out_specs=VMEM,
            compiler_params=pltpu.CompilerParams(vmem_limit_bytes=32 * 2**20),
            cost_estimate=pl.CostEstimate(
                flops=4 * (blocks + 1) * KEYS * (ENCODER_WIDTH + 2 * LANES) * heads * CROSS_HEAD,
                bytes_accessed=8 * 2**20,
                transcendentals=(blocks + 1) * KEYS * BLOCK_LEN * heads,
            ),
            name="cross",
        )(lengths, encoded, last, prior, cross_queries, *operands)

    if not pieced:
        return cross(whole_kernel, CROSS_HEADS, weights)

    def part(done, offsets, *operands):
        kernel = functools.partial(pieces_kernel, offsets, bool(done))
        return [cross(kernel, 2 * len(offsets), cross_weight, *operands, *done)]

    done = part([], (0, 1), pieces, over_core(pieces))
    middle = pieces.shape[0] // 2
    hop = [over_y(after(x_pieces[:middle], *done)), over_x(after(y_pieces[middle:], *done))]
    done = part(
        done,
        (4, 2, 5, 3),
        x_pieces,
        y_pieces,
        *[over_core(after(v, *done)) for v in (x_pieces, y_pieces)],
    )
    hop += [over_core(after(v, *done)) for v in hop]
    return part(done, (6, 7), *hop)[0]


def solution(mesh):
    placed = (
        P(("groups", "cache", "span"), None),
        P(("groups", "cache", "span"), None),
        P(("groups", "cache"), None, None),
        P(("groups", "cache", "span"), None),
        P(("groups", "cache", "span"), None),
        P(("groups", "cache", "span"), None),
        P(),
        P(None, "span"),
    )
    return jax.shard_map(
        per_device,
        mesh=mesh,
        in_specs=placed,
        out_specs=P(("groups", "cache", "span"), None),
        check_vma=False,
    )
```

time: 76.1 us -> 65.9 us (0.87)
  waiting for transfers between devices: 27.4 us -> 16.1 us
  starting transfers between devices: 21.9 us -> 19.4 us
  Pallas kernels: 23.9 us -> 25.9 us
  local copies, waits for them, and re-layouts: 2.45 us -> 3.49 us
    ppermute x20 -> x15, waiting for transfers between devices: 23.4 us -> 13.2 us  [permute(): return lax.ppermute(value, AXES, pairs)]
    ppermute x6 -> x3, starting transfers between devices: 4.12 us -> 2.59 us  [per_device(): lax.ppermute(v, 'cache', [(i, i ^ r) for i in range(peers)])]
    unnamed x16, local copies, waits for them, and re-layouts: 1.21 us -> 2.42 us
    ppermute x20 -> x15, starting transfers between devices: 15.2 us -> 14 us  [permute(): return lax.ppermute(value, AXES, pairs)]
    pallas_call x2 -> x3, Pallas kernels: 16.1 us -> 17.2 us  [cross(): pl.pallas_call(functools.partial(kernel, blocks), out_shape=jax.ShapeDtyp...]
    pallas_call x1 -> x2, Pallas kernels: 6.06 us -> 6.93 us  [encode(): pl.pallas_call(functools.partial(encode_kernel, peers, capacity, cache_sl...]
    ppermute x6 -> x3, waiting for transfers between devices: 2.59 us -> 2.07 us  [per_device(): lax.ppermute(v, 'cache', [(i, i ^ r) for i in range(peers)])]
  transfers between devices with their start and end apart: 27 -> 19, of which waited for: 9 -> 10; matrix products, arithmetic and copies ran while one was open for 0% -> 1% of each run, Pallas kernels for 20% -> 31%
where the time goes in v3:
time: 65.9 us; the launch traced here: 65.7 us
  Pallas kernels  25.9 us (39%)
  starting transfers between devices  19.4 us (29%)
  waiting for transfers between devices  16.1 us (24%)
  local copies, waits for them, and re-layouts  3.49 us (5%)
  other arithmetic  0.7 us (1%)
    pallas_call x3, Pallas kernels, cross(): pl.pallas_call(functools.partial(kernel, blocks), out_shape=jax.ShapeDtyp...  17.2 us
    ppermute x15, starting transfers between devices, permute(): return lax.ppermute(value, AXES, pairs)  14 us
    ppermute x15, waiting for transfers between devices, permute(): return lax.ppermute(value, AXES, pairs)  13.2 us
    pallas_call x2, Pallas kernels, encode(): pl.pallas_call(functools.partial(encode_kernel, peers, capacity, cache_sl...  6.93 us
    ppermute x1, starting transfers between devices, per_device(): prior = lax.ppermute(last, 'span', [(i, i + 1) for i in range(spans - 1)])  2.81 us
    ppermute x3, starting transfers between devices, per_device(): lax.ppermute(v, 'cache', [(i, i ^ r) for i in range(peers)])  2.59 us
    unnamed x16, local copies, waits for them, and re-layouts  2.42 us
    ppermute x3, waiting for transfers between devices, per_device(): lax.ppermute(v, 'cache', [(i, i ^ r) for i in range(peers)])  2.07 us
  transfers between devices with their start and end apart: 19, of which 10 were waited for; matrix products, arithmetic and copies ran while one was open for 1% of the time, Pallas kernels for 31%

profile of v3, /device:TPU:0, one launch (start us, length us, event | category | flops | bytes accessed | tf_op | source)
XLA Modules:
  0.0 65.7 jit_solution(16603718768365757573)
XLA Ops:
  0.0 1.0 %constant_dynamic-slice_fusion = bf16[896,128]{1,0:T(8,128)(2,1)S(1)} fusion(bf16[896,1024]{1,0:T(8,128)(2,1)} %refs_5_.5, s32[]{:T(128)S(6)} %select_n.3), kind=kLoop, calls=%fused_computation.4 | loop fusion | bytes 458756 | tf_op jit(solution)/shard_map/dynamic_slice | solution.py:325
  1.0 5.1 %collective-permute-start.7 = (bf16[896,128]{1,0:T(8,128)(2,1)S(1)}, bf16[896,128]{1,0:T(8,128)(2,1)S(1)}, u32[]{:S(2)}, u32[]{:S(2)}) collective-permute-start(bf16[896,128]{1,0:T(8,128)(2,1)S(1)} %constant_dynamic-slice_fusion), channel_id=1, source_target_pairs={{0,3},{1,2},{2,1},{3,0},{4,7},{5,6},{6,5},{7,4},{8,11},{9,10},{10,... | collective-permute-start | bytes 688136 | tf_op jit(solution)/shard_map/ppermute | solution.py:305
  6.1 0.6 collective-permute-start.9
  6.7 0.7 %add_bitcast_fusion.refs_0_ = s32[2,4]{1,0:T(2,128)S(1)} fusion(s32[4,2]{0,1:T(2,128)} %param.12, s32[4,2]{0,1:T(2,128)} %param.11), kind=kLoop, calls=%fused_computation.3 | loop fusion | flops 16 | bytes 96 | tf_op jit(solution)/shard_map/add | solution.py:348
  7.4 1.7 %collective-permute-start.1 = (s32[2,4]{1,0:T(2,128)S(1)}, s32[2,4]{1,0:T(2,128)S(1)}, u32[]{:S(2)}, u32[]{:S(2)}) collective-permute-start(s32[2,4]{1,0:T(2,128)S(1)} %add_bitcast_fusion.refs_0_), channel_id=1, source_target_pairs={{0,8},{4,12},{8,0},{12,4},{1,9},{5,13},{9,1},{13,5},{2,10},{6,14},... | collective-permute-start | bytes 104 | tf_op jit(solution)/shard_map/ppermute | solution.py:345
  9.1 0.9 %collective-permute-start.2 = (s32[2,4]{1,0:T(2,128)S(1)}, s32[2,4]{1,0:T(2,128)S(1)}, u32[]{:S(2)}, u32[]{:S(2)}) collective-permute-start(s32[2,4]{1,0:T(2,128)S(1)} %add_bitcast_fusion.refs_0_), channel_id=1, source_target_pairs={{0,12},{4,8},{8,4},{12,0},{1,13},{5,9},{9,5},{13,1},{2,14},{6,10},... | collective-permute-start | bytes 104 | tf_op jit(solution)/shard_map/ppermute | solution.py:345
  10.0 1.0 %collective-permute-done.1.refs_1_ = s32[2,4]{1,0:T(2,128)S(1)} collective-permute-done((s32[2,4]{1,0:T(2,128)S(1)}, s32[2,4]{1,0:T(2,128)S(1)}, u32[]{:S(2)}, u32[]{:S(2)}) %collective-permute-start.1) | collective-permute-done | bytes 64 | tf_op jit(solution)/shard_map/ppermute | solution.py:345
  11.0 1.1 %collective-permute-done.2.refs_2_ = s32[2,4]{1,0:T(2,128)S(1)} collective-permute-done((s32[2,4]{1,0:T(2,128)S(1)}, s32[2,4]{1,0:T(2,128)S(1)}, u32[]{:S(2)}, u32[]{:S(2)}) %collective-permute-start.2) | collective-permute-done | bytes 64 | tf_op jit(solution)/shard_map/ppermute | solution.py:345
  12.1 1.2 %copy-done.1 = bf16[8,64,896]{2,1,0:T(8,128)(2,1)S(1)} copy-done((bf16[8,64,896]{2,1,0:T(8,128)(2,1)S(1)}, bf16[8,64,896]{2,1,0:T(8,128)(2,1)}, u32[]{:S(2)}) %copy-start.1) | copy-done | bytes 917528
  13.3 1.8 %fetch.1 = (bf16[2,64,896]{2,1,0:T(8,128)(2,1)S(1)}, bf16[4,64,896]{2,1,0:T(8,128)(2,1)S(1)}) custom-call(s32[2,4]{1,0:T(2,128)S(1)} %collective-permute-done.refs_0_, s32[2,4]{1,0:T(2,128)S(1)} %collective-permute-done.1.refs_1_, s32[2,4]{1,0:T(2,128)S(1)} %collective-permute-done.2.refs_2_, bf16[8,64,896]{2,1,0:T(8,128)(2,1)S(1)} %copy-done.1), custom_call_target="tpu_custom_call" | custom-call | tf_op jit(solution)/shard_map/fetch/pallas_call | solution.py:357
  15.1 1.2 %collective-permute-start.4 = (bf16[4,64,896]{2,1,0:T(8,128)(2,1)S(1)}, bf16[4,64,896]{2,1,0:T(8,128)(2,1)S(1)}, u32[]{:S(2)}, u32[]{:S(2)}) collective-permute-start(bf16[4,64,896]{2,1,0:T(8,128)(2,1)S(1)} %get-tuple-element.17), channel_id=1, source_target_pairs={{0,8},{1,9},{2,10},{3,11},{4,12},{5,13},{6,14},{7,15},{8,0},{9,1},... | collective-permute-start | bytes 1376264 | tf_op jit(solution)/shard_map/ppermute | solution.py:305
  16.3 1.4 %collective-permute-done.8 = bf16[896,128]{1,0:T(8,128)(2,1)S(1)} collective-permute-done((bf16[896,128]{1,0:T(8,128)(2,1)S(1)}, bf16[896,128]{1,0:T(8,128)(2,1)S(1)}, u32[]{:S(2)}, u32[]{:S(2)}) %collective-permute-start.8) | collective-permute-done | bytes 229408 | tf_op jit(solution)/shard_map/ppermute | solution.py:305
  17.7 7.9 %collective-permute-done.9 = bf16[896,128]{1,0:T(8,128)(2,1)S(1)} collective-permute-done((bf16[896,128]{1,0:T(8,128)(2,1)S(1)}, bf16[896,128]{1,0:T(8,128)(2,1)S(1)}, u32[]{:S(2)}, u32[]{:S(2)}) %collective-permute-start.9) | collective-permute-done | bytes 229408 | tf_op jit(solution)/shard_map/ppermute | solution.py:305
  25.7 1.6 %collective-permute-start.13 = (bf16[2688,128]{1,0:T(8,128)(2,1)S(1)}, bf16[2688,128]{1,0:T(8,128)(2,1)S(1)}, u32[]{:S(2)}, u32[]{:S(2)}) collective-permute-start(bf16[2688,128]{1,0:T(8,128)(2,1)S(1)} %constant_dynamic-update-slice_fusion.refs_6_), channel_id=1, source_target_pairs={{0,8},{1,9},{2,10},{3,11},{4,12},{5,13},{6,14},{7,15},{8,0},{9,1},... | collective-permute-start | bytes 2064392 | tf_op jit(solution)/shard_map/ppermute | solution.py:305
  27.3 1.5 %collective-permute-start.10 = (bf16[2688,128]{1,0:T(8,128)(2,1)S(1)}, bf16[2688,128]{1,0:T(8,128)(2,1)S(1)}, u32[]{:S(2)}, u32[]{:S(2)}) collective-permute-start(bf16[2688,128]{1,0:T(8,128)(2,1)S(1)} %constant_dynamic-update-slice_fusion.refs_6_), channel_id=1, source_target_pairs={{0,16},{1,17},{2,18},{3,19},{4,20},{5,21},{6,22},{7,23},{8,24},{9,... | collective-permute-start | bytes 2064392 | tf_op jit(solution)/shard_map/ppermute | solution.py:305
  28.8 0.6 collective-permute-start.5
  29.4 0.9 %collective-permute-done.3.refs_5_ = bf16[2,64,896]{2,1,0:T(8,128)(2,1)S(1)} collective-permute-done((bf16[2,64,896]{2,1,0:T(8,128)(2,1)S(1)}, bf16[2,64,896]{2,1,0:T(8,128)(2,1)S(1)}, u32[]{:S(2)}, u32[]{:S(2)}) %collective-permute-start.3) | collective-permute-done | bytes 229408 | tf_op jit(solution)/shard_map/ppermute | solution.py:305
  30.3 0.3 collective-permute-done.5.refs_7_
  30.7 1.2 %copy-done.5 = bf16[256,1792]{1,0:T(8,128)(2,1)S(1)} copy-done((bf16[256,1792]{1,0:T(8,128)(2,1)S(1)}, bf16[256,1792]{1,0:T(8,128)(2,1)}, u32[]{:S(2)}) %copy-start.5) | copy-done | bytes 917528
  31.8 2.0 %encode.3.refs_2_ = bf16[144,896]{1,0:T(8,128)(2,1)S(1)} custom-call(s32[2,4]{1,0:T(2,128)S(1)} %add_bitcast_fusion.refs_0_, s32[2,4]{1,0:T(2,128)S(1)} %bitcast.3, bf16[256,1792]{1,0:T(8,128)(2,1)S(1)} %copy-done.5, bf16[896,896]{1,0:T(8,128)(2,1)S(1)} %copy-done.3, bf16[8,64,896]{2,1,0:T(8,128)(2,1)S(1)} %copy-done.2, ...), custom_call_target="tpu_custom_call" | custom-call | flops 322961408 | bytes 2097152 | tf_op jit(solution)/shard_map/encode/pallas_call | solution.py:383
  33.9 2.8 %collective-permute-start.6 = (bf16[144,896]{1,0:T(8,128)(2,1)S(1)}, bf16[144,896]{1,0:T(8,128)(2,1)S(1)}, u32[]{:S(2)}, u32[]{:S(2)}) collective-permute-start(bf16[144,896]{1,0:T(8,128)(2,1)S(1)} %encode.3.refs_2_), channel_id=1, source_target_pairs={{0,1},{1,2},{2,3},{4,5},{5,6},{6,7},{8,9},{9,10},{10,11},{12,13},{... | collective-permute-start | bytes 774152 | tf_op jit(solution)/shard_map/ppermute | solution.py:403
  36.7 4.9 %encode.2.refs_1_ = bf16[384,896]{1,0:T(8,128)(2,1)S(1)} custom-call(s32[2,4]{1,0:T(2,128)S(1)} %add_bitcast_fusion.refs_0_, s32[2,4]{1,0:T(2,128)S(1)} %bitcast.4, bf16[256,1792]{1,0:T(8,128)(2,1)S(1)} %copy-done.5, bf16[896,896]{1,0:T(8,128)(2,1)S(1)} %copy-done.3, bf16[8,64,896]{2,1,0:T(8,128)(2,1)S(1)} %copy-done.2, ...), custom_call_target="tpu_custom_call" | custom-call | flops 968884224 | bytes 6291456 | tf_op jit(solution)/shard_map/encode/pallas_call | solution.py:383
  41.6 0.8 %collective-permute-done.6.refs_3_ = bf16[144,896]{1,0:T(8,128)(2,1)S(1)} collective-permute-done((bf16[144,896]{1,0:T(8,128)(2,1)S(1)}, bf16[144,896]{1,0:T(8,128)(2,1)S(1)}, u32[]{:S(2)}, u32[]{:S(2)}) %collective-permute-start.6) | collective-permute-done | bytes 258080 | tf_op jit(solution)/shard_map/ppermute | solution.py:403
  42.4 4.3 %cross.3.refs_10_ = bf16[256,2048]{1,0:T(8,128)(2,1)S(1)} custom-call(s32[2,4]{1,0:T(2,128)S(1)} %bitcast.5, bf16[384,896]{1,0:T(8,128)(2,1)S(1)} %encode.2.refs_1_, bf16[144,896]{1,0:T(8,128)(2,1)S(1)} %encode.3.refs_2_, bf16[144,896]{1,0:T(8,128)(2,1)S(1)} %collective-permute-done.6.refs_3_, bf16[256,2048]{1,0:T(8,128)(2,1)S(1)} %copy-done.4, ...), custom_call_target="tpu_custom_call" | custom-call | flops 1509949440 | bytes 8388608 | tf_op jit(solution)/shard_map/cross/pallas_call | solution.py:407
  46.8 0.5 collective-permute-start.15
  47.3 1.6 %collective-permute-start.14 = (bf16[1344,128]{1,0:T(8,128)(2,1)S(1)}, bf16[1344,128]{1,0:T(8,128)(2,1)S(1)}, u32[]{:S(2)}, u32[]{:S(2)}) collective-permute-start(bf16[1344,128]{1,0:T(8,128)(2,1)S(1)} %slice.14), channel_id=1, source_target_pairs={{0,16},{1,17},{2,18},{3,19},{4,20},{5,21},{6,22},{7,23},{8,24},{9,... | collective-permute-start | bytes 1032200 | tf_op jit(solution)/shard_map/ppermute | solution.py:305
  48.9 1.1 %collective-permute-start.12 = (bf16[1344,128]{1,0:T(8,128)(2,1)S(1)}, bf16[1344,128]{1,0:T(8,128)(2,1)S(1)}, u32[]{:S(2)}, u32[]{:S(2)}) collective-permute-start(bf16[1344,128]{1,0:T(8,128)(2,1)S(1)} %slice.13), channel_id=1, source_target_pairs={{0,8},{1,9},{2,10},{3,11},{4,12},{5,13},{6,14},{7,15},{8,0},{9,1},... | collective-permute-start | bytes 1032200 | tf_op jit(solution)/shard_map/ppermute | solution.py:305
  50.0 7.6 %cross.4.refs_10_ = bf16[256,2048]{1,0:T(8,128)(2,1)S(1)} custom-call(s32[2,4]{1,0:T(2,128)S(1)} %bitcast.6, bf16[384,896]{1,0:T(8,128)(2,1)S(1)} %encode.2.refs_1_, bf16[144,896]{1,0:T(8,128)(2,1)S(1)} %encode.3.refs_2_, bf16[144,896]{1,0:T(8,128)(2,1)S(1)} %collective-permute-done.6.refs_3_, bf16[256,2048]{1,0:T(8,128)(2,1)S(1)} %copy-done.4, ...), custom_call_target="tpu_custom_call" | custom-call | flops 3019898880 | bytes 8388608 | tf_op jit(solution)/shard_map/cross/pallas_call | solution.py:407
  57.7 1.0 %collective-permute-done.12.refs_6_ = bf16[1344,128]{1,0:T(8,128)(2,1)S(1)} collective-permute-done((bf16[1344,128]{1,0:T(8,128)(2,1)S(1)}, bf16[1344,128]{1,0:T(8,128)(2,1)S(1)}, u32[]{:S(2)}, u32[]{:S(2)}) %collective-permute-start.12) | collective-permute-done | bytes 344096 | tf_op jit(solution)/shard_map/ppermute | solution.py:305
  58.7 0.6 collective-permute-done.18.refs_9_
  59.4 1.0 %collective-permute-done.17.refs_8_ = bf16[1344,128]{1,0:T(8,128)(2,1)S(1)} collective-permute-done((bf16[1344,128]{1,0:T(8,128)(2,1)S(1)}, bf16[1344,128]{1,0:T(8,128)(2,1)S(1)}, u32[]{:S(2)}, u32[]{:S(2)}) %collective-permute-start.17) | collective-permute-done | bytes 344096 | tf_op jit(solution)/shard_map/ppermute | solution.py:305
  60.4 5.3 %cross.5 = bf16[256,2048]{1,0:T(8,128)(2,1)} custom-call(s32[2,4]{1,0:T(2,128)S(1)} %bitcast.7, bf16[384,896]{1,0:T(8,128)(2,1)S(1)} %encode.2.refs_1_, bf16[144,896]{1,0:T(8,128)(2,1)S(1)} %encode.3.refs_2_, bf16[144,896]{1,0:T(8,128)(2,1)S(1)} %collective-permute-done.6.refs_3_, bf16[256,2048]{1,0:T(8,128)(2,1)S(1)} %copy-done.4, ...), custom_call_target="tpu_custom_call" | custom-call | flops 1509949440 | bytes 8388608 | tf_op jit(solution)/shard_map/cross/pallas_call | solution.py:407
  (34 shorter events, 0.4 us)
Async XLA Ops:
  0.0 30.6 %copy-start.6 = (s32[4,2]{0,1:T(2,128)S(1)}, s32[4,2]{0,1:T(2,128)}, u32[]{:S(2)}) copy-start(s32[4,2]{0,1:T(2,128)} %param.13) | copy-start | bytes 100
  1.0 15.3 %collective-permute-start.7 = (bf16[896,128]{1,0:T(8,128)(2,1)S(1)}, bf16[896,128]{1,0:T(8,128)(2,1)S(1)}, u32[]{:S(2)}, u32[]{:S(2)}) collective-permute-start(bf16[896,128]{1,0:T(8,128)(2,1)S(1)} %constant_dynamic-slice_fusion), channel_id=1, source_target_pairs={{0,3},{1,2},{2,1},{3,0},{4,7},{5,6},{6,5},{7,4},{8,11},{9,10},{10,... | collective-permute-start | bytes 688136 | tf_op jit(solution)/shard_map/ppermute | solution.py:305
  6.1 11.6 %collective-permute-start.8 = (bf16[896,128]{1,0:T(8,128)(2,1)S(1)}, bf16[896,128]{1,0:T(8,128)(2,1)S(1)}, u32[]{:S(2)}, u32[]{:S(2)}) collective-permute-start(bf16[896,128]{1,0:T(8,128)(2,1)S(1)} %constant_dynamic-slice_fusion), channel_id=1, source_target_pairs={{0,1},{1,0},{2,3},{3,2},{4,5},{5,4},{6,7},{7,6},{8,9},{9,8},{10,11... | collective-permute-start | bytes 688136 | tf_op jit(solution)/shard_map/ppermute | solution.py:305
  6.1 19.5 %collective-permute-start.9 = (bf16[896,128]{1,0:T(8,128)(2,1)S(1)}, bf16[896,128]{1,0:T(8,128)(2,1)S(1)}, u32[]{:S(2)}, u32[]{:S(2)}) collective-permute-start(bf16[896,128]{1,0:T(8,128)(2,1)S(1)} %constant_dynamic-slice_fusion), channel_id=1, source_target_pairs={{0,2},{1,3},{2,0},{3,1},{4,6},{5,7},{6,4},{7,5},{8,10},{9,11},{10,... | collective-permute-start | bytes 688136 | tf_op jit(solution)/shard_map/ppermute | solution.py:305
  7.4 1.7 %collective-permute-start = (s32[2,4]{1,0:T(2,128)S(1)}, s32[2,4]{1,0:T(2,128)S(1)}, u32[]{:S(2)}, u32[]{:S(2)}) collective-permute-start(s32[2,4]{1,0:T(2,128)S(1)} %add_bitcast_fusion.refs_0_), channel_id=1, source_target_pairs={{0,4},{4,0},{8,12},{12,8},{1,5},{5,1},{9,13},{13,9},{2,6},{6,2},{1... | collective-permute-start | bytes 104 | tf_op jit(solution)/shard_map/ppermute | solution.py:345
  7.4 3.6 %collective-permute-start.1 = (s32[2,4]{1,0:T(2,128)S(1)}, s32[2,4]{1,0:T(2,128)S(1)}, u32[]{:S(2)}, u32[]{:S(2)}) collective-permute-start(s32[2,4]{1,0:T(2,128)S(1)} %add_bitcast_fusion.refs_0_), channel_id=1, source_target_pairs={{0,8},{4,12},{8,0},{12,4},{1,9},{5,13},{9,1},{13,5},{2,10},{6,14},... | collective-permute-start | bytes 104 | tf_op jit(solution)/shard_map/ppermute | solution.py:345
  9.1 3.0 %collective-permute-start.2 = (s32[2,4]{1,0:T(2,128)S(1)}, s32[2,4]{1,0:T(2,128)S(1)}, u32[]{:S(2)}, u32[]{:S(2)}) collective-permute-start(s32[2,4]{1,0:T(2,128)S(1)} %add_bitcast_fusion.refs_0_), channel_id=1, source_target_pairs={{0,12},{4,8},{8,4},{12,0},{1,13},{5,9},{9,5},{13,1},{2,14},{6,10},... | collective-permute-start | bytes 104 | tf_op jit(solution)/shard_map/ppermute | solution.py:345
  12.1 1.2 %copy-start.1 = (bf16[8,64,896]{2,1,0:T(8,128)(2,1)S(1)}, bf16[8,64,896]{2,1,0:T(8,128)(2,1)}, u32[]{:S(2)}) copy-start(bf16[8,64,896]{2,1,0:T(8,128)(2,1)} %refs_4_.6) | copy-start | bytes 2752516
  13.3 17.4 %copy-start.2 = (bf16[8,64,896]{2,1,0:T(8,128)(2,1)S(1)}, bf16[8,64,896]{2,1,0:T(8,128)(2,1)}, u32[]{:S(2)}) copy-start(bf16[8,64,896]{2,1,0:T(8,128)(2,1)} %refs_4_.6) | copy-start | bytes 2752516
  13.3 17.4 %copy-start.3 = (bf16[896,896]{1,0:T(8,128)(2,1)S(1)}, bf16[896,896]{1,0:T(8,128)(2,1)}, u32[]{:S(2)}) copy-start(bf16[896,896]{1,0:T(8,128)(2,1)} %refs_3_.5) | copy-start | bytes 4816900
  15.1 13.8 %collective-permute-start.4 = (bf16[4,64,896]{2,1,0:T(8,128)(2,1)S(1)}, bf16[4,64,896]{2,1,0:T(8,128)(2,1)S(1)}, u32[]{:S(2)}, u32[]{:S(2)}) collective-permute-start(bf16[4,64,896]{2,1,0:T(8,128)(2,1)S(1)} %get-tuple-element.17), channel_id=1, source_target_pairs={{0,8},{1,9},{2,10},{3,11},{4,12},{5,13},{6,14},{7,15},{8,0},{9,1},... | collective-permute-start | bytes 1376264 | tf_op jit(solution)/shard_map/ppermute | solution.py:305
  25.7 16.0 %collective-permute-start.11 = (bf16[2688,128]{1,0:T(8,128)(2,1)S(1)}, bf16[2688,128]{1,0:T(8,128)(2,1)S(1)}, u32[]{:S(2)}, u32[]{:S(2)}) collective-permute-start(bf16[2688,128]{1,0:T(8,128)(2,1)S(1)} %constant_dynamic-update-slice_fusion.refs_6_), channel_id=1, source_target_pairs={{0,4},{1,5},{2,6},{3,7},{4,0},{5,1},{6,2},{7,3},{8,12},{9,13},{10,... | collective-permute-start | bytes 2064392 | tf_op jit(solution)/shard_map/ppermute | solution.py:305
  25.7 21.0 %collective-permute-start.13 = (bf16[2688,128]{1,0:T(8,128)(2,1)S(1)}, bf16[2688,128]{1,0:T(8,128)(2,1)S(1)}, u32[]{:S(2)}, u32[]{:S(2)}) collective-permute-start(bf16[2688,128]{1,0:T(8,128)(2,1)S(1)} %constant_dynamic-update-slice_fusion.refs_6_), channel_id=1, source_target_pairs={{0,8},{1,9},{2,10},{3,11},{4,12},{5,13},{6,14},{7,15},{8,0},{9,1},... | collective-permute-start | bytes 2064392 | tf_op jit(solution)/shard_map/ppermute | solution.py:305
  27.3 19.5 %collective-permute-start.10 = (bf16[2688,128]{1,0:T(8,128)(2,1)S(1)}, bf16[2688,128]{1,0:T(8,128)(2,1)S(1)}, u32[]{:S(2)}, u32[]{:S(2)}) collective-permute-start(bf16[2688,128]{1,0:T(8,128)(2,1)S(1)} %constant_dynamic-update-slice_fusion.refs_6_), channel_id=1, source_target_pairs={{0,16},{1,17},{2,18},{3,19},{4,20},{5,21},{6,22},{7,23},{8,24},{9,... | collective-permute-start | bytes 2064392 | tf_op jit(solution)/shard_map/ppermute | solution.py:305
  28.8 1.5 %collective-permute-start.3 = (bf16[2,64,896]{2,1,0:T(8,128)(2,1)S(1)}, bf16[2,64,896]{2,1,0:T(8,128)(2,1)S(1)}, u32[]{:S(2)}, u32[]{:S(2)}) collective-permute-start(bf16[2,64,896]{2,1,0:T(8,128)(2,1)S(1)} %get-tuple-element.16), channel_id=1, source_target_pairs={{0,4},{1,5},{2,6},{3,7},{4,0},{5,1},{6,2},{7,3},{8,12},{9,13},{10,... | collective-permute-start | bytes 688136 | tf_op jit(solution)/shard_map/ppermute | solution.py:305
  28.8 1.8 %collective-permute-start.5 = (bf16[2,64,896]{2,1,0:T(8,128)(2,1)S(1)}, bf16[2,64,896]{2,1,0:T(8,128)(2,1)S(1)}, u32[]{:S(2)}, u32[]{:S(2)}) collective-permute-start(bf16[2,64,896]{2,1,0:T(8,128)(2,1)S(1)} %slice.12), channel_id=1, source_target_pairs={{0,4},{1,5},{2,6},{3,7},{4,0},{5,1},{6,2},{7,3},{8,12},{9,13},{10,... | collective-permute-start | bytes 688136 | tf_op jit(solution)/shard_map/ppermute | solution.py:305
  30.6 1.2 %copy-start.5 = (bf16[256,1792]{1,0:T(8,128)(2,1)S(1)}, bf16[256,1792]{1,0:T(8,128)(2,1)}, u32[]{:S(2)}) copy-start(bf16[256,1792]{1,0:T(8,128)(2,1)} %refs_2_.3) | copy-start | bytes 2752516
  33.9 8.6 %copy-start = (bf16[896,1024]{1,0:T(8,128)(2,1)S(1)}, bf16[896,1024]{1,0:T(8,128)(2,1)}, u32[]{:S(2)}) copy-start(bf16[896,1024]{1,0:T(8,128)(2,1)} %refs_5_.5) | copy-start | bytes 5505028
  33.9 8.6 %copy-start.4 = (bf16[256,2048]{1,0:T(8,128)(2,1)S(1)}, bf16[256,2048]{1,0:T(8,128)(2,1)}, u32[]{:S(2)}) copy-start(bf16[256,2048]{1,0:T(8,128)(2,1)} %refs_4_.9) | copy-start | bytes 3145732
  33.9 8.6 %collective-permute-start.6 = (bf16[144,896]{1,0:T(8,128)(2,1)S(1)}, bf16[144,896]{1,0:T(8,128)(2,1)S(1)}, u32[]{:S(2)}, u32[]{:S(2)}) collective-permute-start(bf16[144,896]{1,0:T(8,128)(2,1)S(1)} %encode.3.refs_2_), channel_id=1, source_target_pairs={{0,1},{1,2},{2,3},{4,5},{5,6},{6,7},{8,9},{9,10},{10,11},{12,13},{... | collective-permute-start | bytes 774152 | tf_op jit(solution)/shard_map/ppermute | solution.py:403
  46.7 3.3 %collective-permute-start.16 = (bf16[2688,128]{1,0:T(8,128)(2,1)S(1)}, bf16[2688,128]{1,0:T(8,128)(2,1)S(1)}, u32[]{:S(2)}, u32[]{:S(2)}) collective-permute-start(bf16[2688,128]{1,0:T(8,128)(2,1)S(1)} %collective-permute-done.13.refs_7_), channel_id=1, source_target_pairs={{0,4},{1,5},{2,6},{3,7},{4,0},{5,1},{6,2},{7,3},{8,12},{9,13},{10,... | collective-permute-start | bytes 2064392 | tf_op jit(solution)/shard_map/ppermute | solution.py:305
  46.8 3.2 %collective-permute-start.15 = (bf16[2688,128]{1,0:T(8,128)(2,1)S(1)}, bf16[2688,128]{1,0:T(8,128)(2,1)S(1)}, u32[]{:S(2)}, u32[]{:S(2)}) collective-permute-start(bf16[2688,128]{1,0:T(8,128)(2,1)S(1)} %collective-permute-done.10.refs_6_), channel_id=1, source_target_pairs={{0,4},{1,5},{2,6},{3,7},{4,0},{5,1},{6,2},{7,3},{8,12},{9,13},{10,... | collective-permute-start | bytes 2064392 | tf_op jit(solution)/shard_map/ppermute | solution.py:305
  47.3 10.4 %collective-permute-start.14 = (bf16[1344,128]{1,0:T(8,128)(2,1)S(1)}, bf16[1344,128]{1,0:T(8,128)(2,1)S(1)}, u32[]{:S(2)}, u32[]{:S(2)}) collective-permute-start(bf16[1344,128]{1,0:T(8,128)(2,1)S(1)} %slice.14), channel_id=1, source_target_pairs={{0,16},{1,17},{2,18},{3,19},{4,20},{5,21},{6,22},{7,23},{8,24},{9,... | collective-permute-start | bytes 1032200 | tf_op jit(solution)/shard_map/ppermute | solution.py:305
  48.9 9.8 %collective-permute-start.12 = (bf16[1344,128]{1,0:T(8,128)(2,1)S(1)}, bf16[1344,128]{1,0:T(8,128)(2,1)S(1)}, u32[]{:S(2)}, u32[]{:S(2)}) collective-permute-start(bf16[1344,128]{1,0:T(8,128)(2,1)S(1)} %slice.13), channel_id=1, source_target_pairs={{0,8},{1,9},{2,10},{3,11},{4,12},{5,13},{6,14},{7,15},{8,0},{9,1},... | collective-permute-start | bytes 1032200 | tf_op jit(solution)/shard_map/ppermute | solution.py:305
  57.7 1.7 %collective-permute-start.18 = (bf16[1344,128]{1,0:T(8,128)(2,1)S(1)}, bf16[1344,128]{1,0:T(8,128)(2,1)S(1)}, u32[]{:S(2)}, u32[]{:S(2)}) collective-permute-start(bf16[1344,128]{1,0:T(8,128)(2,1)S(1)} %collective-permute-done.14.refs_7_), channel_id=1, source_target_pairs={{0,4},{1,5},{2,6},{3,7},{4,0},{5,1},{6,2},{7,3},{8,12},{9,13},{10,... | collective-permute-start | bytes 1032200 | tf_op jit(solution)/shard_map/ppermute | solution.py:305
  58.7 1.7 %collective-permute-start.17 = (bf16[1344,128]{1,0:T(8,128)(2,1)S(1)}, bf16[1344,128]{1,0:T(8,128)(2,1)S(1)}, u32[]{:S(2)}, u32[]{:S(2)}) collective-permute-start(bf16[1344,128]{1,0:T(8,128)(2,1)S(1)} %collective-permute-done.12.refs_6_), channel_id=1, source_target_pairs={{0,4},{1,5},{2,6},{3,7},{4,0},{5,1},{6,2},{7,3},{8,12},{9,13},{10,... | collective-permute-start | bytes 1032200 | tf_op jit(solution)/shard_map/ppermute | solution.py:305

commit v4 on v3

--- a/solution.py
+++ b/solution.py
@@ -21,7 +21,8 @@
 LANES = 128
 FLAG_ROWS = 16
 EDGE = 16
-PAIRS_AT_ONCE = 2
+PAIRS_AT_ONCE = 7
+HEADS_AT_ONCE = 4
 DISTANCES = (3, 1, 2)
 
 MASKED_SCORE = -1e30
@@ -189,28 +190,28 @@
             [prior_ref[:KEYS, :], encoded_ref[...], last_ref[:KEYS, :]], axis=0
         )
         states = dot(rows, weights).astype(jnp.bfloat16)
-        return [states[b * KEYS : (b + 1) * KEYS] for b in range(blocks + 1)]
-
-    states = project(items[0][2])
-    for n, (columns, target, _) in enumerate(items):
-        scores, values = [], []
-        for (start, stop), state, flag in zip(ranges, states, flags):
-            left, right = state[:, :CROSS_HEAD], state[:, CROSS_HEAD:]
-            if swap is not None:
-                left, right = jnp.where(swap, right, left), jnp.where(swap, left, right)
-            score = dot(queries_ref[start:stop, columns], left, NT) * scale
-            scores.append(jnp.where(flag, score, MASKED_SCORE))
-            values.append(right)
-        scores = jnp.concatenate(scores, axis=0)
-        if n + 1 < len(items):
-            states = project(items[n + 1][2])
+        left, right = states[:, :CROSS_HEAD], states[:, CROSS_HEAD:]
+        if swap is None:
+            return left, right
+        return jnp.where(swap, right, left), jnp.where(swap, left, right)
+
+    def scores_of(columns, keys):
+        scores = []
+        for u, (start, stop) in enumerate(ranges):
+            score = dot(queries_ref[start:stop, columns], keys[u * KEYS : (u + 1) * KEYS], NT)
+            scores.append(jnp.where(flags[u], score * scale, MASKED_SCORE))
+        return jnp.concatenate(scores, axis=0)
+
+    def softmax(scores):
         weights = jnp.exp(scores - jnp.max(scores, axis=1, keepdims=True))
         weights = weights * (1.0 / jnp.sum(weights, axis=1, keepdims=True))
-        weights = weights.astype(jnp.bfloat16)
+        return weights.astype(jnp.bfloat16)
+
+    def finish(weights, values, target):
         at, tail = 0, None
         for u, (start, stop) in enumerate(ranges):
             part = weights[at : at + stop - start]
-            result = dot(part, values[u]).astype(jnp.bfloat16)
+            result = dot(part, values[u * KEYS : (u + 1) * KEYS]).astype(jnp.bfloat16)
             at += stop - start
             if u == 0:
                 result = jnp.where(span > 0, result, jnp.zeros_like(result))
@@ -222,6 +223,16 @@
                 out_ref[start : stop - EDGE, target] = result[: stop - EDGE - start]
                 tail = result[stop - EDGE - start :]
 
+    groups = [items[at : at + HEADS_AT_ONCE] for at in range(0, len(items), HEADS_AT_ONCE)]
+    states = [project(load) for _, _, load in groups[0]]
+    for n, group in enumerate(groups):
+        scores = [scores_of(columns, keys) for (columns, _, _), (keys, _) in zip(group, states)]
+        ahead = [project(load) for _, _, load in groups[n + 1]] if n + 1 < len(groups) else None
+        weights = [softmax(score) for score in scores]
+        for weight, (_, values), (_, target, _) in zip(weights, states, group):
+            finish(weight, values, target)
+        states = ahead
+
 
 def head_columns(head):
     if isinstance(head, int):
@@ -254,27 +265,27 @@
 
 
 def pieces_kernel(offsets, resumed, blocks, *refs):
+    core = lax.axis_index("cache") % 2
     lengths_ref, encoded_ref, last_ref, prior_ref, queries_ref, weight_ref = refs[:6]
     out_ref = refs[-1]
     groups = refs[6:-1]
     if resumed:
         out_ref[...] = groups[-1][...]
         groups = groups[:-1]
-    share = len(groups) // len(offsets)
 
     def piece(held, distance):
         start = DISTANCES.index(distance) * ENCODER_WIDTH
-        stop = start + ENCODER_WIDTH
-        parts = []
-        for ref in held:
-            rows = ref.shape[0]
-            if start < rows and stop > 0:
-                parts.append(ref[max(start, 0) : min(stop, rows), :])
-            start, stop = start - rows, stop - rows
-        return parts[0] if len(parts) == 1 else jnp.concatenate(parts, axis=0)
+        return held[start : start + ENCODER_WIDTH, :]
 
     def item(offset, held, own):
-        column = offset ^ place_of()
+        first_hop, second_hop, crossed = offset
+        origin = core ^ 1 if crossed else core
+        near = jnp.where(origin == 0, 4, 2)
+        column = place_of() ^ int(crossed)
+        if first_hop:
+            column = column ^ near
+        if second_hop:
+            column = column ^ (6 - near)
 
         def load():
             if own:
@@ -285,8 +296,7 @@
         return columns, columns, load
 
     items = []
-    for n, offset in enumerate(offsets):
-        held = groups[n * share : (n + 1) * share]
+    for offset, held in zip(offsets, groups):
         items += [item(offset, held, False), item(offset, held, True)]
     swap = lax.axis_index("span") >= 2
     cross_heads(
@@ -305,12 +315,16 @@
     return lax.ppermute(value, AXES, pairs)
 
 
-def over_x(value):
-    return permute(value, lambda g, c, s: (g ^ 1, c, s))
-
-
 def over_y(value):
     return permute(value, lambda g, c, s: (g, c ^ 2, s))
+
+
+def over_first(value):
+    return permute(value, lambda g, c, s: (g, c ^ 2, s) if c % 2 else (g ^ 1, c, s))
+
+
+def over_second(value):
+    return permute(value, lambda g, c, s: (g ^ 1, c, s) if c % 2 else (g, c ^ 2, s))
 
 
 def over_core(value):
@@ -374,7 +388,8 @@
         beside = over_y(fetched[1])
         arrived = [over_core(fetched[0]), beside, over_core(beside[capacity:])]
         pieces = jnp.concatenate([after(v, fetched[0]) for v in pieces], axis=0)
-        x_pieces, y_pieces = over_x(pieces), over_y(pieces)
+        first_hop = over_first(pieces)
+        second_hop = over_second(pieces)
     else:
         arrived = [swap(v, r) for r, v in enumerate(fetched, 1)]
 
@@ -401,6 +416,7 @@
 
     last = encode(range(blocks - 1, blocks), FLAG_ROWS)
     prior = lax.ppermute(last, "span", [(i, i + 1) for i in range(spans - 1)])
+    ids = after(ids, last)
     encoded = encode(range(blocks - 1), 0)
 
     def cross(kernel, heads, *operands):
@@ -425,18 +441,21 @@
         kernel = functools.partial(pieces_kernel, offsets, bool(done))
         return [cross(kernel, 2 * len(offsets), cross_weight, *operands, *done)]
 
-    done = part([], (0, 1), pieces, over_core(pieces))
-    middle = pieces.shape[0] // 2
-    hop = [over_y(after(x_pieces[:middle], *done)), over_x(after(y_pieces[middle:], *done))]
+    both_hops = over_second(after(first_hop, encoded))
+    near = [pieces, first_hop, second_hop]
+    hops = ((False, False), (True, False), (False, True))
     done = part(
+        [],
+        [(*hop, crossed) for crossed in (False, True) for hop in hops],
+        *near,
+        *[over_core(after(v, encoded, prior)) for v in near],
+    )
+    return part(
         done,
-        (4, 2, 5, 3),
-        x_pieces,
-        y_pieces,
-        *[over_core(after(v, *done)) for v in (x_pieces, y_pieces)],
-    )
-    hop += [over_core(after(v, *done)) for v in hop]
-    return part(done, (6, 7), *hop)[0]
+        [(True, True, False), (True, True, True)],
+        both_hops,
+        over_core(after(both_hops, *done)),
+    )[0]
 
 
 def solution(mesh):

time: 65.9 us -> 61.2 us (0.929)
  Pallas kernels: 25.9 us -> 18.1 us
  waiting for transfers between devices: 16.1 us -> 20.3 us
  starting transfers between devices: 19.4 us -> 18.2 us
    pallas_call x3 -> x2, Pallas kernels: 17.2 us -> 10.5 us  [cross(): pl.pallas_call(functools.partial(kernel, blocks), out_shape=jax.ShapeDtyp...]
    ppermute x15 -> x13, waiting for transfers between devices: 13.2 us -> 18.2 us  [permute(): return lax.ppermute(value, AXES, pairs)]
    ppermute x15 -> x13, starting transfers between devices: 14 us -> 12.7 us  [permute(): return lax.ppermute(value, AXES, pairs)]
    pallas_call x2, Pallas kernels: 6.93 us -> 5.86 us  [encode(): pl.pallas_call(functools.partial(encode_kernel, peers, capacity, cache_sl...]
    ppermute x1, waiting for transfers between devices: 0.82 us -> 0.01 us  [per_device(): prior = lax.ppermute(last, 'span', [(i, i + 1) for i in range(spans - 1)])]
  transfers between devices with their start and end apart: 19 -> 17, of which waited for: 10 -> 11; matrix products, arithmetic and copies ran while one was open for 1% -> 1% of each run, Pallas kernels for 31% -> 24%
where the time goes in v4:
time: 61.2 us; the launch traced here: 60.9 us
  waiting for transfers between devices  20.3 us (33%)
  starting transfers between devices  18.2 us (30%)
  Pallas kernels  18.1 us (30%)
  local copies, waits for them, and re-layouts  3.44 us (6%)
  other arithmetic  0.7 us (1%)
    ppermute x13, waiting for transfers between devices, permute(): return lax.ppermute(value, AXES, pairs)  18.2 us
    ppermute x13, starting transfers between devices, permute(): return lax.ppermute(value, AXES, pairs)  12.7 us
    pallas_call x2, Pallas kernels, cross(): pl.pallas_call(functools.partial(kernel, blocks), out_shape=jax.ShapeDtyp...  10.5 us
    pallas_call x2, Pallas kernels, encode(): pl.pallas_call(functools.partial(encode_kernel, peers, capacity, cache_sl...  5.86 us
    ppermute x1, starting transfers between devices, per_device(): prior = lax.ppermute(last, 'span', [(i, i + 1) for i in range(spans - 1)])  2.89 us
    ppermute x3, starting transfers between devices, per_device(): lax.ppermute(v, 'cache', [(i, i ^ r) for i in range(peers)])  2.59 us
    unnamed x16, local copies, waits for them, and re-layouts  2.42 us
    ppermute x3, waiting for transfers between devices, per_device(): lax.ppermute(v, 'cache', [(i, i ^ r) for i in range(peers)])  2.07 us
  transfers between devices with their start and end apart: 17, of which 11 were waited for; matrix products, arithmetic and copies ran while one was open for 1% of the time, Pallas kernels for 24%

profile of v4, /device:TPU:0, one launch (start us, length us, event | category | flops | bytes accessed | tf_op | source)
XLA Modules:
  0.0 60.9 jit_solution(5628680730578175377)
XLA Ops:
  0.0 1.0 %constant_dynamic-slice_fusion = bf16[896,128]{1,0:T(8,128)(2,1)S(1)} fusion(bf16[896,1024]{1,0:T(8,128)(2,1)} %refs_5_.3, s32[]{:T(128)S(6)} %select_n.3), kind=kLoop, calls=%fused_computation.4 | loop fusion | bytes 458756 | tf_op jit(solution)/shard_map/dynamic_slice | solution.py:339
  1.0 5.1 %collective-permute-start.7 = (bf16[896,128]{1,0:T(8,128)(2,1)S(1)}, bf16[896,128]{1,0:T(8,128)(2,1)S(1)}, u32[]{:S(2)}, u32[]{:S(2)}) collective-permute-start(bf16[896,128]{1,0:T(8,128)(2,1)S(1)} %constant_dynamic-slice_fusion), channel_id=1, source_target_pairs={{0,3},{1,2},{2,1},{3,0},{4,7},{5,6},{6,5},{7,4},{8,11},{9,10},{10,... | collective-permute-start | bytes 688136 | tf_op jit(solution)/shard_map/ppermute | solution.py:315
  6.1 0.6 %collective-permute-start.9 = (bf16[896,128]{1,0:T(8,128)(2,1)S(1)}, bf16[896,128]{1,0:T(8,128)(2,1)S(1)}, u32[]{:S(2)}, u32[]{:S(2)}) collective-permute-start(bf16[896,128]{1,0:T(8,128)(2,1)S(1)} %constant_dynamic-slice_fusion), channel_id=1, source_target_pairs={{0,2},{1,3},{2,0},{3,1},{4,6},{5,7},{6,4},{7,5},{8,10},{9,11},{10,... | collective-permute-start | bytes 688136 | tf_op jit(solution)/shard_map/ppermute | solution.py:315
  6.7 0.7 %add_bitcast_fusion.refs_0_ = s32[2,4]{1,0:T(2,128)S(1)} fusion(s32[4,2]{0,1:T(2,128)} %param.12, s32[4,2]{0,1:T(2,128)} %param.11), kind=kLoop, calls=%fused_computation.3 | loop fusion | flops 16 | bytes 96 | tf_op jit(solution)/shard_map/add | solution.py:362
  7.4 1.7 %collective-permute-start.1 = (s32[2,4]{1,0:T(2,128)S(1)}, s32[2,4]{1,0:T(2,128)S(1)}, u32[]{:S(2)}, u32[]{:S(2)}) collective-permute-start(s32[2,4]{1,0:T(2,128)S(1)} %add_bitcast_fusion.refs_0_), channel_id=1, source_target_pairs={{0,8},{4,12},{8,0},{12,4},{1,9},{5,13},{9,1},{13,5},{2,10},{6,14},... | collective-permute-start | bytes 104 | tf_op jit(solution)/shard_map/ppermute | solution.py:359
  9.1 0.9 %collective-permute-start.2 = (s32[2,4]{1,0:T(2,128)S(1)}, s32[2,4]{1,0:T(2,128)S(1)}, u32[]{:S(2)}, u32[]{:S(2)}) collective-permute-start(s32[2,4]{1,0:T(2,128)S(1)} %add_bitcast_fusion.refs_0_), channel_id=1, source_target_pairs={{0,12},{4,8},{8,4},{12,0},{1,13},{5,9},{9,5},{13,1},{2,14},{6,10},... | collective-permute-start | bytes 104 | tf_op jit(solution)/shard_map/ppermute | solution.py:359
  10.0 1.0 %collective-permute-done.1.refs_1_ = s32[2,4]{1,0:T(2,128)S(1)} collective-permute-done((s32[2,4]{1,0:T(2,128)S(1)}, s32[2,4]{1,0:T(2,128)S(1)}, u32[]{:S(2)}, u32[]{:S(2)}) %collective-permute-start.1) | collective-permute-done | bytes 64 | tf_op jit(solution)/shard_map/ppermute | solution.py:359
  11.0 1.1 %collective-permute-done.2.refs_2_ = s32[2,4]{1,0:T(2,128)S(1)} collective-permute-done((s32[2,4]{1,0:T(2,128)S(1)}, s32[2,4]{1,0:T(2,128)S(1)}, u32[]{:S(2)}, u32[]{:S(2)}) %collective-permute-start.2) | collective-permute-done | bytes 64 | tf_op jit(solution)/shard_map/ppermute | solution.py:359
  12.1 1.2 %copy-done = bf16[8,64,896]{2,1,0:T(8,128)(2,1)S(1)} copy-done((bf16[8,64,896]{2,1,0:T(8,128)(2,1)S(1)}, bf16[8,64,896]{2,1,0:T(8,128)(2,1)}, u32[]{:S(2)}) %copy-start) | copy-done | bytes 917528
  13.3 1.8 %fetch.1 = (bf16[2,64,896]{2,1,0:T(8,128)(2,1)S(1)}, bf16[4,64,896]{2,1,0:T(8,128)(2,1)S(1)}) custom-call(s32[2,4]{1,0:T(2,128)S(1)} %collective-permute-done.refs_0_, s32[2,4]{1,0:T(2,128)S(1)} %collective-permute-done.1.refs_1_, s32[2,4]{1,0:T(2,128)S(1)} %collective-permute-done.2.refs_2_, bf16[8,64,896]{2,1,0:T(8,128)(2,1)S(1)} %copy-done), custom_call_target="tpu_custom_call" | custom-call | tf_op jit(solution)/shard_map/fetch/pallas_call | solution.py:371
  15.1 1.2 %collective-permute-start.4 = (bf16[4,64,896]{2,1,0:T(8,128)(2,1)S(1)}, bf16[4,64,896]{2,1,0:T(8,128)(2,1)S(1)}, u32[]{:S(2)}, u32[]{:S(2)}) collective-permute-start(bf16[4,64,896]{2,1,0:T(8,128)(2,1)S(1)} %get-tuple-element.17), channel_id=1, source_target_pairs={{0,8},{1,9},{2,10},{3,11},{4,12},{5,13},{6,14},{7,15},{8,0},{9,1},... | collective-permute-start | bytes 1376264 | tf_op jit(solution)/shard_map/ppermute | solution.py:315
  16.3 1.4 %collective-permute-done.8 = bf16[896,128]{1,0:T(8,128)(2,1)S(1)} collective-permute-done((bf16[896,128]{1,0:T(8,128)(2,1)S(1)}, bf16[896,128]{1,0:T(8,128)(2,1)S(1)}, u32[]{:S(2)}, u32[]{:S(2)}) %collective-permute-start.8) | collective-permute-done | bytes 229408 | tf_op jit(solution)/shard_map/ppermute | solution.py:315
  17.7 7.9 %collective-permute-done.9 = bf16[896,128]{1,0:T(8,128)(2,1)S(1)} collective-permute-done((bf16[896,128]{1,0:T(8,128)(2,1)S(1)}, bf16[896,128]{1,0:T(8,128)(2,1)S(1)}, u32[]{:S(2)}, u32[]{:S(2)}) %collective-permute-start.9) | collective-permute-done | bytes 229408 | tf_op jit(solution)/shard_map/ppermute | solution.py:315
  25.7 1.6 %collective-permute-start.12 = (bf16[2688,128]{1,0:T(8,128)(2,1)S(1)}, bf16[2688,128]{1,0:T(8,128)(2,1)S(1)}, u32[]{:S(2)}, u32[]{:S(2)}) collective-permute-start(bf16[2688,128]{1,0:T(8,128)(2,1)S(1)} %constant_dynamic-update-slice_fusion.refs_6_), channel_id=1, source_target_pairs={{0,8},{1,9},{2,10},{3,11},{4,20},{5,21},{6,22},{7,23},{8,0},{9,1},... | collective-permute-start | bytes 2064392 | tf_op jit(solution)/shard_map/ppermute | solution.py:315
  27.3 1.5 %collective-permute-start.10 = (bf16[2688,128]{1,0:T(8,128)(2,1)S(1)}, bf16[2688,128]{1,0:T(8,128)(2,1)S(1)}, u32[]{:S(2)}, u32[]{:S(2)}) collective-permute-start(bf16[2688,128]{1,0:T(8,128)(2,1)S(1)} %constant_dynamic-update-slice_fusion.refs_6_), channel_id=1, source_target_pairs={{0,16},{1,17},{2,18},{3,19},{4,12},{5,13},{6,14},{7,15},{8,24},{9,... | collective-permute-start | bytes 2064392 | tf_op jit(solution)/shard_map/ppermute | solution.py:315
  28.8 0.6 collective-permute-start.5
  29.3 0.9 %collective-permute-done.3.refs_5_ = bf16[2,64,896]{2,1,0:T(8,128)(2,1)S(1)} collective-permute-done((bf16[2,64,896]{2,1,0:T(8,128)(2,1)S(1)}, bf16[2,64,896]{2,1,0:T(8,128)(2,1)S(1)}, u32[]{:S(2)}, u32[]{:S(2)}) %collective-permute-start.3) | collective-permute-done | bytes 229408 | tf_op jit(solution)/shard_map/ppermute | solution.py:315
  30.2 0.3 collective-permute-done.5.refs_7_
  30.6 1.2 %copy-done.3 = bf16[256,1792]{1,0:T(8,128)(2,1)S(1)} copy-done((bf16[256,1792]{1,0:T(8,128)(2,1)S(1)}, bf16[256,1792]{1,0:T(8,128)(2,1)}, u32[]{:S(2)}) %copy-start.3) | copy-done | bytes 917528
  31.8 1.9 %encode.2.refs_2_ = bf16[144,896]{1,0:T(8,128)(2,1)S(1)} custom-call(s32[2,4]{1,0:T(2,128)S(1)} %add_bitcast_fusion.refs_0_, s32[2,4]{1,0:T(2,128)S(1)} %bitcast.3, bf16[256,1792]{1,0:T(8,128)(2,1)S(1)} %copy-done.3, bf16[896,896]{1,0:T(8,128)(2,1)S(1)} %copy-done.2, bf16[8,64,896]{2,1,0:T(8,128)(2,1)S(1)} %copy-done.1, ...), custom_call_target="tpu_custom_call" | custom-call | flops 322961408 | bytes 2097152 | tf_op jit(solution)/shard_map/encode/pallas_call | solution.py:398
  33.7 2.9 %collective-permute-start.6 = (bf16[144,896]{1,0:T(8,128)(2,1)S(1)}, bf16[144,896]{1,0:T(8,128)(2,1)S(1)}, u32[]{:S(2)}, u32[]{:S(2)}) collective-permute-start(bf16[144,896]{1,0:T(8,128)(2,1)S(1)} %encode.2.refs_2_), channel_id=1, source_target_pairs={{0,1},{1,2},{2,3},{4,5},{5,6},{6,7},{8,9},{9,10},{10,11},{12,13},{... | collective-permute-start | bytes 774152 | tf_op jit(solution)/shard_map/ppermute | solution.py:418
  36.6 4.0 %encode.3.refs_1_ = bf16[384,896]{1,0:T(8,128)(2,1)S(1)} custom-call(s32[2,4]{1,0:T(2,128)S(1)} %add_bitcast_fusion.refs_0_, s32[2,4]{1,0:T(2,128)S(1)} %bitcast.4, bf16[256,1792]{1,0:T(8,128)(2,1)S(1)} %copy-done.3, bf16[896,896]{1,0:T(8,128)(2,1)S(1)} %copy-done.2, bf16[8,64,896]{2,1,0:T(8,128)(2,1)S(1)} %copy-done.1, ...), custom_call_target="tpu_custom_call" | custom-call | flops 968884224 | bytes 6291456 | tf_op jit(solution)/shard_map/encode/pallas_call | solution.py:398
  40.5 2.9 %collective-permute-done.12.refs_8_ = bf16[2688,128]{1,0:T(8,128)(2,1)S(1)} collective-permute-done((bf16[2688,128]{1,0:T(8,128)(2,1)S(1)}, bf16[2688,128]{1,0:T(8,128)(2,1)S(1)}, u32[]{:S(2)}, u32[]{:S(2)}) %collective-permute-start.12) | collective-permute-done | bytes 688160 | tf_op jit(solution)/shard_map/ppermute | solution.py:315
  43.4 0.5 collective-permute-start.14
  43.9 0.1 collective-permute-start.13
  44.0 1.5 %collective-permute-start.11 = (bf16[2688,128]{1,0:T(8,128)(2,1)S(1)}, bf16[2688,128]{1,0:T(8,128)(2,1)S(1)}, u32[]{:S(2)}, u32[]{:S(2)}) collective-permute-start(bf16[2688,128]{1,0:T(8,128)(2,1)S(1)} %collective-permute-done.10.refs_7_), channel_id=1, source_target_pairs={{0,8},{1,9},{2,10},{3,11},{4,20},{5,21},{6,22},{7,23},{8,0},{9,1},... | collective-permute-start | bytes 2064392 | tf_op jit(solution)/shard_map/ppermute | solution.py:315
  45.6 1.0 %collective-permute-done.14.refs_10_ = bf16[2688,128]{1,0:T(8,128)(2,1)S(1)} collective-permute-done((bf16[2688,128]{1,0:T(8,128)(2,1)S(1)}, bf16[2688,128]{1,0:T(8,128)(2,1)S(1)}, u32[]{:S(2)}, u32[]{:S(2)}) %collective-permute-start.14) | collective-permute-done | bytes 688160 | tf_op jit(solution)/shard_map/ppermute | solution.py:315
  46.6 1.0 %collective-permute-done.13.refs_9_ = bf16[2688,128]{1,0:T(8,128)(2,1)S(1)} collective-permute-done((bf16[2688,128]{1,0:T(8,128)(2,1)S(1)}, bf16[2688,128]{1,0:T(8,128)(2,1)S(1)}, u32[]{:S(2)}, u32[]{:S(2)}) %collective-permute-start.13) | collective-permute-done | bytes 688160 | tf_op jit(solution)/shard_map/ppermute | solution.py:315
  47.6 6.7 %cross.2.refs_8_ = bf16[256,2048]{1,0:T(8,128)(2,1)S(1)} custom-call(s32[2,4]{1,0:T(2,128)S(1)} %bitcast.5, bf16[384,896]{1,0:T(8,128)(2,1)S(1)} %encode.3.refs_1_, bf16[144,896]{1,0:T(8,128)(2,1)S(1)} %encode.2.refs_2_, bf16[144,896]{1,0:T(8,128)(2,1)S(1)} %collective-permute-done.6.refs_3_, bf16[256,2048]{1,0:T(8,128)(2,1)S(1)} %copy-done.5, ...), custom_call_target="tpu_custom_call" | custom-call | flops 4529848320 | bytes 8388608 | tf_op jit(solution)/shard_map/cross/pallas_call | solution.py:423
  54.3 0.7 %collective-permute-done.11.refs_6_ = bf16[2688,128]{1,0:T(8,128)(2,1)S(1)} collective-permute-done((bf16[2688,128]{1,0:T(8,128)(2,1)S(1)}, bf16[2688,128]{1,0:T(8,128)(2,1)S(1)}, u32[]{:S(2)}, u32[]{:S(2)}) %collective-permute-start.11) | collective-permute-done | bytes 688160 | tf_op jit(solution)/shard_map/ppermute | solution.py:315
  55.0 2.1 %collective-permute-done.16.refs_7_ = bf16[2688,128]{1,0:T(8,128)(2,1)S(1)} collective-permute-done((bf16[2688,128]{1,0:T(8,128)(2,1)S(1)}, bf16[2688,128]{1,0:T(8,128)(2,1)S(1)}, u32[]{:S(2)}, u32[]{:S(2)}) %collective-permute-start.16) | collective-permute-done | bytes 688160 | tf_op jit(solution)/shard_map/ppermute | solution.py:315
  57.1 3.8 %cross.3 = bf16[256,2048]{1,0:T(8,128)(2,1)} custom-call(s32[2,4]{1,0:T(2,128)S(1)} %bitcast.6, bf16[384,896]{1,0:T(8,128)(2,1)S(1)} %encode.3.refs_1_, bf16[144,896]{1,0:T(8,128)(2,1)S(1)} %encode.2.refs_2_, bf16[144,896]{1,0:T(8,128)(2,1)S(1)} %collective-permute-done.6.refs_3_, bf16[256,2048]{1,0:T(8,128)(2,1)S(1)} %copy-done.5, ...), custom_call_target="tpu_custom_call" | custom-call | flops 1509949440 | bytes 8388608 | tf_op jit(solution)/shard_map/cross/pallas_call | solution.py:423
  (27 shorter events, 0.2 us)
Async XLA Ops:
  0.0 30.6 %copy-start.6 = (s32[4,2]{0,1:T(2,128)S(1)}, s32[4,2]{0,1:T(2,128)}, u32[]{:S(2)}) copy-start(s32[4,2]{0,1:T(2,128)} %param.13) | copy-start | bytes 100
  1.0 15.3 %collective-permute-start.7 = (bf16[896,128]{1,0:T(8,128)(2,1)S(1)}, bf16[896,128]{1,0:T(8,128)(2,1)S(1)}, u32[]{:S(2)}, u32[]{:S(2)}) collective-permute-start(bf16[896,128]{1,0:T(8,128)(2,1)S(1)} %constant_dynamic-slice_fusion), channel_id=1, source_target_pairs={{0,3},{1,2},{2,1},{3,0},{4,7},{5,6},{6,5},{7,4},{8,11},{9,10},{10,... | collective-permute-start | bytes 688136 | tf_op jit(solution)/shard_map/ppermute | solution.py:315
  6.1 11.6 %collective-permute-start.8 = (bf16[896,128]{1,0:T(8,128)(2,1)S(1)}, bf16[896,128]{1,0:T(8,128)(2,1)S(1)}, u32[]{:S(2)}, u32[]{:S(2)}) collective-permute-start(bf16[896,128]{1,0:T(8,128)(2,1)S(1)} %constant_dynamic-slice_fusion), channel_id=1, source_target_pairs={{0,1},{1,0},{2,3},{3,2},{4,5},{5,4},{6,7},{7,6},{8,9},{9,8},{10,11... | collective-permute-start | bytes 688136 | tf_op jit(solution)/shard_map/ppermute | solution.py:315
  6.1 19.5 %collective-permute-start.9 = (bf16[896,128]{1,0:T(8,128)(2,1)S(1)}, bf16[896,128]{1,0:T(8,128)(2,1)S(1)}, u32[]{:S(2)}, u32[]{:S(2)}) collective-permute-start(bf16[896,128]{1,0:T(8,128)(2,1)S(1)} %constant_dynamic-slice_fusion), channel_id=1, source_target_pairs={{0,2},{1,3},{2,0},{3,1},{4,6},{5,7},{6,4},{7,5},{8,10},{9,11},{10,... | collective-permute-start | bytes 688136 | tf_op jit(solution)/shard_map/ppermute | solution.py:315
  7.4 1.7 %collective-permute-start = (s32[2,4]{1,0:T(2,128)S(1)}, s32[2,4]{1,0:T(2,128)S(1)}, u32[]{:S(2)}, u32[]{:S(2)}) collective-permute-start(s32[2,4]{1,0:T(2,128)S(1)} %add_bitcast_fusion.refs_0_), channel_id=1, source_target_pairs={{0,4},{4,0},{8,12},{12,8},{1,5},{5,1},{9,13},{13,9},{2,6},{6,2},{1... | collective-permute-start | bytes 104 | tf_op jit(solution)/shard_map/ppermute | solution.py:359
  7.4 3.6 %collective-permute-start.1 = (s32[2,4]{1,0:T(2,128)S(1)}, s32[2,4]{1,0:T(2,128)S(1)}, u32[]{:S(2)}, u32[]{:S(2)}) collective-permute-start(s32[2,4]{1,0:T(2,128)S(1)} %add_bitcast_fusion.refs_0_), channel_id=1, source_target_pairs={{0,8},{4,12},{8,0},{12,4},{1,9},{5,13},{9,1},{13,5},{2,10},{6,14},... | collective-permute-start | bytes 104 | tf_op jit(solution)/shard_map/ppermute | solution.py:359
  9.1 3.0 %collective-permute-start.2 = (s32[2,4]{1,0:T(2,128)S(1)}, s32[2,4]{1,0:T(2,128)S(1)}, u32[]{:S(2)}, u32[]{:S(2)}) collective-permute-start(s32[2,4]{1,0:T(2,128)S(1)} %add_bitcast_fusion.refs_0_), channel_id=1, source_target_pairs={{0,12},{4,8},{8,4},{12,0},{1,13},{5,9},{9,5},{13,1},{2,14},{6,10},... | collective-permute-start | bytes 104 | tf_op jit(solution)/shard_map/ppermute | solution.py:359
  12.1 1.2 %copy-start = (bf16[8,64,896]{2,1,0:T(8,128)(2,1)S(1)}, bf16[8,64,896]{2,1,0:T(8,128)(2,1)}, u32[]{:S(2)}) copy-start(bf16[8,64,896]{2,1,0:T(8,128)(2,1)} %refs_4_.5) | copy-start | bytes 2752516
  13.3 17.3 %copy-start.1 = (bf16[8,64,896]{2,1,0:T(8,128)(2,1)S(1)}, bf16[8,64,896]{2,1,0:T(8,128)(2,1)}, u32[]{:S(2)}) copy-start(bf16[8,64,896]{2,1,0:T(8,128)(2,1)} %refs_4_.5) | copy-start | bytes 2752516
  13.3 17.3 %copy-start.2 = (bf16[896,896]{1,0:T(8,128)(2,1)S(1)}, bf16[896,896]{1,0:T(8,128)(2,1)}, u32[]{:S(2)}) copy-start(bf16[896,896]{1,0:T(8,128)(2,1)} %refs_3_.5) | copy-start | bytes 4816900
  15.1 13.7 %collective-permute-start.4 = (bf16[4,64,896]{2,1,0:T(8,128)(2,1)S(1)}, bf16[4,64,896]{2,1,0:T(8,128)(2,1)S(1)}, u32[]{:S(2)}, u32[]{:S(2)}) collective-permute-start(bf16[4,64,896]{2,1,0:T(8,128)(2,1)S(1)} %get-tuple-element.17), channel_id=1, source_target_pairs={{0,8},{1,9},{2,10},{3,11},{4,12},{5,13},{6,14},{7,15},{8,0},{9,1},... | collective-permute-start | bytes 1376264 | tf_op jit(solution)/shard_map/ppermute | solution.py:315
  25.7 17.8 %collective-permute-start.12 = (bf16[2688,128]{1,0:T(8,128)(2,1)S(1)}, bf16[2688,128]{1,0:T(8,128)(2,1)S(1)}, u32[]{:S(2)}, u32[]{:S(2)}) collective-permute-start(bf16[2688,128]{1,0:T(8,128)(2,1)S(1)} %constant_dynamic-update-slice_fusion.refs_6_), channel_id=1, source_target_pairs={{0,8},{1,9},{2,10},{3,11},{4,20},{5,21},{6,22},{7,23},{8,0},{9,1},... | collective-permute-start | bytes 2064392 | tf_op jit(solution)/shard_map/ppermute | solution.py:315
  27.3 16.2 %collective-permute-start.10 = (bf16[2688,128]{1,0:T(8,128)(2,1)S(1)}, bf16[2688,128]{1,0:T(8,128)(2,1)S(1)}, u32[]{:S(2)}, u32[]{:S(2)}) collective-permute-start(bf16[2688,128]{1,0:T(8,128)(2,1)S(1)} %constant_dynamic-update-slice_fusion.refs_6_), channel_id=1, source_target_pairs={{0,16},{1,17},{2,18},{3,19},{4,12},{5,13},{6,14},{7,15},{8,24},{9,... | collective-permute-start | bytes 2064392 | tf_op jit(solution)/shard_map/ppermute | solution.py:315
  28.7 1.5 %collective-permute-start.3 = (bf16[2,64,896]{2,1,0:T(8,128)(2,1)S(1)}, bf16[2,64,896]{2,1,0:T(8,128)(2,1)S(1)}, u32[]{:S(2)}, u32[]{:S(2)}) collective-permute-start(bf16[2,64,896]{2,1,0:T(8,128)(2,1)S(1)} %get-tuple-element.16), channel_id=1, source_target_pairs={{0,4},{1,5},{2,6},{3,7},{4,0},{5,1},{6,2},{7,3},{8,12},{9,13},{10,... | collective-permute-start | bytes 688136 | tf_op jit(solution)/shard_map/ppermute | solution.py:315
  28.8 1.8 %collective-permute-start.5 = (bf16[2,64,896]{2,1,0:T(8,128)(2,1)S(1)}, bf16[2,64,896]{2,1,0:T(8,128)(2,1)S(1)}, u32[]{:S(2)}, u32[]{:S(2)}) collective-permute-start(bf16[2,64,896]{2,1,0:T(8,128)(2,1)S(1)} %slice.4), channel_id=1, source_target_pairs={{0,4},{1,5},{2,6},{3,7},{4,0},{5,1},{6,2},{7,3},{8,12},{9,13},{10,... | collective-permute-start | bytes 688136 | tf_op jit(solution)/shard_map/ppermute | solution.py:315
  30.6 1.2 %copy-start.3 = (bf16[256,1792]{1,0:T(8,128)(2,1)S(1)}, bf16[256,1792]{1,0:T(8,128)(2,1)}, u32[]{:S(2)}) copy-start(bf16[256,1792]{1,0:T(8,128)(2,1)} %refs_2_.3) | copy-start | bytes 2752516
  33.6 13.9 %copy-start.4 = (bf16[896,1024]{1,0:T(8,128)(2,1)S(1)}, bf16[896,1024]{1,0:T(8,128)(2,1)}, u32[]{:S(2)}) copy-start(bf16[896,1024]{1,0:T(8,128)(2,1)} %refs_5_.3) | copy-start | bytes 5505028
  33.7 13.9 %copy-start.5 = (bf16[256,2048]{1,0:T(8,128)(2,1)S(1)}, bf16[256,2048]{1,0:T(8,128)(2,1)}, u32[]{:S(2)}) copy-start(bf16[256,2048]{1,0:T(8,128)(2,1)} %refs_4_.7) | copy-start | bytes 3145732
  33.7 9.8 %collective-permute-start.6 = (bf16[144,896]{1,0:T(8,128)(2,1)S(1)}, bf16[144,896]{1,0:T(8,128)(2,1)S(1)}, u32[]{:S(2)}, u32[]{:S(2)}) collective-permute-start(bf16[144,896]{1,0:T(8,128)(2,1)S(1)} %encode.2.refs_2_), channel_id=1, source_target_pairs={{0,1},{1,2},{2,3},{4,5},{5,6},{6,7},{8,9},{9,10},{10,11},{12,13},{... | collective-permute-start | bytes 774152 | tf_op jit(solution)/shard_map/ppermute | solution.py:418
  43.4 2.1 %collective-permute-start.15 = (bf16[2688,128]{1,0:T(8,128)(2,1)S(1)}, bf16[2688,128]{1,0:T(8,128)(2,1)S(1)}, u32[]{:S(2)}, u32[]{:S(2)}) collective-permute-start(bf16[2688,128]{1,0:T(8,128)(2,1)S(1)} %collective-permute-done.12.refs_8_), channel_id=1, source_target_pairs={{0,4},{1,5},{2,6},{3,7},{4,0},{5,1},{6,2},{7,3},{8,12},{9,13},{10,... | collective-permute-start | bytes 2064392 | tf_op jit(solution)/shard_map/ppermute | solution.py:315
  43.4 3.1 %collective-permute-start.14 = (bf16[2688,128]{1,0:T(8,128)(2,1)S(1)}, bf16[2688,128]{1,0:T(8,128)(2,1)S(1)}, u32[]{:S(2)}, u32[]{:S(2)}) collective-permute-start(bf16[2688,128]{1,0:T(8,128)(2,1)S(1)} %collective-permute-done.10.refs_7_), channel_id=1, source_target_pairs={{0,4},{1,5},{2,6},{3,7},{4,0},{5,1},{6,2},{7,3},{8,12},{9,13},{10,... | collective-permute-start | bytes 2064392 | tf_op jit(solution)/shard_map/ppermute | solution.py:315
  43.9 3.6 %collective-permute-start.13 = (bf16[2688,128]{1,0:T(8,128)(2,1)S(1)}, bf16[2688,128]{1,0:T(8,128)(2,1)S(1)}, u32[]{:S(2)}, u32[]{:S(2)}) collective-permute-start(bf16[2688,128]{1,0:T(8,128)(2,1)S(1)} %constant_dynamic-update-slice_fusion.refs_6_), channel_id=1, source_target_pairs={{0,4},{1,5},{2,6},{3,7},{4,0},{5,1},{6,2},{7,3},{8,12},{9,13},{10,... | collective-permute-start | bytes 2064392 | tf_op jit(solution)/shard_map/ppermute | solution.py:315
  44.0 10.9 %collective-permute-start.11 = (bf16[2688,128]{1,0:T(8,128)(2,1)S(1)}, bf16[2688,128]{1,0:T(8,128)(2,1)S(1)}, u32[]{:S(2)}, u32[]{:S(2)}) collective-permute-start(bf16[2688,128]{1,0:T(8,128)(2,1)S(1)} %collective-permute-done.10.refs_7_), channel_id=1, source_target_pairs={{0,8},{1,9},{2,10},{3,11},{4,20},{5,21},{6,22},{7,23},{8,0},{9,1},... | collective-permute-start | bytes 2064392 | tf_op jit(solution)/shard_map/ppermute | solution.py:315
  55.0 2.1 %collective-permute-start.16 = (bf16[2688,128]{1,0:T(8,128)(2,1)S(1)}, bf16[2688,128]{1,0:T(8,128)(2,1)S(1)}, u32[]{:S(2)}, u32[]{:S(2)}) collective-permute-start(bf16[2688,128]{1,0:T(8,128)(2,1)S(1)} %collective-permute-done.11.refs_6_), channel_id=1, source_target_pairs={{0,4},{1,5},{2,6},{3,7},{4,0},{5,1},{6,2},{7,3},{8,12},{9,13},{10,... | collective-permute-start | bytes 2064392 | tf_op jit(solution)/shard_map/ppermute | solution.py:315

commit v5 on v4

--- a/solution.py
+++ b/solution.py
@@ -450,12 +450,9 @@
         *near,
         *[over_core(after(v, encoded, prior)) for v in near],
     )
-    return part(
-        done,
-        [(True, True, False), (True, True, True)],
-        both_hops,
-        over_core(after(both_hops, *done)),
-    )[0]
+    crossed = over_core(after(both_hops, *done))
+    done = part(done, [(True, True, False)], both_hops)
+    return part(done, [(True, True, True)], crossed)[0]
 
 
 def solution(mesh):

time: 61.2 us -> 60.2 us (0.984)
  waiting for transfers between devices: 20.3 us -> 18.2 us
  Pallas kernels: 18.1 us -> 19.4 us
    ppermute x13, waiting for transfers between devices: 18.2 us -> 16.1 us  [permute(): return lax.ppermute(value, AXES, pairs)]
    pallas_call x2 -> x3, Pallas kernels: 10.5 us -> 11.5 us  [cross(): pl.pallas_call(functools.partial(kernel, blocks), out_shape=jax.ShapeDtyp...]
  transfers between devices with their start and end apart: 17 -> 17, of which waited for: 11 -> 11; matrix products, arithmetic and copies ran while one was open for 1% -> 1% of each run, Pallas kernels for 24% -> 27%
where the time goes in v5:
time: 60.2 us; the launch traced here: 60 us
  Pallas kernels  19.4 us (32%)
  starting transfers between devices  18.2 us (30%)
  waiting for transfers between devices  18.2 us (30%)
  local copies, waits for them, and re-layouts  3.44 us (6%)
  other arithmetic  0.7 us (1%)
    ppermute x13, waiting for transfers between devices, permute(): return lax.ppermute(value, AXES, pairs)  16.1 us
    ppermute x13, starting transfers between devices, permute(): return lax.ppermute(value, AXES, pairs)  12.7 us
    pallas_call x3, Pallas kernels, cross(): pl.pallas_call(functools.partial(kernel, blocks), out_shape=jax.ShapeDtyp...  11.5 us
    pallas_call x2, Pallas kernels, encode(): pl.pallas_call(functools.partial(encode_kernel, peers, capacity, cache_sl...  6.04 us
    ppermute x1, starting transfers between devices, per_device(): prior = lax.ppermute(last, 'span', [(i, i + 1) for i in range(spans - 1)])  2.89 us
    ppermute x3, starting transfers between devices, per_device(): lax.ppermute(v, 'cache', [(i, i ^ r) for i in range(peers)])  2.59 us
    unnamed x16, local copies, waits for them, and re-layouts  2.42 us
    ppermute x3, waiting for transfers between devices, per_device(): lax.ppermute(v, 'cache', [(i, i ^ r) for i in range(peers)])  2.07 us
  transfers between devices with their start and end apart: 17, of which 11 were waited for; matrix products, arithmetic and copies ran while one was open for 1% of the time, Pallas kernels for 27%

profile of v5, /device:TPU:0, one launch (start us, length us, event | category | flops | bytes accessed | tf_op | source)
XLA Modules:
  0.0 60.0 jit_solution(12020350171356235166)
XLA Ops:
  0.0 1.0 %constant_dynamic-slice_fusion = bf16[896,128]{1,0:T(8,128)(2,1)S(1)} fusion(bf16[896,1024]{1,0:T(8,128)(2,1)} %refs_5_.5, s32[]{:T(128)S(6)} %select_n.3), kind=kLoop, calls=%fused_computation.4 | loop fusion | bytes 458756 | tf_op jit(solution)/shard_map/dynamic_slice | solution.py:339
  1.0 5.1 %collective-permute-start.7 = (bf16[896,128]{1,0:T(8,128)(2,1)S(1)}, bf16[896,128]{1,0:T(8,128)(2,1)S(1)}, u32[]{:S(2)}, u32[]{:S(2)}) collective-permute-start(bf16[896,128]{1,0:T(8,128)(2,1)S(1)} %constant_dynamic-slice_fusion), channel_id=1, source_target_pairs={{0,3},{1,2},{2,1},{3,0},{4,7},{5,6},{6,5},{7,4},{8,11},{9,10},{10,... | collective-permute-start | bytes 688136 | tf_op jit(solution)/shard_map/ppermute | solution.py:315
  6.1 0.6 %collective-permute-start.9 = (bf16[896,128]{1,0:T(8,128)(2,1)S(1)}, bf16[896,128]{1,0:T(8,128)(2,1)S(1)}, u32[]{:S(2)}, u32[]{:S(2)}) collective-permute-start(bf16[896,128]{1,0:T(8,128)(2,1)S(1)} %constant_dynamic-slice_fusion), channel_id=1, source_target_pairs={{0,2},{1,3},{2,0},{3,1},{4,6},{5,7},{6,4},{7,5},{8,10},{9,11},{10,... | collective-permute-start | bytes 688136 | tf_op jit(solution)/shard_map/ppermute | solution.py:315
  6.7 0.7 %add_bitcast_fusion.refs_0_ = s32[2,4]{1,0:T(2,128)S(1)} fusion(s32[4,2]{0,1:T(2,128)} %param.12, s32[4,2]{0,1:T(2,128)} %param.11), kind=kLoop, calls=%fused_computation.3 | loop fusion | flops 16 | bytes 96 | tf_op jit(solution)/shard_map/add | solution.py:362
  7.4 1.7 %collective-permute-start.1 = (s32[2,4]{1,0:T(2,128)S(1)}, s32[2,4]{1,0:T(2,128)S(1)}, u32[]{:S(2)}, u32[]{:S(2)}) collective-permute-start(s32[2,4]{1,0:T(2,128)S(1)} %add_bitcast_fusion.refs_0_), channel_id=1, source_target_pairs={{0,8},{4,12},{8,0},{12,4},{1,9},{5,13},{9,1},{13,5},{2,10},{6,14},... | collective-permute-start | bytes 104 | tf_op jit(solution)/shard_map/ppermute | solution.py:359
  9.1 0.9 %collective-permute-start.2 = (s32[2,4]{1,0:T(2,128)S(1)}, s32[2,4]{1,0:T(2,128)S(1)}, u32[]{:S(2)}, u32[]{:S(2)}) collective-permute-start(s32[2,4]{1,0:T(2,128)S(1)} %add_bitcast_fusion.refs_0_), channel_id=1, source_target_pairs={{0,12},{4,8},{8,4},{12,0},{1,13},{5,9},{9,5},{13,1},{2,14},{6,10},... | collective-permute-start | bytes 104 | tf_op jit(solution)/shard_map/ppermute | solution.py:359
  10.0 1.0 %collective-permute-done.1.refs_1_ = s32[2,4]{1,0:T(2,128)S(1)} collective-permute-done((s32[2,4]{1,0:T(2,128)S(1)}, s32[2,4]{1,0:T(2,128)S(1)}, u32[]{:S(2)}, u32[]{:S(2)}) %collective-permute-start.1) | collective-permute-done | bytes 64 | tf_op jit(solution)/shard_map/ppermute | solution.py:359
  11.0 1.1 %collective-permute-done.2.refs_2_ = s32[2,4]{1,0:T(2,128)S(1)} collective-permute-done((s32[2,4]{1,0:T(2,128)S(1)}, s32[2,4]{1,0:T(2,128)S(1)}, u32[]{:S(2)}, u32[]{:S(2)}) %collective-permute-start.2) | collective-permute-done | bytes 64 | tf_op jit(solution)/shard_map/ppermute | solution.py:359
  12.1 1.2 %copy-done.1 = bf16[8,64,896]{2,1,0:T(8,128)(2,1)S(1)} copy-done((bf16[8,64,896]{2,1,0:T(8,128)(2,1)S(1)}, bf16[8,64,896]{2,1,0:T(8,128)(2,1)}, u32[]{:S(2)}) %copy-start.1) | copy-done | bytes 917528
  13.3 1.8 %fetch.1 = (bf16[2,64,896]{2,1,0:T(8,128)(2,1)S(1)}, bf16[4,64,896]{2,1,0:T(8,128)(2,1)S(1)}) custom-call(s32[2,4]{1,0:T(2,128)S(1)} %collective-permute-done.refs_0_, s32[2,4]{1,0:T(2,128)S(1)} %collective-permute-done.1.refs_1_, s32[2,4]{1,0:T(2,128)S(1)} %collective-permute-done.2.refs_2_, bf16[8,64,896]{2,1,0:T(8,128)(2,1)S(1)} %copy-done.1), custom_call_target="tpu_custom_call" | custom-call | tf_op jit(solution)/shard_map/fetch/pallas_call | solution.py:371
  15.1 1.2 %collective-permute-start.4 = (bf16[4,64,896]{2,1,0:T(8,128)(2,1)S(1)}, bf16[4,64,896]{2,1,0:T(8,128)(2,1)S(1)}, u32[]{:S(2)}, u32[]{:S(2)}) collective-permute-start(bf16[4,64,896]{2,1,0:T(8,128)(2,1)S(1)} %get-tuple-element.17), channel_id=1, source_target_pairs={{0,8},{1,9},{2,10},{3,11},{4,12},{5,13},{6,14},{7,15},{8,0},{9,1},... | collective-permute-start | bytes 1376264 | tf_op jit(solution)/shard_map/ppermute | solution.py:315
  16.3 1.4 %collective-permute-done.8 = bf16[896,128]{1,0:T(8,128)(2,1)S(1)} collective-permute-done((bf16[896,128]{1,0:T(8,128)(2,1)S(1)}, bf16[896,128]{1,0:T(8,128)(2,1)S(1)}, u32[]{:S(2)}, u32[]{:S(2)}) %collective-permute-start.8) | collective-permute-done | bytes 229408 | tf_op jit(solution)/shard_map/ppermute | solution.py:315
  17.7 7.9 %collective-permute-done.9 = bf16[896,128]{1,0:T(8,128)(2,1)S(1)} collective-permute-done((bf16[896,128]{1,0:T(8,128)(2,1)S(1)}, bf16[896,128]{1,0:T(8,128)(2,1)S(1)}, u32[]{:S(2)}, u32[]{:S(2)}) %collective-permute-start.9) | collective-permute-done | bytes 229408 | tf_op jit(solution)/shard_map/ppermute | solution.py:315
  25.7 1.6 %collective-permute-start.12 = (bf16[2688,128]{1,0:T(8,128)(2,1)S(1)}, bf16[2688,128]{1,0:T(8,128)(2,1)S(1)}, u32[]{:S(2)}, u32[]{:S(2)}) collective-permute-start(bf16[2688,128]{1,0:T(8,128)(2,1)S(1)} %constant_dynamic-update-slice_fusion.refs_6_), channel_id=1, source_target_pairs={{0,8},{1,9},{2,10},{3,11},{4,20},{5,21},{6,22},{7,23},{8,0},{9,1},... | collective-permute-start | bytes 2064392 | tf_op jit(solution)/shard_map/ppermute | solution.py:315
  27.3 1.5 %collective-permute-start.10 = (bf16[2688,128]{1,0:T(8,128)(2,1)S(1)}, bf16[2688,128]{1,0:T(8,128)(2,1)S(1)}, u32[]{:S(2)}, u32[]{:S(2)}) collective-permute-start(bf16[2688,128]{1,0:T(8,128)(2,1)S(1)} %constant_dynamic-update-slice_fusion.refs_6_), channel_id=1, source_target_pairs={{0,16},{1,17},{2,18},{3,19},{4,12},{5,13},{6,14},{7,15},{8,24},{9,... | collective-permute-start | bytes 2064392 | tf_op jit(solution)/shard_map/ppermute | solution.py:315
  28.8 0.6 collective-permute-start.5
  29.3 0.9 %collective-permute-done.3.refs_5_ = bf16[2,64,896]{2,1,0:T(8,128)(2,1)S(1)} collective-permute-done((bf16[2,64,896]{2,1,0:T(8,128)(2,1)S(1)}, bf16[2,64,896]{2,1,0:T(8,128)(2,1)S(1)}, u32[]{:S(2)}, u32[]{:S(2)}) %collective-permute-start.3) | collective-permute-done | bytes 229408 | tf_op jit(solution)/shard_map/ppermute | solution.py:315
  30.2 0.3 collective-permute-done.5.refs_7_
  30.6 1.2 %copy-done.5 = bf16[256,1792]{1,0:T(8,128)(2,1)S(1)} copy-done((bf16[256,1792]{1,0:T(8,128)(2,1)S(1)}, bf16[256,1792]{1,0:T(8,128)(2,1)}, u32[]{:S(2)}) %copy-start.5) | copy-done | bytes 917528
  31.8 1.9 %encode.2.refs_2_ = bf16[144,896]{1,0:T(8,128)(2,1)S(1)} custom-call(s32[2,4]{1,0:T(2,128)S(1)} %add_bitcast_fusion.refs_0_, s32[2,4]{1,0:T(2,128)S(1)} %bitcast.3, bf16[256,1792]{1,0:T(8,128)(2,1)S(1)} %copy-done.5, bf16[896,896]{1,0:T(8,128)(2,1)S(1)} %copy-done.3, bf16[8,64,896]{2,1,0:T(8,128)(2,1)S(1)} %copy-done.2, ...), custom_call_target="tpu_custom_call" | custom-call | flops 322961408 | bytes 2097152 | tf_op jit(solution)/shard_map/encode/pallas_call | solution.py:398
  33.7 2.9 %collective-permute-start.6 = (bf16[144,896]{1,0:T(8,128)(2,1)S(1)}, bf16[144,896]{1,0:T(8,128)(2,1)S(1)}, u32[]{:S(2)}, u32[]{:S(2)}) collective-permute-start(bf16[144,896]{1,0:T(8,128)(2,1)S(1)} %encode.2.refs_2_), channel_id=1, source_target_pairs={{0,1},{1,2},{2,3},{4,5},{5,6},{6,7},{8,9},{9,10},{10,11},{12,13},{... | collective-permute-start | bytes 774152 | tf_op jit(solution)/shard_map/ppermute | solution.py:418
  36.6 4.2 %encode.3.refs_1_ = bf16[384,896]{1,0:T(8,128)(2,1)S(1)} custom-call(s32[2,4]{1,0:T(2,128)S(1)} %add_bitcast_fusion.refs_0_, s32[2,4]{1,0:T(2,128)S(1)} %bitcast.4, bf16[256,1792]{1,0:T(8,128)(2,1)S(1)} %copy-done.5, bf16[896,896]{1,0:T(8,128)(2,1)S(1)} %copy-done.3, bf16[8,64,896]{2,1,0:T(8,128)(2,1)S(1)} %copy-done.2, ...), custom_call_target="tpu_custom_call" | custom-call | flops 968884224 | bytes 6291456 | tf_op jit(solution)/shard_map/encode/pallas_call | solution.py:398
  40.7 2.7 %collective-permute-done.12.refs_8_ = bf16[2688,128]{1,0:T(8,128)(2,1)S(1)} collective-permute-done((bf16[2688,128]{1,0:T(8,128)(2,1)S(1)}, bf16[2688,128]{1,0:T(8,128)(2,1)S(1)}, u32[]{:S(2)}, u32[]{:S(2)}) %collective-permute-start.12) | collective-permute-done | bytes 688160 | tf_op jit(solution)/shard_map/ppermute | solution.py:315
  43.4 0.5 collective-permute-start.14
  44.0 1.5 %collective-permute-start.11 = (bf16[2688,128]{1,0:T(8,128)(2,1)S(1)}, bf16[2688,128]{1,0:T(8,128)(2,1)S(1)}, u32[]{:S(2)}, u32[]{:S(2)}) collective-permute-start(bf16[2688,128]{1,0:T(8,128)(2,1)S(1)} %collective-permute-done.10.refs_7_), channel_id=1, source_target_pairs={{0,8},{1,9},{2,10},{3,11},{4,20},{5,21},{6,22},{7,23},{8,0},{9,1},... | collective-permute-start | bytes 2064392 | tf_op jit(solution)/shard_map/ppermute | solution.py:315
  45.6 1.0 %collective-permute-done.14.refs_10_ = bf16[2688,128]{1,0:T(8,128)(2,1)S(1)} collective-permute-done((bf16[2688,128]{1,0:T(8,128)(2,1)S(1)}, bf16[2688,128]{1,0:T(8,128)(2,1)S(1)}, u32[]{:S(2)}, u32[]{:S(2)}) %collective-permute-start.14) | collective-permute-done | bytes 688160 | tf_op jit(solution)/shard_map/ppermute | solution.py:315
  46.6 1.0 %collective-permute-done.13.refs_9_ = bf16[2688,128]{1,0:T(8,128)(2,1)S(1)} collective-permute-done((bf16[2688,128]{1,0:T(8,128)(2,1)S(1)}, bf16[2688,128]{1,0:T(8,128)(2,1)S(1)}, u32[]{:S(2)}, u32[]{:S(2)}) %collective-permute-start.13) | collective-permute-done | bytes 688160 | tf_op jit(solution)/shard_map/ppermute | solution.py:315
  47.6 6.7 %cross.3.refs_7_ = bf16[256,2048]{1,0:T(8,128)(2,1)S(1)} custom-call(s32[2,4]{1,0:T(2,128)S(1)} %bitcast.5, bf16[384,896]{1,0:T(8,128)(2,1)S(1)} %encode.3.refs_1_, bf16[144,896]{1,0:T(8,128)(2,1)S(1)} %encode.2.refs_2_, bf16[144,896]{1,0:T(8,128)(2,1)S(1)} %collective-permute-done.6.refs_3_, bf16[256,2048]{1,0:T(8,128)(2,1)S(1)} %copy-done.4, ...), custom_call_target="tpu_custom_call" | custom-call | flops 4529848320 | bytes 8388608 | tf_op jit(solution)/shard_map/cross/pallas_call | solution.py:423
  54.3 0.7 %collective-permute-done.11.refs_6_ = bf16[2688,128]{1,0:T(8,128)(2,1)S(1)} collective-permute-done((bf16[2688,128]{1,0:T(8,128)(2,1)S(1)}, bf16[2688,128]{1,0:T(8,128)(2,1)S(1)}, u32[]{:S(2)}, u32[]{:S(2)}) %collective-permute-start.11) | collective-permute-done | bytes 688160 | tf_op jit(solution)/shard_map/ppermute | solution.py:315
  55.0 1.9 %cross.4.refs_7_ = bf16[256,2048]{1,0:T(8,128)(2,1)S(1)} custom-call(s32[2,4]{1,0:T(2,128)S(1)} %bitcast.6, bf16[384,896]{1,0:T(8,128)(2,1)S(1)} %encode.3.refs_1_, bf16[144,896]{1,0:T(8,128)(2,1)S(1)} %encode.2.refs_2_, bf16[144,896]{1,0:T(8,128)(2,1)S(1)} %collective-permute-done.6.refs_3_, bf16[256,2048]{1,0:T(8,128)(2,1)S(1)} %copy-done.4, ...), custom_call_target="tpu_custom_call" | custom-call | flops 754974720 | bytes 8388608 | tf_op jit(solution)/shard_map/cross/pallas_call | solution.py:423
  56.9 0.2 collective-permute-done.16.refs_6_
  57.1 2.9 %cross.5 = bf16[256,2048]{1,0:T(8,128)(2,1)} custom-call(s32[2,4]{1,0:T(2,128)S(1)} %bitcast.7, bf16[384,896]{1,0:T(8,128)(2,1)S(1)} %encode.3.refs_1_, bf16[144,896]{1,0:T(8,128)(2,1)S(1)} %encode.2.refs_2_, bf16[144,896]{1,0:T(8,128)(2,1)S(1)} %collective-permute-done.6.refs_3_, bf16[256,2048]{1,0:T(8,128)(2,1)S(1)} %copy-done.4, ...), custom_call_target="tpu_custom_call" | custom-call | flops 754974720 | bytes 8388608 | tf_op jit(solution)/shard_map/cross/pallas_call | solution.py:423
  (28 shorter events, 0.3 us)
Async XLA Ops:
  0.0 30.6 %copy-start.6 = (s32[4,2]{0,1:T(2,128)S(1)}, s32[4,2]{0,1:T(2,128)}, u32[]{:S(2)}) copy-start(s32[4,2]{0,1:T(2,128)} %param.13) | copy-start | bytes 100
  1.0 15.3 %collective-permute-start.7 = (bf16[896,128]{1,0:T(8,128)(2,1)S(1)}, bf16[896,128]{1,0:T(8,128)(2,1)S(1)}, u32[]{:S(2)}, u32[]{:S(2)}) collective-permute-start(bf16[896,128]{1,0:T(8,128)(2,1)S(1)} %constant_dynamic-slice_fusion), channel_id=1, source_target_pairs={{0,3},{1,2},{2,1},{3,0},{4,7},{5,6},{6,5},{7,4},{8,11},{9,10},{10,... | collective-permute-start | bytes 688136 | tf_op jit(solution)/shard_map/ppermute | solution.py:315
  6.1 11.6 %collective-permute-start.8 = (bf16[896,128]{1,0:T(8,128)(2,1)S(1)}, bf16[896,128]{1,0:T(8,128)(2,1)S(1)}, u32[]{:S(2)}, u32[]{:S(2)}) collective-permute-start(bf16[896,128]{1,0:T(8,128)(2,1)S(1)} %constant_dynamic-slice_fusion), channel_id=1, source_target_pairs={{0,1},{1,0},{2,3},{3,2},{4,5},{5,4},{6,7},{7,6},{8,9},{9,8},{10,11... | collective-permute-start | bytes 688136 | tf_op jit(solution)/shard_map/ppermute | solution.py:315
  6.1 19.5 %collective-permute-start.9 = (bf16[896,128]{1,0:T(8,128)(2,1)S(1)}, bf16[896,128]{1,0:T(8,128)(2,1)S(1)}, u32[]{:S(2)}, u32[]{:S(2)}) collective-permute-start(bf16[896,128]{1,0:T(8,128)(2,1)S(1)} %constant_dynamic-slice_fusion), channel_id=1, source_target_pairs={{0,2},{1,3},{2,0},{3,1},{4,6},{5,7},{6,4},{7,5},{8,10},{9,11},{10,... | collective-permute-start | bytes 688136 | tf_op jit(solution)/shard_map/ppermute | solution.py:315
  7.4 1.7 %collective-permute-start = (s32[2,4]{1,0:T(2,128)S(1)}, s32[2,4]{1,0:T(2,128)S(1)}, u32[]{:S(2)}, u32[]{:S(2)}) collective-permute-start(s32[2,4]{1,0:T(2,128)S(1)} %add_bitcast_fusion.refs_0_), channel_id=1, source_target_pairs={{0,4},{4,0},{8,12},{12,8},{1,5},{5,1},{9,13},{13,9},{2,6},{6,2},{1... | collective-permute-start | bytes 104 | tf_op jit(solution)/shard_map/ppermute | solution.py:359
  7.4 3.6 %collective-permute-start.1 = (s32[2,4]{1,0:T(2,128)S(1)}, s32[2,4]{1,0:T(2,128)S(1)}, u32[]{:S(2)}, u32[]{:S(2)}) collective-permute-start(s32[2,4]{1,0:T(2,128)S(1)} %add_bitcast_fusion.refs_0_), channel_id=1, source_target_pairs={{0,8},{4,12},{8,0},{12,4},{1,9},{5,13},{9,1},{13,5},{2,10},{6,14},... | collective-permute-start | bytes 104 | tf_op jit(solution)/shard_map/ppermute | solution.py:359
  9.1 3.0 %collective-permute-start.2 = (s32[2,4]{1,0:T(2,128)S(1)}, s32[2,4]{1,0:T(2,128)S(1)}, u32[]{:S(2)}, u32[]{:S(2)}) collective-permute-start(s32[2,4]{1,0:T(2,128)S(1)} %add_bitcast_fusion.refs_0_), channel_id=1, source_target_pairs={{0,12},{4,8},{8,4},{12,0},{1,13},{5,9},{9,5},{13,1},{2,14},{6,10},... | collective-permute-start | bytes 104 | tf_op jit(solution)/shard_map/ppermute | solution.py:359
  12.1 1.2 %copy-start.1 = (bf16[8,64,896]{2,1,0:T(8,128)(2,1)S(1)}, bf16[8,64,896]{2,1,0:T(8,128)(2,1)}, u32[]{:S(2)}) copy-start(bf16[8,64,896]{2,1,0:T(8,128)(2,1)} %refs_4_.6) | copy-start | bytes 2752516
  13.3 17.3 %copy-start.2 = (bf16[8,64,896]{2,1,0:T(8,128)(2,1)S(1)}, bf16[8,64,896]{2,1,0:T(8,128)(2,1)}, u32[]{:S(2)}) copy-start(bf16[8,64,896]{2,1,0:T(8,128)(2,1)} %refs_4_.6) | copy-start | bytes 2752516
  13.3 17.3 %copy-start.3 = (bf16[896,896]{1,0:T(8,128)(2,1)S(1)}, bf16[896,896]{1,0:T(8,128)(2,1)}, u32[]{:S(2)}) copy-start(bf16[896,896]{1,0:T(8,128)(2,1)} %refs_3_.5) | copy-start | bytes 4816900
  15.1 13.7 %collective-permute-start.4 = (bf16[4,64,896]{2,1,0:T(8,128)(2,1)S(1)}, bf16[4,64,896]{2,1,0:T(8,128)(2,1)S(1)}, u32[]{:S(2)}, u32[]{:S(2)}) collective-permute-start(bf16[4,64,896]{2,1,0:T(8,128)(2,1)S(1)} %get-tuple-element.17), channel_id=1, source_target_pairs={{0,8},{1,9},{2,10},{3,11},{4,12},{5,13},{6,14},{7,15},{8,0},{9,1},... | collective-permute-start | bytes 1376264 | tf_op jit(solution)/shard_map/ppermute | solution.py:315
  25.7 17.8 %collective-permute-start.12 = (bf16[2688,128]{1,0:T(8,128)(2,1)S(1)}, bf16[2688,128]{1,0:T(8,128)(2,1)S(1)}, u32[]{:S(2)}, u32[]{:S(2)}) collective-permute-start(bf16[2688,128]{1,0:T(8,128)(2,1)S(1)} %constant_dynamic-update-slice_fusion.refs_6_), channel_id=1, source_target_pairs={{0,8},{1,9},{2,10},{3,11},{4,20},{5,21},{6,22},{7,23},{8,0},{9,1},... | collective-permute-start | bytes 2064392 | tf_op jit(solution)/shard_map/ppermute | solution.py:315
  27.3 16.2 %collective-permute-start.10 = (bf16[2688,128]{1,0:T(8,128)(2,1)S(1)}, bf16[2688,128]{1,0:T(8,128)(2,1)S(1)}, u32[]{:S(2)}, u32[]{:S(2)}) collective-permute-start(bf16[2688,128]{1,0:T(8,128)(2,1)S(1)} %constant_dynamic-update-slice_fusion.refs_6_), channel_id=1, source_target_pairs={{0,16},{1,17},{2,18},{3,19},{4,12},{5,13},{6,14},{7,15},{8,24},{9,... | collective-permute-start | bytes 2064392 | tf_op jit(solution)/shard_map/ppermute | solution.py:315
  28.7 1.5 %collective-permute-start.3 = (bf16[2,64,896]{2,1,0:T(8,128)(2,1)S(1)}, bf16[2,64,896]{2,1,0:T(8,128)(2,1)S(1)}, u32[]{:S(2)}, u32[]{:S(2)}) collective-permute-start(bf16[2,64,896]{2,1,0:T(8,128)(2,1)S(1)} %get-tuple-element.16), channel_id=1, source_target_pairs={{0,4},{1,5},{2,6},{3,7},{4,0},{5,1},{6,2},{7,3},{8,12},{9,13},{10,... | collective-permute-start | bytes 688136 | tf_op jit(solution)/shard_map/ppermute | solution.py:315
  28.8 1.8 %collective-permute-start.5 = (bf16[2,64,896]{2,1,0:T(8,128)(2,1)S(1)}, bf16[2,64,896]{2,1,0:T(8,128)(2,1)S(1)}, u32[]{:S(2)}, u32[]{:S(2)}) collective-permute-start(bf16[2,64,896]{2,1,0:T(8,128)(2,1)S(1)} %slice.4), channel_id=1, source_target_pairs={{0,4},{1,5},{2,6},{3,7},{4,0},{5,1},{6,2},{7,3},{8,12},{9,13},{10,... | collective-permute-start | bytes 688136 | tf_op jit(solution)/shard_map/ppermute | solution.py:315
  30.6 1.2 %copy-start.5 = (bf16[256,1792]{1,0:T(8,128)(2,1)S(1)}, bf16[256,1792]{1,0:T(8,128)(2,1)}, u32[]{:S(2)}) copy-start(bf16[256,1792]{1,0:T(8,128)(2,1)} %refs_2_.3) | copy-start | bytes 2752516
  33.6 13.9 %copy-start = (bf16[896,1024]{1,0:T(8,128)(2,1)S(1)}, bf16[896,1024]{1,0:T(8,128)(2,1)}, u32[]{:S(2)}) copy-start(bf16[896,1024]{1,0:T(8,128)(2,1)} %refs_5_.5) | copy-start | bytes 5505028
  33.7 13.9 %copy-start.4 = (bf16[256,2048]{1,0:T(8,128)(2,1)S(1)}, bf16[256,2048]{1,0:T(8,128)(2,1)}, u32[]{:S(2)}) copy-start(bf16[256,2048]{1,0:T(8,128)(2,1)} %refs_4_.9) | copy-start | bytes 3145732
  33.7 9.8 %collective-permute-start.6 = (bf16[144,896]{1,0:T(8,128)(2,1)S(1)}, bf16[144,896]{1,0:T(8,128)(2,1)S(1)}, u32[]{:S(2)}, u32[]{:S(2)}) collective-permute-start(bf16[144,896]{1,0:T(8,128)(2,1)S(1)} %encode.2.refs_2_), channel_id=1, source_target_pairs={{0,1},{1,2},{2,3},{4,5},{5,6},{6,7},{8,9},{9,10},{10,11},{12,13},{... | collective-permute-start | bytes 774152 | tf_op jit(solution)/shard_map/ppermute | solution.py:418
  43.4 2.1 %collective-permute-start.15 = (bf16[2688,128]{1,0:T(8,128)(2,1)S(1)}, bf16[2688,128]{1,0:T(8,128)(2,1)S(1)}, u32[]{:S(2)}, u32[]{:S(2)}) collective-permute-start(bf16[2688,128]{1,0:T(8,128)(2,1)S(1)} %collective-permute-done.12.refs_8_), channel_id=1, source_target_pairs={{0,4},{1,5},{2,6},{3,7},{4,0},{5,1},{6,2},{7,3},{8,12},{9,13},{10,... | collective-permute-start | bytes 2064392 | tf_op jit(solution)/shard_map/ppermute | solution.py:315
  43.4 3.1 %collective-permute-start.14 = (bf16[2688,128]{1,0:T(8,128)(2,1)S(1)}, bf16[2688,128]{1,0:T(8,128)(2,1)S(1)}, u32[]{:S(2)}, u32[]{:S(2)}) collective-permute-start(bf16[2688,128]{1,0:T(8,128)(2,1)S(1)} %collective-permute-done.10.refs_7_), channel_id=1, source_target_pairs={{0,4},{1,5},{2,6},{3,7},{4,0},{5,1},{6,2},{7,3},{8,12},{9,13},{10,... | collective-permute-start | bytes 2064392 | tf_op jit(solution)/shard_map/ppermute | solution.py:315
  43.9 3.6 %collective-permute-start.13 = (bf16[2688,128]{1,0:T(8,128)(2,1)S(1)}, bf16[2688,128]{1,0:T(8,128)(2,1)S(1)}, u32[]{:S(2)}, u32[]{:S(2)}) collective-permute-start(bf16[2688,128]{1,0:T(8,128)(2,1)S(1)} %constant_dynamic-update-slice_fusion.refs_6_), channel_id=1, source_target_pairs={{0,4},{1,5},{2,6},{3,7},{4,0},{5,1},{6,2},{7,3},{8,12},{9,13},{10,... | collective-permute-start | bytes 2064392 | tf_op jit(solution)/shard_map/ppermute | solution.py:315
  44.0 10.9 %collective-permute-start.11 = (bf16[2688,128]{1,0:T(8,128)(2,1)S(1)}, bf16[2688,128]{1,0:T(8,128)(2,1)S(1)}, u32[]{:S(2)}, u32[]{:S(2)}) collective-permute-start(bf16[2688,128]{1,0:T(8,128)(2,1)S(1)} %collective-permute-done.10.refs_7_), channel_id=1, source_target_pairs={{0,8},{1,9},{2,10},{3,11},{4,20},{5,21},{6,22},{7,23},{8,0},{9,1},... | collective-permute-start | bytes 2064392 | tf_op jit(solution)/shard_map/ppermute | solution.py:315
  55.0 2.1 %collective-permute-start.16 = (bf16[2688,128]{1,0:T(8,128)(2,1)S(1)}, bf16[2688,128]{1,0:T(8,128)(2,1)S(1)}, u32[]{:S(2)}, u32[]{:S(2)}) collective-permute-start(bf16[2688,128]{1,0:T(8,128)(2,1)S(1)} %collective-permute-done.11.refs_6_), channel_id=1, source_target_pairs={{0,4},{1,5},{2,6},{3,7},{4,0},{5,1},{6,2},{7,3},{8,12},{9,13},{10,... | collective-permute-start | bytes 2064392 | tf_op jit(solution)/shard_map/ppermute | solution.py:315

commit v6 on v5

--- a/solution.py
+++ b/solution.py
@@ -264,12 +264,14 @@
     return ((low ^ lax.axis_index("span")) & 1) * 8 + place
 
 
-def pieces_kernel(offsets, resumed, blocks, *refs):
+def pieces_kernel(offsets, resumed, placed, blocks, *refs):
     core = lax.axis_index("cache") % 2
     lengths_ref, encoded_ref, last_ref, prior_ref, queries_ref, weight_ref = refs[:6]
-    out_ref = refs[-1]
-    groups = refs[6:-1]
-    if resumed:
+    if placed:
+        groups, (out_ref, own_ref, sem) = refs[6:-3], refs[-3:]
+    else:
+        groups, out_ref = refs[6:-1], refs[-1]
+    if resumed and not placed:
         out_ref[...] = groups[-1][...]
         groups = groups[:-1]
 
@@ -293,15 +295,26 @@
             return [piece(held, 1), piece(held, 3)]
 
         columns = head_columns(head_of(0 if own else 1, column))
-        return columns, columns, load
+        target = head_columns(2 * offsets.index(offset) + int(own)) if placed else columns
+        return columns, target, load
 
     items = []
     for offset, held in zip(offsets, groups):
         items += [item(offset, held, False), item(offset, held, True)]
     swap = lax.axis_index("span") >= 2
+    target_ref = own_ref if placed else out_ref
     cross_heads(
-        blocks, lengths_ref, encoded_ref, last_ref, prior_ref, queries_ref, out_ref, items, swap
+        blocks, lengths_ref, encoded_ref, last_ref, prior_ref, queries_ref, target_ref, items, swap
     )
+    if placed:
+        copies = [
+            pltpu.make_async_copy(own_ref.at[:, target], out_ref.at[:, columns], sem.at[n])
+            for n, (columns, target, _) in enumerate(items)
+        ]
+        for copy in copies:
+            copy.start()
+        for copy in copies:
+            copy.wait()
 
 
 def permute(value, move):
@@ -419,12 +432,18 @@
     ids = after(ids, last)
     encoded = encode(range(blocks - 1), 0)
 
-    def cross(kernel, heads, *operands):
+    def cross(kernel, heads, *operands, placed=False):
         return pl.pallas_call(
             functools.partial(kernel, blocks),
             out_shape=jax.ShapeDtypeStruct(cross_queries.shape, jnp.bfloat16),
-            in_specs=[SMEM] + [VMEM] * (4 + len(operands)),
-            out_specs=VMEM,
+            in_specs=[SMEM] + [VMEM] * (4 + len(operands) - placed) + [ANY] * placed,
+            out_specs=ANY if placed else VMEM,
+            scratch_shapes=[
+                pltpu.VMEM((blocks * BLOCK_LEN, heads * CROSS_HEAD), jnp.bfloat16),
+                pltpu.SemaphoreType.DMA((heads,)),
+            ]
+            * placed,
+            input_output_aliases={4 + len(operands): 0} if placed else {},
             compiler_params=pltpu.CompilerParams(vmem_limit_bytes=32 * 2**20),
             cost_estimate=pl.CostEstimate(
                 flops=4 * (blocks + 1) * KEYS * (ENCODER_WIDTH + 2 * LANES) * heads * CROSS_HEAD,
@@ -437,9 +456,9 @@
     if not pieced:
         return cross(whole_kernel, CROSS_HEADS, weights)
 
-    def part(done, offsets, *operands):
-        kernel = functools.partial(pieces_kernel, offsets, bool(done))
-        return [cross(kernel, 2 * len(offsets), cross_weight, *operands, *done)]
+    def part(done, offsets, *operands, placed=False):
+        kernel = functools.partial(pieces_kernel, offsets, bool(done), placed)
+        return [cross(kernel, 2 * len(offsets), cross_weight, *operands, *done, placed=placed)]
 
     both_hops = over_second(after(first_hop, encoded))
     near = [pieces, first_hop, second_hop]
@@ -452,7 +471,7 @@
     )
     crossed = over_core(after(both_hops, *done))
     done = part(done, [(True, True, False)], both_hops)
-    return part(done, [(True, True, True)], crossed)[0]
+    return part(done, [(True, True, True)], crossed, placed=True)[0]
 
 
 def solution(mesh):

time: 60.2 us -> 60.9 us (1.012)
    pallas_call x3, Pallas kernels: 11.5 us -> 12.2 us  [cross(): pl.pallas_call(functools.partial(kernel, blocks), out_shape=jax.ShapeDtyp...]
  transfers between devices with their start and end apart: 17 -> 17, of which waited for: 11 -> 10; matrix products, arithmetic and copies ran while one was open for 1% -> 1% of each run, Pallas kernels for 27% -> 29%
where the time goes in v6:
time: 60.9 us; the launch traced here: 60.6 us
  Pallas kernels  20 us (33%)
  starting transfers between devices  18.2 us (30%)
  waiting for transfers between devices  18 us (30%)
  local copies, waits for them, and re-layouts  3.44 us (6%)
  other arithmetic  0.7 us (1%)
    ppermute x13, waiting for transfers between devices, permute(): return lax.ppermute(value, AXES, pairs)  15.9 us
    ppermute x13, starting transfers between devices, permute(): return lax.ppermute(value, AXES, pairs)  12.7 us
    pallas_call x3, Pallas kernels, cross(): pl.pallas_call(functools.partial(kernel, blocks), out_shape=jax.ShapeDtyp...  12.2 us
    pallas_call x2, Pallas kernels, encode(): pl.pallas_call(functools.partial(encode_kernel, peers, capacity, cache_sl...  6.04 us
    ppermute x1, starting transfers between devices, per_device(): prior = lax.ppermute(last, 'span', [(i, i + 1) for i in range(spans - 1)])  2.89 us
    ppermute x3, starting transfers between devices, per_device(): lax.ppermute(v, 'cache', [(i, i ^ r) for i in range(peers)])  2.59 us
    unnamed x16, local copies, waits for them, and re-layouts  2.42 us
    ppermute x3, waiting for transfers between devices, per_device(): lax.ppermute(v, 'cache', [(i, i ^ r) for i in range(peers)])  2.07 us
  transfers between devices with their start and end apart: 17, of which 10 were waited for; matrix products, arithmetic and copies ran while one was open for 1% of the time, Pallas kernels for 29%

profile of v6, /device:TPU:0, one launch (start us, length us, event | category | flops | bytes accessed | tf_op | source)
XLA Modules:
  0.0 60.6 jit_solution(7264368045872056284)
XLA Ops:
  0.0 1.0 %constant_dynamic-slice_fusion = bf16[896,128]{1,0:T(8,128)(2,1)S(1)} fusion(bf16[896,1024]{1,0:T(8,128)(2,1)} %refs_5_.5, s32[]{:T(128)S(6)} %select_n.3), kind=kLoop, calls=%fused_computation.4 | loop fusion | bytes 458756 | tf_op jit(solution)/shard_map/dynamic_slice | solution.py:352
  1.0 5.1 %collective-permute-start.7 = (bf16[896,128]{1,0:T(8,128)(2,1)S(1)}, bf16[896,128]{1,0:T(8,128)(2,1)S(1)}, u32[]{:S(2)}, u32[]{:S(2)}) collective-permute-start(bf16[896,128]{1,0:T(8,128)(2,1)S(1)} %constant_dynamic-slice_fusion), channel_id=1, source_target_pairs={{0,3},{1,2},{2,1},{3,0},{4,7},{5,6},{6,5},{7,4},{8,11},{9,10},{10,... | collective-permute-start | bytes 688136 | tf_op jit(solution)/shard_map/ppermute | solution.py:328
  6.1 0.6 %collective-permute-start.9 = (bf16[896,128]{1,0:T(8,128)(2,1)S(1)}, bf16[896,128]{1,0:T(8,128)(2,1)S(1)}, u32[]{:S(2)}, u32[]{:S(2)}) collective-permute-start(bf16[896,128]{1,0:T(8,128)(2,1)S(1)} %constant_dynamic-slice_fusion), channel_id=1, source_target_pairs={{0,2},{1,3},{2,0},{3,1},{4,6},{5,7},{6,4},{7,5},{8,10},{9,11},{10,... | collective-permute-start | bytes 688136 | tf_op jit(solution)/shard_map/ppermute | solution.py:328
  6.7 0.7 %add_bitcast_fusion.refs_0_ = s32[2,4]{1,0:T(2,128)S(1)} fusion(s32[4,2]{0,1:T(2,128)} %param.12, s32[4,2]{0,1:T(2,128)} %param.11), kind=kLoop, calls=%fused_computation.3 | loop fusion | flops 16 | bytes 96 | tf_op jit(solution)/shard_map/add | solution.py:375
  7.4 1.7 %collective-permute-start.1 = (s32[2,4]{1,0:T(2,128)S(1)}, s32[2,4]{1,0:T(2,128)S(1)}, u32[]{:S(2)}, u32[]{:S(2)}) collective-permute-start(s32[2,4]{1,0:T(2,128)S(1)} %add_bitcast_fusion.refs_0_), channel_id=1, source_target_pairs={{0,8},{4,12},{8,0},{12,4},{1,9},{5,13},{9,1},{13,5},{2,10},{6,14},... | collective-permute-start | bytes 104 | tf_op jit(solution)/shard_map/ppermute | solution.py:372
  9.1 0.9 %collective-permute-start.2 = (s32[2,4]{1,0:T(2,128)S(1)}, s32[2,4]{1,0:T(2,128)S(1)}, u32[]{:S(2)}, u32[]{:S(2)}) collective-permute-start(s32[2,4]{1,0:T(2,128)S(1)} %add_bitcast_fusion.refs_0_), channel_id=1, source_target_pairs={{0,12},{4,8},{8,4},{12,0},{1,13},{5,9},{9,5},{13,1},{2,14},{6,10},... | collective-permute-start | bytes 104 | tf_op jit(solution)/shard_map/ppermute | solution.py:372
  10.0 1.0 %collective-permute-done.1.refs_1_ = s32[2,4]{1,0:T(2,128)S(1)} collective-permute-done((s32[2,4]{1,0:T(2,128)S(1)}, s32[2,4]{1,0:T(2,128)S(1)}, u32[]{:S(2)}, u32[]{:S(2)}) %collective-permute-start.1) | collective-permute-done | bytes 64 | tf_op jit(solution)/shard_map/ppermute | solution.py:372
  11.0 1.1 %collective-permute-done.2.refs_2_ = s32[2,4]{1,0:T(2,128)S(1)} collective-permute-done((s32[2,4]{1,0:T(2,128)S(1)}, s32[2,4]{1,0:T(2,128)S(1)}, u32[]{:S(2)}, u32[]{:S(2)}) %collective-permute-start.2) | collective-permute-done | bytes 64 | tf_op jit(solution)/shard_map/ppermute | solution.py:372
  12.1 1.2 %copy-done.1 = bf16[8,64,896]{2,1,0:T(8,128)(2,1)S(1)} copy-done((bf16[8,64,896]{2,1,0:T(8,128)(2,1)S(1)}, bf16[8,64,896]{2,1,0:T(8,128)(2,1)}, u32[]{:S(2)}) %copy-start.1) | copy-done | bytes 917528
  13.3 1.8 %fetch.1 = (bf16[2,64,896]{2,1,0:T(8,128)(2,1)S(1)}, bf16[4,64,896]{2,1,0:T(8,128)(2,1)S(1)}) custom-call(s32[2,4]{1,0:T(2,128)S(1)} %collective-permute-done.refs_0_, s32[2,4]{1,0:T(2,128)S(1)} %collective-permute-done.1.refs_1_, s32[2,4]{1,0:T(2,128)S(1)} %collective-permute-done.2.refs_2_, bf16[8,64,896]{2,1,0:T(8,128)(2,1)S(1)} %copy-done.1), custom_call_target="tpu_custom_call" | custom-call | tf_op jit(solution)/shard_map/fetch/pallas_call | solution.py:384
  15.1 1.2 %collective-permute-start.4 = (bf16[4,64,896]{2,1,0:T(8,128)(2,1)S(1)}, bf16[4,64,896]{2,1,0:T(8,128)(2,1)S(1)}, u32[]{:S(2)}, u32[]{:S(2)}) collective-permute-start(bf16[4,64,896]{2,1,0:T(8,128)(2,1)S(1)} %get-tuple-element.17), channel_id=1, source_target_pairs={{0,8},{1,9},{2,10},{3,11},{4,12},{5,13},{6,14},{7,15},{8,0},{9,1},... | collective-permute-start | bytes 1376264 | tf_op jit(solution)/shard_map/ppermute | solution.py:328
  16.3 1.4 %collective-permute-done.8 = bf16[896,128]{1,0:T(8,128)(2,1)S(1)} collective-permute-done((bf16[896,128]{1,0:T(8,128)(2,1)S(1)}, bf16[896,128]{1,0:T(8,128)(2,1)S(1)}, u32[]{:S(2)}, u32[]{:S(2)}) %collective-permute-start.8) | collective-permute-done | bytes 229408 | tf_op jit(solution)/shard_map/ppermute | solution.py:328
  17.7 7.9 %collective-permute-done.9 = bf16[896,128]{1,0:T(8,128)(2,1)S(1)} collective-permute-done((bf16[896,128]{1,0:T(8,128)(2,1)S(1)}, bf16[896,128]{1,0:T(8,128)(2,1)S(1)}, u32[]{:S(2)}, u32[]{:S(2)}) %collective-permute-start.9) | collective-permute-done | bytes 229408 | tf_op jit(solution)/shard_map/ppermute | solution.py:328
  25.7 1.6 %collective-permute-start.12 = (bf16[2688,128]{1,0:T(8,128)(2,1)S(1)}, bf16[2688,128]{1,0:T(8,128)(2,1)S(1)}, u32[]{:S(2)}, u32[]{:S(2)}) collective-permute-start(bf16[2688,128]{1,0:T(8,128)(2,1)S(1)} %constant_dynamic-update-slice_fusion.refs_6_), channel_id=1, source_target_pairs={{0,8},{1,9},{2,10},{3,11},{4,20},{5,21},{6,22},{7,23},{8,0},{9,1},... | collective-permute-start | bytes 2064392 | tf_op jit(solution)/shard_map/ppermute | solution.py:328
  27.3 1.5 %collective-permute-start.10 = (bf16[2688,128]{1,0:T(8,128)(2,1)S(1)}, bf16[2688,128]{1,0:T(8,128)(2,1)S(1)}, u32[]{:S(2)}, u32[]{:S(2)}) collective-permute-start(bf16[2688,128]{1,0:T(8,128)(2,1)S(1)} %constant_dynamic-update-slice_fusion.refs_6_), channel_id=1, source_target_pairs={{0,16},{1,17},{2,18},{3,19},{4,12},{5,13},{6,14},{7,15},{8,24},{9,... | collective-permute-start | bytes 2064392 | tf_op jit(solution)/shard_map/ppermute | solution.py:328
  28.8 0.6 collective-permute-start.5
  29.3 0.9 %collective-permute-done.3.refs_5_ = bf16[2,64,896]{2,1,0:T(8,128)(2,1)S(1)} collective-permute-done((bf16[2,64,896]{2,1,0:T(8,128)(2,1)S(1)}, bf16[2,64,896]{2,1,0:T(8,128)(2,1)S(1)}, u32[]{:S(2)}, u32[]{:S(2)}) %collective-permute-start.3) | collective-permute-done | bytes 229408 | tf_op jit(solution)/shard_map/ppermute | solution.py:328
  30.2 0.3 collective-permute-done.5.refs_7_
  30.6 1.2 %copy-done.5 = bf16[256,1792]{1,0:T(8,128)(2,1)S(1)} copy-done((bf16[256,1792]{1,0:T(8,128)(2,1)S(1)}, bf16[256,1792]{1,0:T(8,128)(2,1)}, u32[]{:S(2)}) %copy-start.5) | copy-done | bytes 917528
  31.8 1.9 %encode.2.refs_2_ = bf16[144,896]{1,0:T(8,128)(2,1)S(1)} custom-call(s32[2,4]{1,0:T(2,128)S(1)} %add_bitcast_fusion.refs_0_, s32[2,4]{1,0:T(2,128)S(1)} %bitcast.3, bf16[256,1792]{1,0:T(8,128)(2,1)S(1)} %copy-done.5, bf16[896,896]{1,0:T(8,128)(2,1)S(1)} %copy-done.3, bf16[8,64,896]{2,1,0:T(8,128)(2,1)S(1)} %copy-done.2, ...), custom_call_target="tpu_custom_call" | custom-call | flops 322961408 | bytes 2097152 | tf_op jit(solution)/shard_map/encode/pallas_call | solution.py:411
  33.7 2.9 %collective-permute-start.6 = (bf16[144,896]{1,0:T(8,128)(2,1)S(1)}, bf16[144,896]{1,0:T(8,128)(2,1)S(1)}, u32[]{:S(2)}, u32[]{:S(2)}) collective-permute-start(bf16[144,896]{1,0:T(8,128)(2,1)S(1)} %encode.2.refs_2_), channel_id=1, source_target_pairs={{0,1},{1,2},{2,3},{4,5},{5,6},{6,7},{8,9},{9,10},{10,11},{12,13},{... | collective-permute-start | bytes 774152 | tf_op jit(solution)/shard_map/ppermute | solution.py:431
  36.6 4.2 %encode.3.refs_1_ = bf16[384,896]{1,0:T(8,128)(2,1)S(1)} custom-call(s32[2,4]{1,0:T(2,128)S(1)} %add_bitcast_fusion.refs_0_, s32[2,4]{1,0:T(2,128)S(1)} %bitcast.4, bf16[256,1792]{1,0:T(8,128)(2,1)S(1)} %copy-done.5, bf16[896,896]{1,0:T(8,128)(2,1)S(1)} %copy-done.3, bf16[8,64,896]{2,1,0:T(8,128)(2,1)S(1)} %copy-done.2, ...), custom_call_target="tpu_custom_call" | custom-call | flops 968884224 | bytes 6291456 | tf_op jit(solution)/shard_map/encode/pallas_call | solution.py:411
  40.7 2.7 %collective-permute-done.12.refs_8_ = bf16[2688,128]{1,0:T(8,128)(2,1)S(1)} collective-permute-done((bf16[2688,128]{1,0:T(8,128)(2,1)S(1)}, bf16[2688,128]{1,0:T(8,128)(2,1)S(1)}, u32[]{:S(2)}, u32[]{:S(2)}) %collective-permute-start.12) | collective-permute-done | bytes 688160 | tf_op jit(solution)/shard_map/ppermute | solution.py:328
  43.4 0.5 collective-permute-start.14
  43.9 0.1 collective-permute-start.13
  44.0 1.5 %collective-permute-start.11 = (bf16[2688,128]{1,0:T(8,128)(2,1)S(1)}, bf16[2688,128]{1,0:T(8,128)(2,1)S(1)}, u32[]{:S(2)}, u32[]{:S(2)}) collective-permute-start(bf16[2688,128]{1,0:T(8,128)(2,1)S(1)} %collective-permute-done.10.refs_7_), channel_id=1, source_target_pairs={{0,8},{1,9},{2,10},{3,11},{4,20},{5,21},{6,22},{7,23},{8,0},{9,1},... | collective-permute-start | bytes 2064392 | tf_op jit(solution)/shard_map/ppermute | solution.py:328
  45.6 1.0 %collective-permute-done.14.refs_10_ = bf16[2688,128]{1,0:T(8,128)(2,1)S(1)} collective-permute-done((bf16[2688,128]{1,0:T(8,128)(2,1)S(1)}, bf16[2688,128]{1,0:T(8,128)(2,1)S(1)}, u32[]{:S(2)}, u32[]{:S(2)}) %collective-permute-start.14) | collective-permute-done | bytes 688160 | tf_op jit(solution)/shard_map/ppermute | solution.py:328
  46.6 1.0 %collective-permute-done.13.refs_9_ = bf16[2688,128]{1,0:T(8,128)(2,1)S(1)} collective-permute-done((bf16[2688,128]{1,0:T(8,128)(2,1)S(1)}, bf16[2688,128]{1,0:T(8,128)(2,1)S(1)}, u32[]{:S(2)}, u32[]{:S(2)}) %collective-permute-start.13) | collective-permute-done | bytes 688160 | tf_op jit(solution)/shard_map/ppermute | solution.py:328
  47.6 6.7 %cross.3.refs_7_ = bf16[256,2048]{1,0:T(8,128)(2,1)S(1)} custom-call(s32[2,4]{1,0:T(2,128)S(1)} %bitcast.5, bf16[384,896]{1,0:T(8,128)(2,1)S(1)} %encode.3.refs_1_, bf16[144,896]{1,0:T(8,128)(2,1)S(1)} %encode.2.refs_2_, bf16[144,896]{1,0:T(8,128)(2,1)S(1)} %collective-permute-done.6.refs_3_, bf16[256,2048]{1,0:T(8,128)(2,1)S(1)} %copy-done.4, ...), custom_call_target="tpu_custom_call" | custom-call | flops 4529848320 | bytes 8388608 | tf_op jit(solution)/shard_map/cross/pallas_call | solution.py:436
  54.3 0.7 %collective-permute-done.11.refs_6_ = bf16[2688,128]{1,0:T(8,128)(2,1)S(1)} collective-permute-done((bf16[2688,128]{1,0:T(8,128)(2,1)S(1)}, bf16[2688,128]{1,0:T(8,128)(2,1)S(1)}, u32[]{:S(2)}, u32[]{:S(2)}) %collective-permute-start.11) | collective-permute-done | bytes 688160 | tf_op jit(solution)/shard_map/ppermute | solution.py:328
  55.0 2.9 %cross.4.refs_7_ = bf16[256,2048]{1,0:T(8,128)(2,1)} custom-call(s32[2,4]{1,0:T(2,128)S(1)} %bitcast.6, bf16[384,896]{1,0:T(8,128)(2,1)S(1)} %encode.3.refs_1_, bf16[144,896]{1,0:T(8,128)(2,1)S(1)} %encode.2.refs_2_, bf16[144,896]{1,0:T(8,128)(2,1)S(1)} %collective-permute-done.6.refs_3_, bf16[256,2048]{1,0:T(8,128)(2,1)S(1)} %copy-done.4, ...), custom_call_target="tpu_custom_call" | custom-call | flops 754974720 | bytes 8388608 | tf_op jit(solution)/shard_map/cross/pallas_call | solution.py:436
  57.9 2.6 %cross.5 = bf16[256,2048]{1,0:T(8,128)(2,1)} custom-call(s32[2,4]{1,0:T(2,128)S(1)} %bitcast.7, bf16[384,896]{1,0:T(8,128)(2,1)S(1)} %encode.3.refs_1_, bf16[144,896]{1,0:T(8,128)(2,1)S(1)} %encode.2.refs_2_, bf16[144,896]{1,0:T(8,128)(2,1)S(1)} %collective-permute-done.6.refs_3_, bf16[256,2048]{1,0:T(8,128)(2,1)S(1)} %copy-done.4, ...), custom_call_target="tpu_custom_call", output_to_operand_aliasing={{}: (7, {})} | custom-call | flops 754974720 | bytes 8388608 | tf_op jit(solution)/shard_map/cross/pallas_call | solution.py:436
  (28 shorter events, 0.2 us)
Async XLA Ops:
  0.0 30.6 %copy-start.6 = (s32[4,2]{0,1:T(2,128)S(1)}, s32[4,2]{0,1:T(2,128)}, u32[]{:S(2)}) copy-start(s32[4,2]{0,1:T(2,128)} %param.13) | copy-start | bytes 100
  1.0 15.3 %collective-permute-start.7 = (bf16[896,128]{1,0:T(8,128)(2,1)S(1)}, bf16[896,128]{1,0:T(8,128)(2,1)S(1)}, u32[]{:S(2)}, u32[]{:S(2)}) collective-permute-start(bf16[896,128]{1,0:T(8,128)(2,1)S(1)} %constant_dynamic-slice_fusion), channel_id=1, source_target_pairs={{0,3},{1,2},{2,1},{3,0},{4,7},{5,6},{6,5},{7,4},{8,11},{9,10},{10,... | collective-permute-start | bytes 688136 | tf_op jit(solution)/shard_map/ppermute | solution.py:328
  6.1 11.6 %collective-permute-start.8 = (bf16[896,128]{1,0:T(8,128)(2,1)S(1)}, bf16[896,128]{1,0:T(8,128)(2,1)S(1)}, u32[]{:S(2)}, u32[]{:S(2)}) collective-permute-start(bf16[896,128]{1,0:T(8,128)(2,1)S(1)} %constant_dynamic-slice_fusion), channel_id=1, source_target_pairs={{0,1},{1,0},{2,3},{3,2},{4,5},{5,4},{6,7},{7,6},{8,9},{9,8},{10,11... | collective-permute-start | bytes 688136 | tf_op jit(solution)/shard_map/ppermute | solution.py:328
  6.1 19.5 %collective-permute-start.9 = (bf16[896,128]{1,0:T(8,128)(2,1)S(1)}, bf16[896,128]{1,0:T(8,128)(2,1)S(1)}, u32[]{:S(2)}, u32[]{:S(2)}) collective-permute-start(bf16[896,128]{1,0:T(8,128)(2,1)S(1)} %constant_dynamic-slice_fusion), channel_id=1, source_target_pairs={{0,2},{1,3},{2,0},{3,1},{4,6},{5,7},{6,4},{7,5},{8,10},{9,11},{10,... | collective-permute-start | bytes 688136 | tf_op jit(solution)/shard_map/ppermute | solution.py:328
  7.4 1.7 %collective-permute-start = (s32[2,4]{1,0:T(2,128)S(1)}, s32[2,4]{1,0:T(2,128)S(1)}, u32[]{:S(2)}, u32[]{:S(2)}) collective-permute-start(s32[2,4]{1,0:T(2,128)S(1)} %add_bitcast_fusion.refs_0_), channel_id=1, source_target_pairs={{0,4},{4,0},{8,12},{12,8},{1,5},{5,1},{9,13},{13,9},{2,6},{6,2},{1... | collective-permute-start | bytes 104 | tf_op jit(solution)/shard_map/ppermute | solution.py:372
  7.4 3.6 %collective-permute-start.1 = (s32[2,4]{1,0:T(2,128)S(1)}, s32[2,4]{1,0:T(2,128)S(1)}, u32[]{:S(2)}, u32[]{:S(2)}) collective-permute-start(s32[2,4]{1,0:T(2,128)S(1)} %add_bitcast_fusion.refs_0_), channel_id=1, source_target_pairs={{0,8},{4,12},{8,0},{12,4},{1,9},{5,13},{9,1},{13,5},{2,10},{6,14},... | collective-permute-start | bytes 104 | tf_op jit(solution)/shard_map/ppermute | solution.py:372
  9.1 3.0 %collective-permute-start.2 = (s32[2,4]{1,0:T(2,128)S(1)}, s32[2,4]{1,0:T(2,128)S(1)}, u32[]{:S(2)}, u32[]{:S(2)}) collective-permute-start(s32[2,4]{1,0:T(2,128)S(1)} %add_bitcast_fusion.refs_0_), channel_id=1, source_target_pairs={{0,12},{4,8},{8,4},{12,0},{1,13},{5,9},{9,5},{13,1},{2,14},{6,10},... | collective-permute-start | bytes 104 | tf_op jit(solution)/shard_map/ppermute | solution.py:372
  12.1 1.2 %copy-start.1 = (bf16[8,64,896]{2,1,0:T(8,128)(2,1)S(1)}, bf16[8,64,896]{2,1,0:T(8,128)(2,1)}, u32[]{:S(2)}) copy-start(bf16[8,64,896]{2,1,0:T(8,128)(2,1)} %refs_4_.6) | copy-start | bytes 2752516
  13.3 17.3 %copy-start.2 = (bf16[8,64,896]{2,1,0:T(8,128)(2,1)S(1)}, bf16[8,64,896]{2,1,0:T(8,128)(2,1)}, u32[]{:S(2)}) copy-start(bf16[8,64,896]{2,1,0:T(8,128)(2,1)} %refs_4_.6) | copy-start | bytes 2752516
  13.3 17.3 %copy-start.3 = (bf16[896,896]{1,0:T(8,128)(2,1)S(1)}, bf16[896,896]{1,0:T(8,128)(2,1)}, u32[]{:S(2)}) copy-start(bf16[896,896]{1,0:T(8,128)(2,1)} %refs_3_.5) | copy-start | bytes 4816900
  15.1 13.7 %collective-permute-start.4 = (bf16[4,64,896]{2,1,0:T(8,128)(2,1)S(1)}, bf16[4,64,896]{2,1,0:T(8,128)(2,1)S(1)}, u32[]{:S(2)}, u32[]{:S(2)}) collective-permute-start(bf16[4,64,896]{2,1,0:T(8,128)(2,1)S(1)} %get-tuple-element.17), channel_id=1, source_target_pairs={{0,8},{1,9},{2,10},{3,11},{4,12},{5,13},{6,14},{7,15},{8,0},{9,1},... | collective-permute-start | bytes 1376264 | tf_op jit(solution)/shard_map/ppermute | solution.py:328
  25.7 17.8 %collective-permute-start.12 = (bf16[2688,128]{1,0:T(8,128)(2,1)S(1)}, bf16[2688,128]{1,0:T(8,128)(2,1)S(1)}, u32[]{:S(2)}, u32[]{:S(2)}) collective-permute-start(bf16[2688,128]{1,0:T(8,128)(2,1)S(1)} %constant_dynamic-update-slice_fusion.refs_6_), channel_id=1, source_target_pairs={{0,8},{1,9},{2,10},{3,11},{4,20},{5,21},{6,22},{7,23},{8,0},{9,1},... | collective-permute-start | bytes 2064392 | tf_op jit(solution)/shard_map/ppermute | solution.py:328
  27.3 16.2 %collective-permute-start.10 = (bf16[2688,128]{1,0:T(8,128)(2,1)S(1)}, bf16[2688,128]{1,0:T(8,128)(2,1)S(1)}, u32[]{:S(2)}, u32[]{:S(2)}) collective-permute-start(bf16[2688,128]{1,0:T(8,128)(2,1)S(1)} %constant_dynamic-update-slice_fusion.refs_6_), channel_id=1, source_target_pairs={{0,16},{1,17},{2,18},{3,19},{4,12},{5,13},{6,14},{7,15},{8,24},{9,... | collective-permute-start | bytes 2064392 | tf_op jit(solution)/shard_map/ppermute | solution.py:328
  28.7 1.5 %collective-permute-start.3 = (bf16[2,64,896]{2,1,0:T(8,128)(2,1)S(1)}, bf16[2,64,896]{2,1,0:T(8,128)(2,1)S(1)}, u32[]{:S(2)}, u32[]{:S(2)}) collective-permute-start(bf16[2,64,896]{2,1,0:T(8,128)(2,1)S(1)} %get-tuple-element.16), channel_id=1, source_target_pairs={{0,4},{1,5},{2,6},{3,7},{4,0},{5,1},{6,2},{7,3},{8,12},{9,13},{10,... | collective-permute-start | bytes 688136 | tf_op jit(solution)/shard_map/ppermute | solution.py:328
  28.8 1.8 %collective-permute-start.5 = (bf16[2,64,896]{2,1,0:T(8,128)(2,1)S(1)}, bf16[2,64,896]{2,1,0:T(8,128)(2,1)S(1)}, u32[]{:S(2)}, u32[]{:S(2)}) collective-permute-start(bf16[2,64,896]{2,1,0:T(8,128)(2,1)S(1)} %slice.4), channel_id=1, source_target_pairs={{0,4},{1,5},{2,6},{3,7},{4,0},{5,1},{6,2},{7,3},{8,12},{9,13},{10,... | collective-permute-start | bytes 688136 | tf_op jit(solution)/shard_map/ppermute | solution.py:328
  30.6 1.2 %copy-start.5 = (bf16[256,1792]{1,0:T(8,128)(2,1)S(1)}, bf16[256,1792]{1,0:T(8,128)(2,1)}, u32[]{:S(2)}) copy-start(bf16[256,1792]{1,0:T(8,128)(2,1)} %refs_2_.3) | copy-start | bytes 2752516
  33.6 13.9 %copy-start = (bf16[896,1024]{1,0:T(8,128)(2,1)S(1)}, bf16[896,1024]{1,0:T(8,128)(2,1)}, u32[]{:S(2)}) copy-start(bf16[896,1024]{1,0:T(8,128)(2,1)} %refs_5_.5) | copy-start | bytes 5505028
  33.7 13.9 %copy-start.4 = (bf16[256,2048]{1,0:T(8,128)(2,1)S(1)}, bf16[256,2048]{1,0:T(8,128)(2,1)}, u32[]{:S(2)}) copy-start(bf16[256,2048]{1,0:T(8,128)(2,1)} %refs_4_.9) | copy-start | bytes 3145732
  33.7 9.8 %collective-permute-start.6 = (bf16[144,896]{1,0:T(8,128)(2,1)S(1)}, bf16[144,896]{1,0:T(8,128)(2,1)S(1)}, u32[]{:S(2)}, u32[]{:S(2)}) collective-permute-start(bf16[144,896]{1,0:T(8,128)(2,1)S(1)} %encode.2.refs_2_), channel_id=1, source_target_pairs={{0,1},{1,2},{2,3},{4,5},{5,6},{6,7},{8,9},{9,10},{10,11},{12,13},{... | collective-permute-start | bytes 774152 | tf_op jit(solution)/shard_map/ppermute | solution.py:431
  43.4 2.1 %collective-permute-start.15 = (bf16[2688,128]{1,0:T(8,128)(2,1)S(1)}, bf16[2688,128]{1,0:T(8,128)(2,1)S(1)}, u32[]{:S(2)}, u32[]{:S(2)}) collective-permute-start(bf16[2688,128]{1,0:T(8,128)(2,1)S(1)} %collective-permute-done.12.refs_8_), channel_id=1, source_target_pairs={{0,4},{1,5},{2,6},{3,7},{4,0},{5,1},{6,2},{7,3},{8,12},{9,13},{10,... | collective-permute-start | bytes 2064392 | tf_op jit(solution)/shard_map/ppermute | solution.py:328
  43.4 3.1 %collective-permute-start.14 = (bf16[2688,128]{1,0:T(8,128)(2,1)S(1)}, bf16[2688,128]{1,0:T(8,128)(2,1)S(1)}, u32[]{:S(2)}, u32[]{:S(2)}) collective-permute-start(bf16[2688,128]{1,0:T(8,128)(2,1)S(1)} %collective-permute-done.10.refs_7_), channel_id=1, source_target_pairs={{0,4},{1,5},{2,6},{3,7},{4,0},{5,1},{6,2},{7,3},{8,12},{9,13},{10,... | collective-permute-start | bytes 2064392 | tf_op jit(solution)/shard_map/ppermute | solution.py:328
  43.9 3.6 %collective-permute-start.13 = (bf16[2688,128]{1,0:T(8,128)(2,1)S(1)}, bf16[2688,128]{1,0:T(8,128)(2,1)S(1)}, u32[]{:S(2)}, u32[]{:S(2)}) collective-permute-start(bf16[2688,128]{1,0:T(8,128)(2,1)S(1)} %constant_dynamic-update-slice_fusion.refs_6_), channel_id=1, source_target_pairs={{0,4},{1,5},{2,6},{3,7},{4,0},{5,1},{6,2},{7,3},{8,12},{9,13},{10,... | collective-permute-start | bytes 2064392 | tf_op jit(solution)/shard_map/ppermute | solution.py:328
  44.0 10.9 %collective-permute-start.11 = (bf16[2688,128]{1,0:T(8,128)(2,1)S(1)}, bf16[2688,128]{1,0:T(8,128)(2,1)S(1)}, u32[]{:S(2)}, u32[]{:S(2)}) collective-permute-start(bf16[2688,128]{1,0:T(8,128)(2,1)S(1)} %collective-permute-done.10.refs_7_), channel_id=1, source_target_pairs={{0,8},{1,9},{2,10},{3,11},{4,20},{5,21},{6,22},{7,23},{8,0},{9,1},... | collective-permute-start | bytes 2064392 | tf_op jit(solution)/shard_map/ppermute | solution.py:328
  55.0 2.9 %collective-permute-start.16 = (bf16[2688,128]{1,0:T(8,128)(2,1)S(1)}, bf16[2688,128]{1,0:T(8,128)(2,1)S(1)}, u32[]{:S(2)}, u32[]{:S(2)}) collective-permute-start(bf16[2688,128]{1,0:T(8,128)(2,1)S(1)} %collective-permute-done.11.refs_6_), channel_id=1, source_target_pairs={{0,4},{1,5},{2,6},{3,7},{4,0},{5,1},{6,2},{7,3},{8,12},{9,13},{10,... | collective-permute-start | bytes 2064392 | tf_op jit(solution)/shard_map/ppermute | solution.py:328

commit v7 on v5

--- a/solution.py
+++ b/solution.py
@@ -22,7 +22,7 @@
 FLAG_ROWS = 16
 EDGE = 16
 PAIRS_AT_ONCE = 7
-HEADS_AT_ONCE = 4
+HEADS_AT_ONCE = 6
 DISTANCES = (3, 1, 2)
 
 MASKED_SCORE = -1e30

time: 60.2 us -> 60.2 us (level)
  no operation moved by 1% of the time
where the time goes in v7:
time: 60.2 us; the launch traced here: 60 us
  Pallas kernels  19.1 us (32%)
  waiting for transfers between devices  18.5 us (31%)
  starting transfers between devices  18.2 us (30%)
  local copies, waits for them, and re-layouts  3.44 us (6%)
  other arithmetic  0.7 us (1%)
    ppermute x13, waiting for transfers between devices, permute(): return lax.ppermute(value, AXES, pairs)  16.4 us
    ppermute x13, starting transfers between devices, permute(): return lax.ppermute(value, AXES, pairs)  12.7 us
    pallas_call x3, Pallas kernels, cross(): pl.pallas_call(functools.partial(kernel, blocks), out_shape=jax.ShapeDtyp...  11.4 us
    pallas_call x2, Pallas kernels, encode(): pl.pallas_call(functools.partial(encode_kernel, peers, capacity, cache_sl...  5.86 us
    ppermute x1, starting transfers between devices, per_device(): prior = lax.ppermute(last, 'span', [(i, i + 1) for i in range(spans - 1)])  2.89 us
    ppermute x3, starting transfers between devices, per_device(): lax.ppermute(v, 'cache', [(i, i ^ r) for i in range(peers)])  2.59 us
    unnamed x16, local copies, waits for them, and re-layouts  2.42 us
    ppermute x3, waiting for transfers between devices, per_device(): lax.ppermute(v, 'cache', [(i, i ^ r) for i in range(peers)])  2.07 us
  transfers between devices with their start and end apart: 17, of which 11 were waited for; matrix products, arithmetic and copies ran while one was open for 1% of the time, Pallas kernels for 27%

profile of v7, /device:TPU:0, one launch (start us, length us, event | category | flops | bytes accessed | tf_op | source)
XLA Modules:
  0.0 60.0 jit_solution(11597347742597238891)
XLA Ops:
  0.0 1.0 %constant_dynamic-slice_fusion = bf16[896,128]{1,0:T(8,128)(2,1)S(1)} fusion(bf16[896,1024]{1,0:T(8,128)(2,1)} %refs_5_.5, s32[]{:T(128)S(6)} %select_n.3), kind=kLoop, calls=%fused_computation.4 | loop fusion | bytes 458756 | tf_op jit(solution)/shard_map/dynamic_slice | solution.py:339
  1.0 5.1 %collective-permute-start.7 = (bf16[896,128]{1,0:T(8,128)(2,1)S(1)}, bf16[896,128]{1,0:T(8,128)(2,1)S(1)}, u32[]{:S(2)}, u32[]{:S(2)}) collective-permute-start(bf16[896,128]{1,0:T(8,128)(2,1)S(1)} %constant_dynamic-slice_fusion), channel_id=1, source_target_pairs={{0,3},{1,2},{2,1},{3,0},{4,7},{5,6},{6,5},{7,4},{8,11},{9,10},{10,... | collective-permute-start | bytes 688136 | tf_op jit(solution)/shard_map/ppermute | solution.py:315
  6.1 0.6 %collective-permute-start.9 = (bf16[896,128]{1,0:T(8,128)(2,1)S(1)}, bf16[896,128]{1,0:T(8,128)(2,1)S(1)}, u32[]{:S(2)}, u32[]{:S(2)}) collective-permute-start(bf16[896,128]{1,0:T(8,128)(2,1)S(1)} %constant_dynamic-slice_fusion), channel_id=1, source_target_pairs={{0,2},{1,3},{2,0},{3,1},{4,6},{5,7},{6,4},{7,5},{8,10},{9,11},{10,... | collective-permute-start | bytes 688136 | tf_op jit(solution)/shard_map/ppermute | solution.py:315
  6.7 0.7 %add_bitcast_fusion.refs_0_ = s32[2,4]{1,0:T(2,128)S(1)} fusion(s32[4,2]{0,1:T(2,128)} %param.12, s32[4,2]{0,1:T(2,128)} %param.11), kind=kLoop, calls=%fused_computation.3 | loop fusion | flops 16 | bytes 96 | tf_op jit(solution)/shard_map/add | solution.py:362
  7.4 1.7 %collective-permute-start.1 = (s32[2,4]{1,0:T(2,128)S(1)}, s32[2,4]{1,0:T(2,128)S(1)}, u32[]{:S(2)}, u32[]{:S(2)}) collective-permute-start(s32[2,4]{1,0:T(2,128)S(1)} %add_bitcast_fusion.refs_0_), channel_id=1, source_target_pairs={{0,8},{4,12},{8,0},{12,4},{1,9},{5,13},{9,1},{13,5},{2,10},{6,14},... | collective-permute-start | bytes 104 | tf_op jit(solution)/shard_map/ppermute | solution.py:359
  9.1 0.9 %collective-permute-start.2 = (s32[2,4]{1,0:T(2,128)S(1)}, s32[2,4]{1,0:T(2,128)S(1)}, u32[]{:S(2)}, u32[]{:S(2)}) collective-permute-start(s32[2,4]{1,0:T(2,128)S(1)} %add_bitcast_fusion.refs_0_), channel_id=1, source_target_pairs={{0,12},{4,8},{8,4},{12,0},{1,13},{5,9},{9,5},{13,1},{2,14},{6,10},... | collective-permute-start | bytes 104 | tf_op jit(solution)/shard_map/ppermute | solution.py:359
  10.0 1.0 %collective-permute-done.1.refs_1_ = s32[2,4]{1,0:T(2,128)S(1)} collective-permute-done((s32[2,4]{1,0:T(2,128)S(1)}, s32[2,4]{1,0:T(2,128)S(1)}, u32[]{:S(2)}, u32[]{:S(2)}) %collective-permute-start.1) | collective-permute-done | bytes 64 | tf_op jit(solution)/shard_map/ppermute | solution.py:359
  11.0 1.1 %collective-permute-done.2.refs_2_ = s32[2,4]{1,0:T(2,128)S(1)} collective-permute-done((s32[2,4]{1,0:T(2,128)S(1)}, s32[2,4]{1,0:T(2,128)S(1)}, u32[]{:S(2)}, u32[]{:S(2)}) %collective-permute-start.2) | collective-permute-done | bytes 64 | tf_op jit(solution)/shard_map/ppermute | solution.py:359
  12.1 1.2 %copy-done.1 = bf16[8,64,896]{2,1,0:T(8,128)(2,1)S(1)} copy-done((bf16[8,64,896]{2,1,0:T(8,128)(2,1)S(1)}, bf16[8,64,896]{2,1,0:T(8,128)(2,1)}, u32[]{:S(2)}) %copy-start.1) | copy-done | bytes 917528
  13.3 1.8 %fetch.1 = (bf16[2,64,896]{2,1,0:T(8,128)(2,1)S(1)}, bf16[4,64,896]{2,1,0:T(8,128)(2,1)S(1)}) custom-call(s32[2,4]{1,0:T(2,128)S(1)} %collective-permute-done.refs_0_, s32[2,4]{1,0:T(2,128)S(1)} %collective-permute-done.1.refs_1_, s32[2,4]{1,0:T(2,128)S(1)} %collective-permute-done.2.refs_2_, bf16[8,64,896]{2,1,0:T(8,128)(2,1)S(1)} %copy-done.1), custom_call_target="tpu_custom_call" | custom-call | tf_op jit(solution)/shard_map/fetch/pallas_call | solution.py:371
  15.1 1.2 %collective-permute-start.4 = (bf16[4,64,896]{2,1,0:T(8,128)(2,1)S(1)}, bf16[4,64,896]{2,1,0:T(8,128)(2,1)S(1)}, u32[]{:S(2)}, u32[]{:S(2)}) collective-permute-start(bf16[4,64,896]{2,1,0:T(8,128)(2,1)S(1)} %get-tuple-element.17), channel_id=1, source_target_pairs={{0,8},{1,9},{2,10},{3,11},{4,12},{5,13},{6,14},{7,15},{8,0},{9,1},... | collective-permute-start | bytes 1376264 | tf_op jit(solution)/shard_map/ppermute | solution.py:315
  16.3 1.4 %collective-permute-done.8 = bf16[896,128]{1,0:T(8,128)(2,1)S(1)} collective-permute-done((bf16[896,128]{1,0:T(8,128)(2,1)S(1)}, bf16[896,128]{1,0:T(8,128)(2,1)S(1)}, u32[]{:S(2)}, u32[]{:S(2)}) %collective-permute-start.8) | collective-permute-done | bytes 229408 | tf_op jit(solution)/shard_map/ppermute | solution.py:315
  17.7 7.9 %collective-permute-done.9 = bf16[896,128]{1,0:T(8,128)(2,1)S(1)} collective-permute-done((bf16[896,128]{1,0:T(8,128)(2,1)S(1)}, bf16[896,128]{1,0:T(8,128)(2,1)S(1)}, u32[]{:S(2)}, u32[]{:S(2)}) %collective-permute-start.9) | collective-permute-done | bytes 229408 | tf_op jit(solution)/shard_map/ppermute | solution.py:315
  25.7 1.6 %collective-permute-start.12 = (bf16[2688,128]{1,0:T(8,128)(2,1)S(1)}, bf16[2688,128]{1,0:T(8,128)(2,1)S(1)}, u32[]{:S(2)}, u32[]{:S(2)}) collective-permute-start(bf16[2688,128]{1,0:T(8,128)(2,1)S(1)} %constant_dynamic-update-slice_fusion.refs_6_), channel_id=1, source_target_pairs={{0,8},{1,9},{2,10},{3,11},{4,20},{5,21},{6,22},{7,23},{8,0},{9,1},... | collective-permute-start | bytes 2064392 | tf_op jit(solution)/shard_map/ppermute | solution.py:315
  27.3 1.5 %collective-permute-start.10 = (bf16[2688,128]{1,0:T(8,128)(2,1)S(1)}, bf16[2688,128]{1,0:T(8,128)(2,1)S(1)}, u32[]{:S(2)}, u32[]{:S(2)}) collective-permute-start(bf16[2688,128]{1,0:T(8,128)(2,1)S(1)} %constant_dynamic-update-slice_fusion.refs_6_), channel_id=1, source_target_pairs={{0,16},{1,17},{2,18},{3,19},{4,12},{5,13},{6,14},{7,15},{8,24},{9,... | collective-permute-start | bytes 2064392 | tf_op jit(solution)/shard_map/ppermute | solution.py:315
  28.8 0.6 collective-permute-start.5
  29.3 0.9 %collective-permute-done.3.refs_5_ = bf16[2,64,896]{2,1,0:T(8,128)(2,1)S(1)} collective-permute-done((bf16[2,64,896]{2,1,0:T(8,128)(2,1)S(1)}, bf16[2,64,896]{2,1,0:T(8,128)(2,1)S(1)}, u32[]{:S(2)}, u32[]{:S(2)}) %collective-permute-start.3) | collective-permute-done | bytes 229408 | tf_op jit(solution)/shard_map/ppermute | solution.py:315
  30.2 0.3 collective-permute-done.5.refs_7_
  30.6 1.2 %copy-done.5 = bf16[256,1792]{1,0:T(8,128)(2,1)S(1)} copy-done((bf16[256,1792]{1,0:T(8,128)(2,1)S(1)}, bf16[256,1792]{1,0:T(8,128)(2,1)}, u32[]{:S(2)}) %copy-start.5) | copy-done | bytes 917528
  31.8 1.9 %encode.2.refs_2_ = bf16[144,896]{1,0:T(8,128)(2,1)S(1)} custom-call(s32[2,4]{1,0:T(2,128)S(1)} %add_bitcast_fusion.refs_0_, s32[2,4]{1,0:T(2,128)S(1)} %bitcast.3, bf16[256,1792]{1,0:T(8,128)(2,1)S(1)} %copy-done.5, bf16[896,896]{1,0:T(8,128)(2,1)S(1)} %copy-done.3, bf16[8,64,896]{2,1,0:T(8,128)(2,1)S(1)} %copy-done.2, ...), custom_call_target="tpu_custom_call" | custom-call | flops 322961408 | bytes 2097152 | tf_op jit(solution)/shard_map/encode/pallas_call | solution.py:398
  33.7 2.9 %collective-permute-start.6 = (bf16[144,896]{1,0:T(8,128)(2,1)S(1)}, bf16[144,896]{1,0:T(8,128)(2,1)S(1)}, u32[]{:S(2)}, u32[]{:S(2)}) collective-permute-start(bf16[144,896]{1,0:T(8,128)(2,1)S(1)} %encode.2.refs_2_), channel_id=1, source_target_pairs={{0,1},{1,2},{2,3},{4,5},{5,6},{6,7},{8,9},{9,10},{10,11},{12,13},{... | collective-permute-start | bytes 774152 | tf_op jit(solution)/shard_map/ppermute | solution.py:418
  36.6 4.0 %encode.3.refs_1_ = bf16[384,896]{1,0:T(8,128)(2,1)S(1)} custom-call(s32[2,4]{1,0:T(2,128)S(1)} %add_bitcast_fusion.refs_0_, s32[2,4]{1,0:T(2,128)S(1)} %bitcast.4, bf16[256,1792]{1,0:T(8,128)(2,1)S(1)} %copy-done.5, bf16[896,896]{1,0:T(8,128)(2,1)S(1)} %copy-done.3, bf16[8,64,896]{2,1,0:T(8,128)(2,1)S(1)} %copy-done.2, ...), custom_call_target="tpu_custom_call" | custom-call | flops 968884224 | bytes 6291456 | tf_op jit(solution)/shard_map/encode/pallas_call | solution.py:398
  40.5 2.9 %collective-permute-done.12.refs_8_ = bf16[2688,128]{1,0:T(8,128)(2,1)S(1)} collective-permute-done((bf16[2688,128]{1,0:T(8,128)(2,1)S(1)}, bf16[2688,128]{1,0:T(8,128)(2,1)S(1)}, u32[]{:S(2)}, u32[]{:S(2)}) %collective-permute-start.12) | collective-permute-done | bytes 688160 | tf_op jit(solution)/shard_map/ppermute | solution.py:315
  43.4 0.5 collective-permute-start.14
  44.0 1.5 %collective-permute-start.11 = (bf16[2688,128]{1,0:T(8,128)(2,1)S(1)}, bf16[2688,128]{1,0:T(8,128)(2,1)S(1)}, u32[]{:S(2)}, u32[]{:S(2)}) collective-permute-start(bf16[2688,128]{1,0:T(8,128)(2,1)S(1)} %collective-permute-done.10.refs_7_), channel_id=1, source_target_pairs={{0,8},{1,9},{2,10},{3,11},{4,20},{5,21},{6,22},{7,23},{8,0},{9,1},... | collective-permute-start | bytes 2064392 | tf_op jit(solution)/shard_map/ppermute | solution.py:315
  45.6 1.0 %collective-permute-done.14.refs_10_ = bf16[2688,128]{1,0:T(8,128)(2,1)S(1)} collective-permute-done((bf16[2688,128]{1,0:T(8,128)(2,1)S(1)}, bf16[2688,128]{1,0:T(8,128)(2,1)S(1)}, u32[]{:S(2)}, u32[]{:S(2)}) %collective-permute-start.14) | collective-permute-done | bytes 688160 | tf_op jit(solution)/shard_map/ppermute | solution.py:315
  46.6 1.0 %collective-permute-done.13.refs_9_ = bf16[2688,128]{1,0:T(8,128)(2,1)S(1)} collective-permute-done((bf16[2688,128]{1,0:T(8,128)(2,1)S(1)}, bf16[2688,128]{1,0:T(8,128)(2,1)S(1)}, u32[]{:S(2)}, u32[]{:S(2)}) %collective-permute-start.13) | collective-permute-done | bytes 688160 | tf_op jit(solution)/shard_map/ppermute | solution.py:315
  47.6 6.6 %cross.3.refs_7_ = bf16[256,2048]{1,0:T(8,128)(2,1)S(1)} custom-call(s32[2,4]{1,0:T(2,128)S(1)} %bitcast.5, bf16[384,896]{1,0:T(8,128)(2,1)S(1)} %encode.3.refs_1_, bf16[144,896]{1,0:T(8,128)(2,1)S(1)} %encode.2.refs_2_, bf16[144,896]{1,0:T(8,128)(2,1)S(1)} %collective-permute-done.6.refs_3_, bf16[256,2048]{1,0:T(8,128)(2,1)S(1)} %copy-done.4, ...), custom_call_target="tpu_custom_call" | custom-call | flops 4529848320 | bytes 8388608 | tf_op jit(solution)/shard_map/cross/pallas_call | solution.py:423
  54.2 0.8 %collective-permute-done.11.refs_6_ = bf16[2688,128]{1,0:T(8,128)(2,1)S(1)} collective-permute-done((bf16[2688,128]{1,0:T(8,128)(2,1)S(1)}, bf16[2688,128]{1,0:T(8,128)(2,1)S(1)}, u32[]{:S(2)}, u32[]{:S(2)}) %collective-permute-start.11) | collective-permute-done | bytes 688160 | tf_op jit(solution)/shard_map/ppermute | solution.py:315
  55.0 1.9 %cross.4.refs_7_ = bf16[256,2048]{1,0:T(8,128)(2,1)S(1)} custom-call(s32[2,4]{1,0:T(2,128)S(1)} %bitcast.6, bf16[384,896]{1,0:T(8,128)(2,1)S(1)} %encode.3.refs_1_, bf16[144,896]{1,0:T(8,128)(2,1)S(1)} %encode.2.refs_2_, bf16[144,896]{1,0:T(8,128)(2,1)S(1)} %collective-permute-done.6.refs_3_, bf16[256,2048]{1,0:T(8,128)(2,1)S(1)} %copy-done.4, ...), custom_call_target="tpu_custom_call" | custom-call | flops 754974720 | bytes 8388608 | tf_op jit(solution)/shard_map/cross/pallas_call | solution.py:423
  56.9 0.2 collective-permute-done.16.refs_6_
  57.1 2.9 %cross.5 = bf16[256,2048]{1,0:T(8,128)(2,1)} custom-call(s32[2,4]{1,0:T(2,128)S(1)} %bitcast.7, bf16[384,896]{1,0:T(8,128)(2,1)S(1)} %encode.3.refs_1_, bf16[144,896]{1,0:T(8,128)(2,1)S(1)} %encode.2.refs_2_, bf16[144,896]{1,0:T(8,128)(2,1)S(1)} %collective-permute-done.6.refs_3_, bf16[256,2048]{1,0:T(8,128)(2,1)S(1)} %copy-done.4, ...), custom_call_target="tpu_custom_call" | custom-call | flops 754974720 | bytes 8388608 | tf_op jit(solution)/shard_map/cross/pallas_call | solution.py:423
  (28 shorter events, 0.3 us)
Async XLA Ops:
  0.0 30.6 %copy-start.6 = (s32[4,2]{0,1:T(2,128)S(1)}, s32[4,2]{0,1:T(2,128)}, u32[]{:S(2)}) copy-start(s32[4,2]{0,1:T(2,128)} %param.13) | copy-start | bytes 100
  1.0 15.3 %collective-permute-start.7 = (bf16[896,128]{1,0:T(8,128)(2,1)S(1)}, bf16[896,128]{1,0:T(8,128)(2,1)S(1)}, u32[]{:S(2)}, u32[]{:S(2)}) collective-permute-start(bf16[896,128]{1,0:T(8,128)(2,1)S(1)} %constant_dynamic-slice_fusion), channel_id=1, source_target_pairs={{0,3},{1,2},{2,1},{3,0},{4,7},{5,6},{6,5},{7,4},{8,11},{9,10},{10,... | collective-permute-start | bytes 688136 | tf_op jit(solution)/shard_map/ppermute | solution.py:315
  6.1 11.6 %collective-permute-start.8 = (bf16[896,128]{1,0:T(8,128)(2,1)S(1)}, bf16[896,128]{1,0:T(8,128)(2,1)S(1)}, u32[]{:S(2)}, u32[]{:S(2)}) collective-permute-start(bf16[896,128]{1,0:T(8,128)(2,1)S(1)} %constant_dynamic-slice_fusion), channel_id=1, source_target_pairs={{0,1},{1,0},{2,3},{3,2},{4,5},{5,4},{6,7},{7,6},{8,9},{9,8},{10,11... | collective-permute-start | bytes 688136 | tf_op jit(solution)/shard_map/ppermute | solution.py:315
  6.1 19.5 %collective-permute-start.9 = (bf16[896,128]{1,0:T(8,128)(2,1)S(1)}, bf16[896,128]{1,0:T(8,128)(2,1)S(1)}, u32[]{:S(2)}, u32[]{:S(2)}) collective-permute-start(bf16[896,128]{1,0:T(8,128)(2,1)S(1)} %constant_dynamic-slice_fusion), channel_id=1, source_target_pairs={{0,2},{1,3},{2,0},{3,1},{4,6},{5,7},{6,4},{7,5},{8,10},{9,11},{10,... | collective-permute-start | bytes 688136 | tf_op jit(solution)/shard_map/ppermute | solution.py:315
  7.4 1.7 %collective-permute-start = (s32[2,4]{1,0:T(2,128)S(1)}, s32[2,4]{1,0:T(2,128)S(1)}, u32[]{:S(2)}, u32[]{:S(2)}) collective-permute-start(s32[2,4]{1,0:T(2,128)S(1)} %add_bitcast_fusion.refs_0_), channel_id=1, source_target_pairs={{0,4},{4,0},{8,12},{12,8},{1,5},{5,1},{9,13},{13,9},{2,6},{6,2},{1... | collective-permute-start | bytes 104 | tf_op jit(solution)/shard_map/ppermute | solution.py:359
  7.4 3.6 %collective-permute-start.1 = (s32[2,4]{1,0:T(2,128)S(1)}, s32[2,4]{1,0:T(2,128)S(1)}, u32[]{:S(2)}, u32[]{:S(2)}) collective-permute-start(s32[2,4]{1,0:T(2,128)S(1)} %add_bitcast_fusion.refs_0_), channel_id=1, source_target_pairs={{0,8},{4,12},{8,0},{12,4},{1,9},{5,13},{9,1},{13,5},{2,10},{6,14},... | collective-permute-start | bytes 104 | tf_op jit(solution)/shard_map/ppermute | solution.py:359
  9.1 3.0 %collective-permute-start.2 = (s32[2,4]{1,0:T(2,128)S(1)}, s32[2,4]{1,0:T(2,128)S(1)}, u32[]{:S(2)}, u32[]{:S(2)}) collective-permute-start(s32[2,4]{1,0:T(2,128)S(1)} %add_bitcast_fusion.refs_0_), channel_id=1, source_target_pairs={{0,12},{4,8},{8,4},{12,0},{1,13},{5,9},{9,5},{13,1},{2,14},{6,10},... | collective-permute-start | bytes 104 | tf_op jit(solution)/shard_map/ppermute | solution.py:359
  12.1 1.2 %copy-start.1 = (bf16[8,64,896]{2,1,0:T(8,128)(2,1)S(1)}, bf16[8,64,896]{2,1,0:T(8,128)(2,1)}, u32[]{:S(2)}) copy-start(bf16[8,64,896]{2,1,0:T(8,128)(2,1)} %refs_4_.6) | copy-start | bytes 2752516
  13.3 17.3 %copy-start.2 = (bf16[8,64,896]{2,1,0:T(8,128)(2,1)S(1)}, bf16[8,64,896]{2,1,0:T(8,128)(2,1)}, u32[]{:S(2)}) copy-start(bf16[8,64,896]{2,1,0:T(8,128)(2,1)} %refs_4_.6) | copy-start | bytes 2752516
  13.3 17.3 %copy-start.3 = (bf16[896,896]{1,0:T(8,128)(2,1)S(1)}, bf16[896,896]{1,0:T(8,128)(2,1)}, u32[]{:S(2)}) copy-start(bf16[896,896]{1,0:T(8,128)(2,1)} %refs_3_.5) | copy-start | bytes 4816900
  15.1 13.7 %collective-permute-start.4 = (bf16[4,64,896]{2,1,0:T(8,128)(2,1)S(1)}, bf16[4,64,896]{2,1,0:T(8,128)(2,1)S(1)}, u32[]{:S(2)}, u32[]{:S(2)}) collective-permute-start(bf16[4,64,896]{2,1,0:T(8,128)(2,1)S(1)} %get-tuple-element.17), channel_id=1, source_target_pairs={{0,8},{1,9},{2,10},{3,11},{4,12},{5,13},{6,14},{7,15},{8,0},{9,1},... | collective-permute-start | bytes 1376264 | tf_op jit(solution)/shard_map/ppermute | solution.py:315
  25.7 17.8 %collective-permute-start.12 = (bf16[2688,128]{1,0:T(8,128)(2,1)S(1)}, bf16[2688,128]{1,0:T(8,128)(2,1)S(1)}, u32[]{:S(2)}, u32[]{:S(2)}) collective-permute-start(bf16[2688,128]{1,0:T(8,128)(2,1)S(1)} %constant_dynamic-update-slice_fusion.refs_6_), channel_id=1, source_target_pairs={{0,8},{1,9},{2,10},{3,11},{4,20},{5,21},{6,22},{7,23},{8,0},{9,1},... | collective-permute-start | bytes 2064392 | tf_op jit(solution)/shard_map/ppermute | solution.py:315
  27.3 16.2 %collective-permute-start.10 = (bf16[2688,128]{1,0:T(8,128)(2,1)S(1)}, bf16[2688,128]{1,0:T(8,128)(2,1)S(1)}, u32[]{:S(2)}, u32[]{:S(2)}) collective-permute-start(bf16[2688,128]{1,0:T(8,128)(2,1)S(1)} %constant_dynamic-update-slice_fusion.refs_6_), channel_id=1, source_target_pairs={{0,16},{1,17},{2,18},{3,19},{4,12},{5,13},{6,14},{7,15},{8,24},{9,... | collective-permute-start | bytes 2064392 | tf_op jit(solution)/shard_map/ppermute | solution.py:315
  28.7 1.5 %collective-permute-start.3 = (bf16[2,64,896]{2,1,0:T(8,128)(2,1)S(1)}, bf16[2,64,896]{2,1,0:T(8,128)(2,1)S(1)}, u32[]{:S(2)}, u32[]{:S(2)}) collective-permute-start(bf16[2,64,896]{2,1,0:T(8,128)(2,1)S(1)} %get-tuple-element.16), channel_id=1, source_target_pairs={{0,4},{1,5},{2,6},{3,7},{4,0},{5,1},{6,2},{7,3},{8,12},{9,13},{10,... | collective-permute-start | bytes 688136 | tf_op jit(solution)/shard_map/ppermute | solution.py:315
  28.8 1.8 %collective-permute-start.5 = (bf16[2,64,896]{2,1,0:T(8,128)(2,1)S(1)}, bf16[2,64,896]{2,1,0:T(8,128)(2,1)S(1)}, u32[]{:S(2)}, u32[]{:S(2)}) collective-permute-start(bf16[2,64,896]{2,1,0:T(8,128)(2,1)S(1)} %slice.4), channel_id=1, source_target_pairs={{0,4},{1,5},{2,6},{3,7},{4,0},{5,1},{6,2},{7,3},{8,12},{9,13},{10,... | collective-permute-start | bytes 688136 | tf_op jit(solution)/shard_map/ppermute | solution.py:315
  30.6 1.2 %copy-start.5 = (bf16[256,1792]{1,0:T(8,128)(2,1)S(1)}, bf16[256,1792]{1,0:T(8,128)(2,1)}, u32[]{:S(2)}) copy-start(bf16[256,1792]{1,0:T(8,128)(2,1)} %refs_2_.3) | copy-start | bytes 2752516
  33.6 13.9 %copy-start = (bf16[896,1024]{1,0:T(8,128)(2,1)S(1)}, bf16[896,1024]{1,0:T(8,128)(2,1)}, u32[]{:S(2)}) copy-start(bf16[896,1024]{1,0:T(8,128)(2,1)} %refs_5_.5) | copy-start | bytes 5505028
  33.7 13.9 %copy-start.4 = (bf16[256,2048]{1,0:T(8,128)(2,1)S(1)}, bf16[256,2048]{1,0:T(8,128)(2,1)}, u32[]{:S(2)}) copy-start(bf16[256,2048]{1,0:T(8,128)(2,1)} %refs_4_.9) | copy-start | bytes 3145732
  33.7 9.8 %collective-permute-start.6 = (bf16[144,896]{1,0:T(8,128)(2,1)S(1)}, bf16[144,896]{1,0:T(8,128)(2,1)S(1)}, u32[]{:S(2)}, u32[]{:S(2)}) collective-permute-start(bf16[144,896]{1,0:T(8,128)(2,1)S(1)} %encode.2.refs_2_), channel_id=1, source_target_pairs={{0,1},{1,2},{2,3},{4,5},{5,6},{6,7},{8,9},{9,10},{10,11},{12,13},{... | collective-permute-start | bytes 774152 | tf_op jit(solution)/shard_map/ppermute | solution.py:418
  43.4 2.1 %collective-permute-start.15 = (bf16[2688,128]{1,0:T(8,128)(2,1)S(1)}, bf16[2688,128]{1,0:T(8,128)(2,1)S(1)}, u32[]{:S(2)}, u32[]{:S(2)}) collective-permute-start(bf16[2688,128]{1,0:T(8,128)(2,1)S(1)} %collective-permute-done.12.refs_8_), channel_id=1, source_target_pairs={{0,4},{1,5},{2,6},{3,7},{4,0},{5,1},{6,2},{7,3},{8,12},{9,13},{10,... | collective-permute-start | bytes 2064392 | tf_op jit(solution)/shard_map/ppermute | solution.py:315
  43.4 3.1 %collective-permute-start.14 = (bf16[2688,128]{1,0:T(8,128)(2,1)S(1)}, bf16[2688,128]{1,0:T(8,128)(2,1)S(1)}, u32[]{:S(2)}, u32[]{:S(2)}) collective-permute-start(bf16[2688,128]{1,0:T(8,128)(2,1)S(1)} %collective-permute-done.10.refs_7_), channel_id=1, source_target_pairs={{0,4},{1,5},{2,6},{3,7},{4,0},{5,1},{6,2},{7,3},{8,12},{9,13},{10,... | collective-permute-start | bytes 2064392 | tf_op jit(solution)/shard_map/ppermute | solution.py:315
  43.9 3.6 %collective-permute-start.13 = (bf16[2688,128]{1,0:T(8,128)(2,1)S(1)}, bf16[2688,128]{1,0:T(8,128)(2,1)S(1)}, u32[]{:S(2)}, u32[]{:S(2)}) collective-permute-start(bf16[2688,128]{1,0:T(8,128)(2,1)S(1)} %constant_dynamic-update-slice_fusion.refs_6_), channel_id=1, source_target_pairs={{0,4},{1,5},{2,6},{3,7},{4,0},{5,1},{6,2},{7,3},{8,12},{9,13},{10,... | collective-permute-start | bytes 2064392 | tf_op jit(solution)/shard_map/ppermute | solution.py:315
  44.0 10.9 %collective-permute-start.11 = (bf16[2688,128]{1,0:T(8,128)(2,1)S(1)}, bf16[2688,128]{1,0:T(8,128)(2,1)S(1)}, u32[]{:S(2)}, u32[]{:S(2)}) collective-permute-start(bf16[2688,128]{1,0:T(8,128)(2,1)S(1)} %collective-permute-done.10.refs_7_), channel_id=1, source_target_pairs={{0,8},{1,9},{2,10},{3,11},{4,20},{5,21},{6,22},{7,23},{8,0},{9,1},... | collective-permute-start | bytes 2064392 | tf_op jit(solution)/shard_map/ppermute | solution.py:315
  55.0 2.1 %collective-permute-start.16 = (bf16[2688,128]{1,0:T(8,128)(2,1)S(1)}, bf16[2688,128]{1,0:T(8,128)(2,1)S(1)}, u32[]{:S(2)}, u32[]{:S(2)}) collective-permute-start(bf16[2688,128]{1,0:T(8,128)(2,1)S(1)} %collective-permute-done.11.refs_6_), channel_id=1, source_target_pairs={{0,4},{1,5},{2,6},{3,7},{4,0},{5,1},{6,2},{7,3},{8,12},{9,13},{10,... | collective-permute-start | bytes 2064392 | tf_op jit(solution)/shard_map/ppermute | solution.py:315
